TPU v7x, 32 devices: a whole 2x2x4 slice. The times are simulated.
32 devices in a mesh: groups: 2 (over x), dp: 4 (over z), tensor: 4 (over y, core).
Axes of the slice: x: 2, y: 2, z: 4, core: 2. Of those that a mesh axis runs over, the one named last changes fastest.
Arguments:
- tokens: bfloat16 [4096, 8192], P(('groups', 'dp'), 'tensor'), parts along dimension 0, may hold values from -6 to 6
- cotangent: bfloat16 [4096, 8192], P(('groups', 'dp'), 'tensor'), parts along dimension 0, may hold values from -6 to 6
- frozen_weight: bfloat16 [8192, 8192], P('tensor'), may hold values from -0.09375 to 0.09375
- adapter_down_table: bfloat16 [32, 8192, 64], P(('groups', 'dp'), 'tensor'), parts along dimension 0, may hold values from -0.75 to 0.75
- adapter_up_table: bfloat16 [32, 64, 8192], P(('groups', 'dp'), None, 'tensor'), parts along dimension 0, may hold values from -0.75 to 0.75
- segment_adapter_id: int32 [32], P(('groups', 'dp')), parts along dimension 0, may hold values from 0 to 15, as said below
- segment_live_length: int32 [32], P(('groups', 'dp')), parts along dimension 0, may hold values from 1 to 128, as said below
- adapter_table_row: int32 [32], P('groups'), parts along dimension 0, may hold values from 0 to 15, as said below
Outputs:
- layer_result: bfloat16 [4096, 8192], P(('groups', 'dp'), 'tensor'), parts along dimension 0
- token_input_gradient: bfloat16 [4096, 8192], P(('groups', 'dp'), 'tensor'), parts along dimension 0
- down_grad: float32 [32, 8192, 64], P(('groups', 'dp'), 'tensor'), parts along dimension 0
- up_grad: float32 [32, 64, 8192], P(('groups', 'dp'), None, 'tensor'), parts along dimension 0
There are 2 independent parts, one for each index of `groups`. A program takes and returns all parts, laid end to end along the dimension named above; an argument that names none is the same for every part. Nothing has to cross between parts.
Inputs may be any that keep to these rules, and one draw needn't show every extreme that they name: `segment_adapter_id`: the owner of an adapter along dp is adapter_table_row of it // 4. At most 2 segments of one device name adapters of one owner; in every draw some owner has exactly 2 segments of every device. `adapter_table_row`: A permutation of the table rows. `segment_live_length`: some segment is full.
All inputs are finite; a program needn't handle non-finite values.
Results may differ from a plain program's by a relative error of at most 0.013.
Values may be sent and summed in bfloat16 or wider, within the bound.
No kernel may reach another device: no remote copies, remote signals or barrier semaphores. Data moves between devices by JAX's collectives and lax.ppermute only.
A program may use at most 192 MiB of HBM per device.

v0:
```python
import jax
import jax.numpy as jnp
from jax import lax
from jax.sharding import PartitionSpec as P

adapter_scale = 0.015625


def split_pair(values):
    upper = values.astype(jnp.bfloat16)
    lower = (values - upper.astype(jnp.float32)).astype(jnp.bfloat16)
    return (upper, lower)


def couple_left(form, pair, other):
    return jnp.einsum(form, pair[0], other, preferred_element_type=jnp.float32) + jnp.einsum(
        form, pair[1], other, preferred_element_type=jnp.float32
    )


def pair_right(form, other, pair):
    return jnp.einsum(form, other, pair[0], preferred_element_type=jnp.float32) + jnp.einsum(
        form, other, pair[1], preferred_element_type=jnp.float32
    )


def output_total(term_cols, full_width):
    return lax.psum_scatter(
        term_cols(0, full_width).astype(jnp.bfloat16), "tensor", scatter_dimension=1, tiled=True
    ).astype(jnp.float32)


def body(
    tokens,
    cotangent,
    frozen_weight,
    adapter_down_table,
    adapter_up_table,
    segment_adapter_id,
    segment_live_length,
    adapter_table_row,
):
    seg_count = segment_adapter_id.shape[0]
    segment_row_count, partition_width = tokens.shape
    full_width = frozen_weight.shape[1]
    seg_rows = segment_row_count // seg_count
    owned_adapter_count = adapter_down_table.shape[0]
    rank_extent_width = adapter_down_table.shape[2]
    peer_count = lax.axis_size("dp")
    capacity = max(2, seg_count // 2)
    slot_table_rows = jnp.take(adapter_table_row, segment_adapter_id)
    owners = slot_table_rows // owned_adapter_count
    local_rows = slot_table_rows % owned_adapter_count
    same_owner = owners[:, None] == owners[None, :]
    seg_ids = jnp.arange(seg_count)
    before = seg_ids[None, :] < seg_ids[:, None]
    order_rank = jnp.sum(jnp.logical_and(same_owner, before), axis=1)
    placement = owners * capacity + order_rank
    placed = placement[:, None] == jnp.arange(peer_count * capacity)[None, :]
    request = jnp.sum(jnp.where(placed, local_rows[:, None] + 1, 0), axis=0) - 1
    request = request.reshape(peer_count, capacity)
    wanted = lax.all_to_all(request, "dp", split_axis=0, concat_axis=0, tiled=True)
    wanted_mask = wanted >= 0
    segment_row_index = jnp.maximum(wanted, 0)
    send_down = jnp.where(
        wanted_mask[:, :, None, None],
        adapter_down_table[segment_row_index],
        jnp.zeros((), jnp.bfloat16),
    )
    send_up = jnp.where(
        wanted_mask[:, :, None, None],
        adapter_up_table[segment_row_index],
        jnp.zeros((), jnp.bfloat16),
    )
    got_down, got_up = (
        lax.all_to_all(send_down, "dp", split_axis=0, concat_axis=0, tiled=True),
        lax.all_to_all(send_up, "dp", split_axis=0, concat_axis=0, tiled=True),
    )
    segment_down_factor = jnp.take(
        got_down.reshape(peer_count * capacity, partition_width, rank_extent_width),
        placement,
        axis=0,
    )
    segment_up_factor = jnp.take(
        got_up.reshape(peer_count * capacity, rank_extent_width, partition_width), placement, axis=0
    )
    live_mask = (jnp.arange(seg_rows)[None, :] < segment_live_length[:, None]).astype(jnp.float32)[
        :, :, None
    ]
    tok_seg = tokens.reshape(seg_count, seg_rows, partition_width)
    segment_cotangent = cotangent.reshape(seg_count, seg_rows, partition_width)
    down_part = jnp.einsum(
        "ksd,kdr->ksr", tok_seg, segment_down_factor, preferred_element_type=jnp.float32
    )
    up_factor_complete = lax.all_gather(segment_up_factor, "tensor", axis=2, tiled=True)
    partial_couple = split_pair(down_part)

    def joined_cols(begin_at, count):
        adapter_columns = couple_left("enu,euz->enz", partial_couple, up_factor_complete) * (
            adapter_scale * live_mask
        )
        return jnp.dot(
            tokens, frozen_weight, preferred_element_type=jnp.float32
        ) + adapter_columns.reshape(segment_row_count, count)

    summed = output_total(joined_cols, full_width)
    down_activation = lax.psum(down_part.astype(jnp.bfloat16), "tensor").astype(jnp.float32)
    block_cols = lax.all_gather(cotangent, "tensor", axis=1, tiled=True)
    block_seg = block_cols.reshape(seg_count, seg_rows, block_cols.shape[1])
    rank_accumulate = jnp.einsum(
        "ksc,krc->ksr", block_seg, up_factor_complete, preferred_element_type=jnp.float32
    )
    backward_total = lax.dot_general(
        block_cols, frozen_weight, (((1,), (1,)), ((), ())), preferred_element_type=jnp.float32
    )
    output_gradient = rank_accumulate * (adapter_scale * live_mask)
    layer_result = summed.astype(jnp.bfloat16)
    gradient_couple = split_pair(output_gradient)
    adapter_backward = couple_left("omj,oxj->omx", gradient_couple, segment_down_factor)
    token_input_gradient = (
        backward_total + adapter_backward.reshape(segment_row_count, partition_width)
    ).astype(jnp.bfloat16)
    down_terms = pair_right("ksd,ksr->kdr", tok_seg, gradient_couple).astype(jnp.bfloat16)
    scaled_activation = down_activation * (adapter_scale * live_mask)
    up_terms = couple_left("ksr,ksd->krd", split_pair(scaled_activation), segment_cotangent).astype(
        jnp.bfloat16
    )
    ret_down = (
        jnp.zeros((peer_count * capacity, partition_width, rank_extent_width), jnp.bfloat16)
        .at[placement]
        .set(down_terms)
    )
    ret_up = (
        jnp.zeros((peer_count * capacity, rank_extent_width, partition_width), jnp.bfloat16)
        .at[placement]
        .set(up_terms)
    )
    ret_down = ret_down.reshape(peer_count, capacity, partition_width, rank_extent_width)
    ret_up = ret_up.reshape(peer_count, capacity, rank_extent_width, partition_width)
    back_down, back_up = (
        lax.all_to_all(ret_down, "dp", split_axis=0, concat_axis=0, tiled=True),
        lax.all_to_all(ret_up, "dp", split_axis=0, concat_axis=0, tiled=True),
    )
    select_onehot = (wanted[:, :, None] == jnp.arange(owned_adapter_count)[None, None, :]).astype(
        jnp.bfloat16
    )
    down_grad = jnp.einsum(
        "pco,pcdr->odr", select_onehot, back_down, preferred_element_type=jnp.float32
    )
    up_grad = jnp.einsum(
        "pco,pcrd->ord", select_onehot, back_up, preferred_element_type=jnp.float32
    )
    return (layer_result, token_input_gradient, down_grad, up_grad)


def solution(mesh):
    placed = (
        P(("groups", "dp"), "tensor"),
        P(("groups", "dp"), "tensor"),
        P("tensor", None),
        P(("groups", "dp"), "tensor", None),
        P(("groups", "dp"), None, "tensor"),
        P(("groups", "dp")),
        P(("groups", "dp")),
        P("groups"),
    )
    return jax.shard_map(
        body,
        mesh=mesh,
        in_specs=placed,
        out_specs=(
            P(("groups", "dp"), "tensor"),
            P(("groups", "dp"), "tensor"),
            P(("groups", "dp"), "tensor", None),
            P(("groups", "dp"), None, "tensor"),
        ),
        check_vma=False,
    )
```

profile of v0, /device:TPU:0, one launch (start us, length us, event | category | flops | bytes accessed | tf_op | source)
XLA Modules:
  0.0 347.2 jit_solution(6328778208205682189)
XLA Ops:
  7.2 0.0 copy-start
  7.2 0.8 compare_select_fusion.1
  8.0 1.3 gather_fusion
  9.3 0.7 and_select_fusion.1
  10.0 0.2 convert_reduce_fusion
  10.2 0.1 select_reduce_fusion
  10.3 0.1 sub.20
  10.3 11.7 %all_to_all.29 = s32[4,1,2]{2,1,0:T(1,128)S(1)} all-to-all(s32[4,1,2]{2,1,0:T(1,128)S(1)} %bitcast.60), channel_id=1, replica_groups=mesh['groups'=2,'dp'=4,'tensor'=4] {'dp'}, dimensions={0} | all-to-all | bytes 64 | tf_op jit(solution)/shard_map/all_to_all | solution.py:62
  22.0 0.1 copy.35
  22.1 0.1 copy.36
  22.2 0.1 reshape.185
  22.3 3.2 gather_fusion.3
  25.6 3.1 broadcast_select_fusion
  28.7 4.5 %all-to-all-start.2 = ((bf16[4,2,64,2048]{3,2,1,0:T(8,128)(2,1)}), bf16[4,2,64,2048]{3,2,1,0:T(8,128)(2,1)}, u32[]{:S(2)}, u32[]{:S(2)}) async-start(bf16[4,2,64,2048]{3,2,1,0:T(8,128)(2,1)} %broadcast_select_fusion), calls=%async_computation.2 | async-start | bytes 4194304 | tf_op jit(solution)/shard_map/all_to_all | solution.py:77
  33.1 0.0 all-gather.3.cloned.1.call-start
  33.2 47.0 %all-to-all-done.2 = bf16[4,2,64,2048]{3,2,1,0:T(8,128)(2,1)} async-done(((bf16[4,2,64,2048]{3,2,1,0:T(8,128)(2,1)}), bf16[4,2,64,2048]{3,2,1,0:T(8,128)(2,1)}, u32[]{:S(2)}, u32[]{:S(2)}) %all-to-all-start.2) | async-done | bytes 2097184 | tf_op jit(solution)/shard_map/all_to_all | solution.py:77
  80.2 3.2 gather_fusion.4
  83.4 2.4 broadcast_select_fusion.2
  85.9 0.0 all-gather.3.cloned.1.call-update
  85.9 0.0 copy-done.4
  85.9 2.0 gather_fusion.1
  87.9 3.1 broadcast_select_fusion.1
  91.0 4.6 %all-to-all-start.1 = ((bf16[4,2,2048,64]{2,3,1,0:T(8,128)(2,1)}), bf16[4,2,2048,64]{2,3,1,0:T(8,128)(2,1)}, u32[]{:S(2)}, u32[]{:S(2)}) async-start(bf16[4,2,2048,64]{2,3,1,0:T(8,128)(2,1)} %broadcast_select_fusion.1), calls=%async_computation.1 | async-start | bytes 4194304 | tf_op jit(solution)/shard_map/all_to_all | solution.py:76
  95.6 0.0 copy-done.7
  95.6 0.1 fusion.19
  95.7 47.7 %all-to-all-done.1 = bf16[4,2,2048,64]{2,3,1,0:T(8,128)(2,1)} async-done(((bf16[4,2,2048,64]{2,3,1,0:T(8,128)(2,1)}), bf16[4,2,2048,64]{2,3,1,0:T(8,128)(2,1)}, u32[]{:S(2)}, u32[]{:S(2)}) %all-to-all-start.1) | async-done | bytes 2097184 | tf_op jit(solution)/shard_map/all_to_all | solution.py:76
  143.4 2.2 gather_fusion.2
  145.6 0.9 fusion.25
  146.5 0.0 copy-start.5
  146.5 0.0 all-gather.3.cloned.1.call-done
  146.6 10.4 %fusion.26 = f32[4,128,8192]{2,1,0:T(8,128)} fusion(bf16[4,128,64]{1,2,0:T(8,128)(2,1)S(1)} %get-tuple-element.24, bf16[4,64,8192]{2,1,0:T(8,128)(2,1)} %all-gather.3.cloned.1.call-done), kind=kOutput, calls=%fused_computation.70 | convolution fusion | flops 536870912 | bytes 21037056 | tf_op jit(solution)/shard_map/enu,euz->enz/dot_general | solution.py:16
  157.0 0.0 copy-done.2
  157.0 10.5 %add_multiply_fusion = f32[4,128,8192]{2,1,0:T(8,128)} fusion(f32[4,128,8192]{2,1,0:T(8,128)} %fusion.26, bf16[4,64,8192]{2,1,0:T(8,128)(2,1)S(1)} %copy-done.2, f32[4,128]{1,0:T(4,128)S(1)} %fusion.19, f32[4,128,64]{1,2,0:T(8,128)S(1)} %get-tuple-element.25, bf16[4,128,64]{1,2,0:T(8,128)(2,1)S(1)} %get-tuple-element.24), kind=kOutput, calls=%fused_computation.9 | convolution fusion | flops 545357824 | bytes 37947392 | tf_op jit(solution)/shard_map/enu,euz->enz/dot_general | solution.py:16
  167.5 0.7 all-reduce.2.cloned.1.call-update
  168.3 0.0 all-gather.5.cloned.1.call-start
  168.3 0.7 all-gather.5.cloned.1.call-update
  169.0 0.2 reduce-scatter.2.cloned.1.call-start
  169.2 31.5 %fusion = bf16[512,8192]{1,0:T(8,128)(2,1)} fusion(f32[4,128,8192]{2,1,0:T(8,128)} %add_multiply_fusion, bf16[512,2048]{1,0:T(8,128)(2,1)S(1)} %copy-done, bf16[2048,8192]{1,0:T(8,128)(2,1)} %param.10), kind=kOutput, calls=%fused_computation.8 | convolution fusion | flops 17188257792 | bytes 60817408 | tf_op jit(solution)/shard_map/dot_general | solution.py:102
  200.8 0.0 reduce-scatter.2.cloned.1.call-update
  200.8 0.7 all-reduce.2.cloned.1.call-done
  201.5 2.2 fusion.9
  203.7 0.0 copy-done.3
  203.8 1.4 fusion.3
  205.2 1.6 broadcast_in_dim.96
  206.8 3.1 scatter_fusion.1
  209.9 5.4 %copy.40 = bf16[4,2,64,2048]{3,1,2,0:T(2,128)(2,1)} copy(bf16[4,2,64,2048]{3,2,1,0:T(8,128)(2,1)} %bitcast.58) | data formatting | bytes 4194304 | tf_op jit(solution)/shard_map/reshape | solution.py:139
  215.2 4.7 %all-to-all-start.4 = ((bf16[4,2,64,2048]{3,1,2,0:T(2,128)(2,1)}), bf16[4,2,64,2048]{3,1,2,0:T(2,128)(2,1)}, u32[]{:S(2)}, u32[]{:S(2)}) async-start(bf16[4,2,64,2048]{3,1,2,0:T(2,128)(2,1)} %copy.40), calls=%async_computation.5 | async-start | bytes 4194304 | tf_op jit(solution)/shard_map/all_to_all | solution.py:142
  219.9 41.6 %all-gather.5.cloned.1.call-done = bf16[512,8192]{1,0:T(8,128)(2,1)} async-done(((bf16[512,2048]{1,0:T(8,128)(2,1)}), bf16[512,8192]{1,0:T(8,128)(2,1)}) %all-gather.5.cloned.1.call-update) | async-done | bytes 8388624 | tf_op jit(solution)/shard_map/all_gather | solution.py:108
  261.5 7.7 %fusion.7 = f32[4,128,64]{1,2,0:T(8,128)S(1)} fusion(bf16[4,64,8192]{2,1,0:T(8,128)(2,1)} %all-gather.3.cloned.1.call-done, bf16[4,128,8192]{2,1,0:T(8,128)(2,1)} %bitcast.56, f32[4,128]{1,0:T(4,128)S(1)} %fusion.19), kind=kOutput, calls=%fused_computation.25 | convolution fusion | flops 536903680 | bytes 12716032 | tf_op jit(solution)/shard_map/ksc,krc->ksr/dot_general | solution.py:110
  269.2 0.4 fusion.21
  269.6 1.5 fusion.4
  271.1 0.2 broadcast_in_dim.95
  271.3 2.2 scatter_fusion
  273.6 3.5 %copy.38 = bf16[4,2,2048,64]{2,1,3,0:T(2,128)(2,1)} copy(bf16[4,2,2048,64]{2,3,1,0:T(8,128)(2,1)S(1)} %bitcast.57) | data formatting | bytes 4194304 | tf_op jit(solution)/shard_map/reshape | solution.py:138
  277.0 0.8 fusion.23
  277.8 2.7 convolution_add_fusion
  280.5 0.0 all-to-all-done.4
  280.5 4.7 %all-to-all-start.3 = ((bf16[4,2,2048,64]{2,1,3,0:T(2,128)(2,1)}), bf16[4,2,2048,64]{2,1,3,0:T(2,128)(2,1)}, u32[]{:S(2)}, u32[]{:S(2)}) async-start(bf16[4,2,2048,64]{2,1,3,0:T(2,128)(2,1)} %copy.38), calls=%async_computation.4 | async-start | bytes 4194304 | tf_op jit(solution)/shard_map/all_to_all | solution.py:141
  285.3 25.7 %fusion.1 = bf16[512,2048]{1,0:T(8,128)(2,1)} fusion(f32[4,128,2048]{2,1,0:T(8,128)} %convolution_add_fusion, bf16[512,8192]{1,0:T(8,128)(2,1)} %all-gather.5.cloned.1.call-done, bf16[2048,8192]{1,0:T(8,128)(2,1)} %param.10), kind=kOutput, calls=%fused_computation.11 | convolution fusion | flops 17181966336 | bytes 48234496 | tf_op jit(solution)/shard_map/dot_general | solution.py:113
  311.0 4.1 %convolution_bitcast_fusion = f32[4,64,2048]{2,0,1:T(4,128)S(1)} fusion(bf16[4,2,64,2048]{3,1,2,0:T(2,128)(2,1)} %all-to-all-done.4, s32[4,2]{0,1:T(2,128)S(1)} %bitcast.61), kind=kOutput, calls=%fused_computation.13 | convolution fusion | flops 8388640 | bytes 4194336 | tf_op jit(solution)/shard_map/pco,pcrd->ord/dot_general | solution.py:150
  315.1 2.5 copy.43
  317.6 16.3 %all-to-all-done.3 = bf16[4,2,2048,64]{2,1,3,0:T(2,128)(2,1)} async-done(((bf16[4,2,2048,64]{2,1,3,0:T(2,128)(2,1)}), bf16[4,2,2048,64]{2,1,3,0:T(2,128)(2,1)}, u32[]{:S(2)}, u32[]{:S(2)}) %all-to-all-start.3) | async-done | bytes 2097184 | tf_op jit(solution)/shard_map/all_to_all | solution.py:141
  333.9 4.2 %convolution_bitcast_fusion.1 = f32[4,2048,64]{1,0,2:T(4,128)S(1)} fusion(bf16[4,2,2048,64]{2,1,3,0:T(2,128)(2,1)} %all-to-all-done.3, s32[4,2]{0,1:T(2,128)S(1)} %bitcast.62), kind=kOutput, calls=%fused_computation.15 | convolution fusion | flops 8388640 | bytes 4194336 | tf_op jit(solution)/shard_map/pco,pcdr->odr/dot_general | solution.py:147
  338.1 2.5 copy.42
  (21 shorter events, 0.1 us)
Async XLA Ops:
  7.2 138.5 %copy-start = (bf16[512,2048]{1,0:T(8,128)(2,1)S(1)}, bf16[512,2048]{1,0:T(8,128)(2,1)}, u32[]{:S(2)}) copy-start(bf16[512,2048]{1,0:T(8,128)(2,1)} %param.8) | copy-start | bytes 6291460
  28.7 51.6 %all-to-all-start.2 = ((bf16[4,2,64,2048]{3,2,1,0:T(8,128)(2,1)}), bf16[4,2,64,2048]{3,2,1,0:T(8,128)(2,1)}, u32[]{:S(2)}, u32[]{:S(2)}) async-start(bf16[4,2,64,2048]{3,2,1,0:T(8,128)(2,1)} %broadcast_select_fusion), calls=%async_computation.2 | async-start | bytes 4194304 | tf_op jit(solution)/shard_map/all_to_all | solution.py:77
  33.1 113.4 %all-gather.3.cloned.1.call-start = ((), (), s32[]{:S(2)}) async-start(), calls=%async_computation.6 | async-start | bytes 5242880 | tf_op jit(solution)/shard_map/all_gather | solution.py:95
  83.4 2.5 copy-start.4
  91.0 4.6 %copy-start.7 = (s32[4]{0:T(128)S(1)}, s32[4]{0:T(128)}, u32[]{:S(2)}) copy-start(s32[4]{0:T(128)} %param.14) | copy-start | bytes 52
  91.0 52.4 %all-to-all-start.1 = ((bf16[4,2,2048,64]{2,3,1,0:T(8,128)(2,1)}), bf16[4,2,2048,64]{2,3,1,0:T(8,128)(2,1)}, u32[]{:S(2)}, u32[]{:S(2)}) async-start(bf16[4,2,2048,64]{2,3,1,0:T(8,128)(2,1)} %broadcast_select_fusion.1), calls=%async_computation.1 | async-start | bytes 4194304 | tf_op jit(solution)/shard_map/all_to_all | solution.py:76
  146.5 10.5 %copy-start.5 = (bf16[4,128,64]{1,2,0:T(8,128)(2,1)}, bf16[4,128,64]{1,2,0:T(8,128)(2,1)S(1)}, u32[]{:S(2)}) copy-start(bf16[4,128,64]{1,2,0:T(8,128)(2,1)S(1)} %get-tuple-element.24) | copy-start | bytes 196612
  146.6 10.5 %copy-start.2 = (bf16[4,64,8192]{2,1,0:T(8,128)(2,1)S(1)}, bf16[4,64,8192]{2,1,0:T(8,128)(2,1)}, u32[]{:S(2)}) copy-start(bf16[4,64,8192]{2,1,0:T(8,128)(2,1)} %all-gather.3.cloned.1.call-done) | copy-start | bytes 12582916
  167.5 34.0 %all-reduce.2.cloned.1.call-start = ((), (), s32[]{:S(2)}) async-start(), calls=%async_computation.9 | async-start | bytes 131072 | tf_op jit(solution)/shard_map/psum | solution.py:107
  168.3 93.2 %all-gather.5.cloned.1.call-start = ((), (), s32[]{:S(2)}) async-start(), calls=%async_computation.8 | async-start | bytes 10485760 | tf_op jit(solution)/shard_map/all_gather | solution.py:108
  169.0 171.7 %reduce-scatter.2.cloned.1.call-start = ((), (), s32[]{:S(2)}) async-start(), calls=%async_computation.7 | async-start | bytes 10485760 | tf_op jit(solution)/shard_map/reduce_scatter | solution.py:28
  201.5 2.3 copy-start.3
  201.5 2.3 copy-start.6
  215.2 65.3 %all-to-all-start.4 = ((bf16[4,2,64,2048]{3,1,2,0:T(2,128)(2,1)}), bf16[4,2,64,2048]{3,1,2,0:T(2,128)(2,1)}, u32[]{:S(2)}, u32[]{:S(2)}) async-start(bf16[4,2,64,2048]{3,1,2,0:T(2,128)(2,1)} %copy.40), calls=%async_computation.5 | async-start | bytes 4194304 | tf_op jit(solution)/shard_map/all_to_all | solution.py:142
  280.5 53.4 %all-to-all-start.3 = ((bf16[4,2,2048,64]{2,1,3,0:T(2,128)(2,1)}), bf16[4,2,2048,64]{2,1,3,0:T(2,128)(2,1)}, u32[]{:S(2)}, u32[]{:S(2)}) async-start(bf16[4,2,2048,64]{2,1,3,0:T(2,128)(2,1)} %copy.38), calls=%async_computation.4 | async-start | bytes 4194304 | tf_op jit(solution)/shard_map/all_to_all | solution.py:141
  333.9 6.8 %copy-start.1 = (bf16[512,2048]{1,0:T(8,128)(2,1)S(1)}, bf16[512,2048]{1,0:T(8,128)(2,1)}, u32[]{:S(2)}) copy-start(bf16[512,2048]{1,0:T(8,128)(2,1)} %param.8) | copy-start | bytes 6291460
Sparse Core Ops, SparseCore 0:
  86.0 33.5 all-gather.2
  171.3 30.2 all-reduce.1
  203.2 58.2 all-gather.4
  264.7 71.7 reduce-scatter.1
where the time goes:
time: 348 us; the launch traced here: 347 us
  waiting for transfers between devices  155 us (45%)
  matrix products  104 us (30%)
  local copies, waits for them, and re-layouts  33.4 us (10%)
  starting transfers between devices  18.7 us (5%)
  between operations  13.9 us (4%)
  blocking collectives  11.7 us (3%)
  other arithmetic  10.6 us (3%)
    all_to_all x1, waiting for transfers between devices, body(): lax.all_to_all(send_down, 'dp', split_axis=0, concat_axis=0, tiled=True)  47.7 us
    all_to_all x1, waiting for transfers between devices, body(): lax.all_to_all(send_up, 'dp', split_axis=0, concat_axis=0, tiled=True)  47 us
    all_gather x1, waiting for transfers between devices, body(): block_cols = lax.all_gather(cotangent, 'tensor', axis=1, tiled=True)  41.6 us
    dot_general x1, matrix products, joined_cols(): jnp.dot(tokens, frozen_weight, preferred_element_type=jnp.float32)  31.5 us
    dot_general x1, matrix products, body(): lax.dot_general(block_cols, frozen_weight, (((1,), (1,)), ((), ())), pref...  25.7 us
    all_to_all x1, waiting for transfers between devices, body(): lax.all_to_all(ret_down, 'dp', split_axis=0, concat_axis=0, tiled=True)  16.3 us
    dot_general x3, matrix products, couple_left(): jnp.einsum(form, pair[1], other, preferred_element_type=jnp.float32)  14.6 us
    dot_general x3, matrix products, couple_left(): jnp.einsum(form, pair[0], other, preferred_element_type=jnp.float32)  13.4 us
  transfers between devices with their start and end apart: 8, of which 5 were waited for; matrix products, arithmetic and copies ran while one was open for 32% of the time, Pallas kernels for 0%

commit v1 on v0

v1 whole, which is shorter than its diff:
```python
import functools

import jax
import jax.numpy as jnp
from jax import lax
from jax.experimental import pallas as pl
from jax.experimental.pallas import tpu as pltpu
from jax.sharding import PartitionSpec as P

SCALE = 0.015625
COLS = 128
TILE = 512
SEND, SOURCE, TERM, GIVEN, OWN = range(5)
F32, BF16 = jnp.float32, jnp.bfloat16
SMEM = pl.BlockSpec(memory_space=pltpu.SMEM)
VMEM = pl.BlockSpec(memory_space=pltpu.VMEM)
ANYWHERE = pl.BlockSpec(memory_space=pl.ANY)
HBM = pl.BlockSpec(memory_space=pltpu.HBM)
PARAMS = pltpu.CompilerParams(vmem_limit_bytes=56 << 20)


def cost(flops, nbytes):
    return pl.CostEstimate(flops=flops, bytes_accessed=nbytes, transcendentals=0)


def call(kernel, args, in_specs, after=(), scalars=0, grid=(), out_specs=None, scratch=(), **rest):
    n_in = len(args)

    def body(*refs):
        kernel(*refs[:n_in], *refs[n_in + len(after) :])

    return pl.pallas_call(
        body,
        grid_spec=pltpu.PrefetchScalarGridSpec(
            num_scalar_prefetch=scalars,
            grid=grid,
            in_specs=list(in_specs) + [ANYWHERE] * len(after),
            out_specs=out_specs,
            scratch_shapes=list(scratch),
        ),
        compiler_params=PARAMS,
        **rest,
    )(*args, *after)


def copy_rows(rows, table_ref, outs, held, sem):
    capacity = outs[0].shape[0]
    reads = [
        pltpu.make_async_copy(table_ref.at[row], held.at[c], sem.at[0, c])
        for c, row in enumerate(rows)
    ]
    writes = [
        pltpu.make_async_copy(held.at[c], outs[c // capacity].at[c % capacity], sem.at[1, c])
        for c in range(len(rows))
    ]
    for read in reads:
        read.start()
    for read, write in zip(reads, writes):
        read.wait()
        write.start()
    for write in writes:
        write.wait()


def copies_of(table, count):
    return [
        pltpu.VMEM((count,) + table.shape[1:], table.dtype),
        pltpu.SemaphoreType.DMA((2, count)),
    ]


def request_kernel(capacity, me_ref, rel_ref, table_ref, *rest):
    outs, (plan_ref, held, sem) = rest[:-3], rest[-3:]
    n_dev, n_seg = rel_ref.shape
    n_own = table_ref.shape[0]
    me = me_ref[0]
    for c in range((n_dev - 1) * capacity):
        plan_ref[SEND, c] = 0
        plan_ref[TERM, c] = -1
        plan_ref[GIVEN, c] = -1
    spare = COLS - 1
    for s in range(n_dev):
        slots = [rel_ref[s, k] for k in range(n_seg)]
        owners = [lax.div(v, n_own) for v in slots]
        for k in range(n_seg):
            local = slots[k] - owners[k] * n_own
            order = jnp.int32(0)
            for q in range(k):
                order = order + (owners[q] == owners[k]).astype(jnp.int32)
            if s == 0:
                away = lax.rem(owners[k] - me + n_dev, n_dev)
                plan_ref[OWN, k] = jnp.where(away == 0, local, -1)
                from_owner = (n_dev - away - 1) * capacity + order
                plan_ref[SOURCE, k] = jnp.where(away == 0, local, n_own + from_owner)
                plan_ref[TERM, jnp.where(away == 0, spare, (away - 1) * capacity + order)] = k
            else:
                mine = owners[k] == me
                there = (n_dev - s - 1) * capacity + order
                plan_ref[SEND, jnp.where(mine, there, spare)] = local
                plan_ref[GIVEN, jnp.where(mine, (s - 1) * capacity + order, spare)] = local
    rows = [plan_ref[SEND, c] for c in range(len(outs) * capacity)]
    copy_rows(rows, table_ref, outs, held, sem)


def request(me, relative, table, capacity):
    count = relative.shape[0] - 1
    block = jax.ShapeDtypeStruct((capacity,) + table.shape[1:], table.dtype)
    *sends, plan = call(
        functools.partial(request_kernel, capacity),
        (me.reshape(1), relative, table),
        [SMEM, SMEM, ANYWHERE],
        out_shape=[block] * count + [jax.ShapeDtypeStruct((8, COLS), jnp.int32)],
        out_specs=[HBM] * count + [SMEM],
        scratch=copies_of(table, count * capacity),
        cost_estimate=cost(0, table.size * 4),
        name="request",
    )
    return sends, plan


def rows_kernel(row, plan_ref, table_ref, *rest):
    outs, (held, sem) = rest[:-2], rest[-2:]
    rows = [jnp.maximum(plan_ref[row, c], 0) for c in range(len(outs) * outs[0].shape[0])]
    copy_rows(rows, table_ref, outs, held, sem)


def rows_of(plan, row, table, count, capacity, after=()):
    block = jax.ShapeDtypeStruct((capacity,) + table.shape[1:], table.dtype)
    return call(
        functools.partial(rows_kernel, row),
        (plan, table),
        [SMEM, ANYWHERE],
        after,
        out_shape=[block] * count,
        out_specs=[HBM] * count,
        scratch=copies_of(table, count * capacity),
        cost_estimate=cost(0, table.size * 4),
        name="rows",
    )


def low_rank_kernel(plan_ref, act_ref, table_ref, *rest):
    blocks, (factor_ref, part_ref, sem) = rest[:-3], rest[-3:]
    n_own = table_ref.shape[0]
    n_seg, capacity = factor_ref.shape[0], blocks[0].shape[0]
    for k in range(n_seg):
        at = plan_ref[SOURCE, k]

        @pl.when(at < n_own)
        def _(k=k, at=at):
            pltpu.make_async_copy(table_ref.at[at], factor_ref.at[k], sem.at[k]).start()

        for n, ref in enumerate(blocks):
            slot = at - n_own - n * capacity

            @pl.when((slot >= 0) & (slot < capacity))
            def _(k=k, slot=slot, ref=ref):
                pltpu.make_async_copy(ref.at[slot], factor_ref.at[k], sem.at[k]).start()

    seg_rows = act_ref.shape[0] // n_seg
    for k in range(n_seg):
        pltpu.make_async_copy(table_ref.at[0], factor_ref.at[k], sem.at[k]).wait()
        part_ref[k] = lax.dot_general(
            factor_ref[k],
            act_ref[k * seg_rows : (k + 1) * seg_rows],
            (((1,), (1,)), ((), ())),
            preferred_element_type=F32,
        ).astype(part_ref.dtype)


def low_rank(plan, act, table, blocks, n_seg, after=()):
    _, rank, width = table.shape
    return call(
        low_rank_kernel,
        (plan, act, table, *blocks),
        [SMEM, VMEM] + [ANYWHERE] * (1 + len(blocks)),
        after,
        out_shape=[
            jax.ShapeDtypeStruct((n_seg, rank, width), BF16),
            jax.ShapeDtypeStruct((n_seg, rank, act.shape[0] // n_seg), BF16),
        ],
        out_specs=[VMEM, VMEM],
        scratch=[pltpu.SemaphoreType.DMA((n_seg,))],
        cost_estimate=cost(2 * act.size * rank, 4 * act.size),
        name="low_rank",
    )


def terms_kernel(live_ref, *rest):
    parts, (right_ref, act_ref, term_ref) = rest[:-3], rest[-3:]
    total = parts[0][0].astype(F32)
    for part in parts[1:]:
        total = total + part[0].astype(F32)
    column = lax.broadcasted_iota(jnp.int32, total.shape, 1)
    act = jnp.where(column < live_ref[pl.program_id(0)], total * SCALE, 0.0).astype(BF16)
    act_ref[0] = act
    term_ref[0] = jnp.dot(act, right_ref[...], preferred_element_type=F32).astype(BF16)


def make_terms(live_length, parts, right, after=()):
    n_seg, rank, seg_rows = parts[0].shape
    width = right.shape[1]
    small = pl.BlockSpec((1, rank, seg_rows), lambda k, *_: (k, 0, 0))
    return call(
        terms_kernel,
        (live_length, *parts, right),
        [small] * len(parts) + [pl.BlockSpec((seg_rows, width), lambda k, *_: (k, 0))],
        after,
        scalars=1,
        grid=(n_seg,),
        out_shape=[
            jax.ShapeDtypeStruct((n_seg, rank, seg_rows), BF16),
            jax.ShapeDtypeStruct((n_seg, rank, width), BF16),
        ],
        out_specs=[small, pl.BlockSpec((1, rank, width), lambda k, *_: (k, 0, 0))],
        cost_estimate=cost(2 * right.size * rank, 4 * right.size),
        name="terms",
    )


def total_kernel(plan_ref, terms_ref, *rest):
    blocks, out_ref = rest[:-1], rest[-1]
    capacity = blocks[0].shape[0]
    out_ref[...] = jnp.zeros_like(out_ref)
    sources = [(plan_ref[OWN, k], terms_ref, k) for k in range(terms_ref.shape[0])]
    for n, ref in enumerate(blocks):
        for j in range(capacity):
            sources.append((plan_ref[GIVEN, n * capacity + j], ref, j))
    for at, ref, k in sources:

        @pl.when(at >= 0)
        def _(at=at, ref=ref, k=k):
            out_ref[at] += ref[k].astype(F32)


def totals(plan, terms, blocks, n_own, after=()):
    n_seg, rank, width = terms.shape
    tile = min(512, width)

    def here(n):
        return pl.BlockSpec((n, rank, tile), lambda j: (0, 0, j))

    return call(
        total_kernel,
        (plan, terms, *blocks),
        [SMEM, here(n_seg)] + [here(b.shape[0]) for b in blocks],
        after,
        grid=(width // tile,),
        out_shape=jax.ShapeDtypeStruct((n_own, rank, width), F32),
        out_specs=here(n_own),
        cost_estimate=cost(0, 4 * terms.size),
        name="totals",
    )


def segment_sum(act_ref, factor_ref):
    return jnp.concatenate(
        [
            lax.dot_general(
                act_ref[k], factor_ref[k], (((0,), (0,)), ((), ())), preferred_element_type=F32
            )
            for k in range(act_ref.shape[0])
        ],
        axis=0,
    )


def forward_kernel(x_ref, w_ref, *rest):
    out = jnp.dot(x_ref[...], w_ref[...], preferred_element_type=F32)
    rest[-1][...] = out.astype(rest[-1].dtype)


def forward(x, weight, first, last, done=None, after=()):
    rows, width = x.shape
    full = weight.shape[1]
    args = [x, weight] + ([] if done is None else [done])
    return call(
        forward_kernel,
        args,
        [
            pl.BlockSpec((rows, width), lambda j: (0, 0)),
            pl.BlockSpec((width, TILE), lambda j: (0, first + j)),
        ]
        + [ANYWHERE] * (len(args) - 2),
        after,
        grid=(last - first,),
        out_shape=jax.ShapeDtypeStruct((rows, full), BF16),
        out_specs=pl.BlockSpec((rows, TILE), lambda j: (0, first + j)),
        input_output_aliases={} if done is None else {2: 0},
        cost_estimate=cost(2 * rows * width * (last - first) * TILE, 2 * width * full),
        name="forward",
    )


def backward_kernel(x_ref, w_ref, act_ref, factor_ref, out_ref):
    out = lax.dot_general(
        x_ref[...], w_ref[...], (((1,), (1,)), ((), ())), preferred_element_type=F32
    )
    out_ref[...] = (out + segment_sum(act_ref, factor_ref)).astype(out_ref.dtype)


def backward(x, weight, act, factors, after=()):
    rows, full = x.shape
    width = weight.shape[0]
    n_seg, rank, seg_rows = act.shape
    tile = min(256, width)
    return call(
        backward_kernel,
        (x, weight, act, factors),
        [
            pl.BlockSpec((rows, full), lambda j: (0, 0)),
            pl.BlockSpec((tile, full), lambda j: (j, 0)),
            pl.BlockSpec((n_seg, rank, seg_rows), lambda j: (0, 0, 0)),
            pl.BlockSpec((n_seg, rank, tile), lambda j: (0, 0, j)),
        ],
        after,
        grid=(width // tile,),
        out_shape=jax.ShapeDtypeStruct((rows, width), BF16),
        out_specs=pl.BlockSpec((rows, tile), lambda j: (0, j)),
        cost_estimate=cost(2 * rows * width * full, 2 * width * full),
        name="backward",
    )


def adapt_kernel(x_ref, act_ref, factor_ref, out_ref):
    out = x_ref[...].astype(F32) + segment_sum(act_ref, factor_ref)
    out_ref[...] = out.astype(out_ref.dtype)


def adapt(x, act, factors, after=()):
    rows, width = x.shape
    n_seg, rank, seg_rows = act.shape
    tile = min(512, width)
    here = pl.BlockSpec((rows, tile), lambda j: (0, j))
    return call(
        adapt_kernel,
        (x, act, factors),
        [
            here,
            pl.BlockSpec((n_seg, rank, seg_rows), lambda j: (0, 0, 0)),
            pl.BlockSpec((n_seg, rank, tile), lambda j: (0, 0, j)),
        ],
        after,
        grid=(width // tile,),
        out_shape=jax.ShapeDtypeStruct((rows, width), BF16),
        out_specs=here,
        cost_estimate=cost(2 * rows * width * rank, 4 * rows * width),
        name="adapt",
    )


def body(
    tokens,
    cotangent,
    weight,
    down_table,
    up_table,
    segment_adapter_id,
    segment_live_length,
    adapter_table_row,
):
    n_seg = segment_adapter_id.shape[0]
    n_own = down_table.shape[0]
    n_dev = lax.axis_size("dp")
    n_tensor = lax.axis_size("tensor")
    n_chips = n_tensor // 2
    capacity = max(2, n_seg // 2)

    def over_core(x):
        return lax.ppermute(x, "tensor", [(i, i ^ 1) for i in range(n_tensor)])

    def over_chips(x, s):
        pairs = [(i, (i // 2 + s) % n_chips * 2 + i % 2) for i in range(n_tensor)]
        return lax.ppermute(x, "tensor", pairs)

    def over_line(x, s):
        return lax.ppermute(x, "dp", [(i, (i + s) % n_dev) for i in range(n_dev)])

    shifts = range(1, n_dev)
    hops = range(1, n_chips)

    cot_rows = lax.all_gather(cotangent, "tensor", axis=1, tiled=True)

    one = segment_adapter_id[:, None] == jnp.arange(adapter_table_row.shape[0])[None, :]
    slots = jnp.sum(jnp.where(one, adapter_table_row[None, :], 0), axis=1).astype(jnp.int32)
    relative = jnp.stack([slots] + [over_line(slots, s) for s in shifts])

    down_t = jnp.swapaxes(down_table, 1, 2)
    me_dev = lax.axis_index("dp").astype(jnp.int32)
    sends, plan = request(me_dev, relative, down_t, capacity)
    down_got = [over_line(x, s) for x, s in zip(sends, shifts)]

    sends = rows_of(plan, SEND, up_table, n_dev - 1, capacity, [sends[-1]])
    up_got = [over_line(x, s) for x, s in zip(sends, shifts)]

    tiles = weight.shape[1] // TILE
    partial = forward(tokens, weight, 0, tiles - 1, after=[sends[-1]])
    partial = forward(tokens, weight, tiles - 1, tiles, partial, down_got)
    layer = lax.psum_scatter(partial, "tensor", scatter_dimension=1, tiled=True)

    def summed(part):
        part = (part.astype(F32) + over_core(part).astype(F32)).astype(BF16)
        return [part] + [over_chips(part, s) for s in hops]

    def give(terms):
        sends = rows_of(plan, TERM, terms, n_dev - 1, capacity)
        return sends, [over_line(x, s) for x, s in zip(sends, shifts)]

    down_seg, part = low_rank(plan, tokens, down_t, down_got, n_seg, [partial])
    act, up_terms = make_terms(segment_live_length, summed(part), cotangent)

    sends, up_back = give(up_terms)
    up_seg, part = low_rank(plan, cotangent, up_table, up_got, n_seg, [sends[-1]])
    grad, down_terms = make_terms(segment_live_length, summed(part), tokens)

    sends, down_back = give(down_terms)
    up_grad = totals(plan, up_terms, up_back, n_own, [sends[-1]])
    token_input_gradient = backward(cot_rows, weight, grad, down_seg, [up_grad])
    layer_result = adapt(layer, act, up_seg, [token_input_gradient])
    down_grad = totals(plan, down_terms, down_back, n_own, [layer_result])
    return layer_result, token_input_gradient, jnp.swapaxes(down_grad, 1, 2), up_grad


def solution(mesh):
    placed = (
        P(("groups", "dp"), "tensor"),
        P(("groups", "dp"), "tensor"),
        P("tensor", None),
        P(("groups", "dp"), "tensor", None),
        P(("groups", "dp"), None, "tensor"),
        P(("groups", "dp")),
        P(("groups", "dp")),
        P("groups"),
    )
    return jax.shard_map(
        body,
        mesh=mesh,
        in_specs=placed,
        out_specs=(
            P(("groups", "dp"), "tensor"),
            P(("groups", "dp"), "tensor"),
            P(("groups", "dp"), "tensor", None),
            P(("groups", "dp"), None, "tensor"),
        ),
        check_vma=False,
    )
```

time: 348 us -> 227 us (0.65)
  the two profiles are of different devices: /device:TPU:0 before, /device:TPU:13 now
where the time goes in v1:
time: 227 us; the launch traced here: 225 us
  Pallas kernels  102 us (45%)
  waiting for transfers between devices  74.6 us (33%)
  starting transfers between devices  25.3 us (11%)
  between operations  14.2 us (6%)
  local copies, waits for them, and re-layouts  6.61 us (3%)
  other arithmetic  2.53 us (1%)
    pallas_call x14, Pallas kernels, call(): pl.pallas_call(body, grid_spec=pltpu.PrefetchScalarGridSpec(num_scalar_pr...  102 us
    ppermute x15, waiting for transfers between devices, over_line(): return lax.ppermute(x, 'dp', [(i, (i + s) % n_dev) for i in range(n_dev)])  65.3 us
    ppermute x15, starting transfers between devices, over_line(): return lax.ppermute(x, 'dp', [(i, (i + s) % n_dev) for i in range(n_dev)])  20.6 us
    unnamed x42, local copies, waits for them, and re-layouts  6.61 us
    ppermute x2, waiting for transfers between devices, over_chips(): return lax.ppermute(x, 'tensor', pairs)  6.31 us
  transfers between devices with their start and end apart: 21, of which 11 were waited for; matrix products, arithmetic and copies ran while one was open for 1% of the time, Pallas kernels for 44%

profile of v1, /device:TPU:13, one launch (start us, length us, event | category | flops | bytes accessed | tf_op | source)
XLA Modules:
  0.0 225.4 jit_solution(15573969386954956993)
XLA Ops:
  7.2 0.0 all-gather.2.cloned.1.call-start
  7.2 0.7 all-gather.2.cloned.1.call-update
  7.9 0.0 reduce-scatter.2.cloned.1.call-start
  8.0 0.2 select_reduce_fusion
  8.2 0.2 collective-permute-start.2
  8.4 2.3 %collective-permute-start.1 = (s32[4]{0:T(128)S(1)}, s32[4]{0:T(128)S(1)}, u32[]{:S(2)}, u32[]{:S(2)}) collective-permute-start(s32[4]{0:T(128)S(1)} %select_reduce_fusion), channel_id=1, source_target_pairs={{0,8},{4,12},{8,0},{12,4},{1,9},{5,13},{9,1},{13,5},{2,10},{6,14},... | collective-permute-start | bytes 56 | tf_op jit(solution)/shard_map/ppermute | solution.py:377
  10.7 2.2 collective-permute-start
  12.9 0.0 collective-permute-done.2
  12.9 0.0 collective-permute-done.1
  12.9 0.7 collective-permute-done
  13.6 0.6 pad_add_fusion.refs_1_
  14.2 4.1 %request.1 = (bf16[2,64,2048]{2,1,0:T(8,128)(2,1)}, bf16[2,64,2048]{2,1,0:T(8,128)(2,1)}, bf16[2,64,2048]{2,1,0:T(8,128)(2,1)}, s32[8,128]{1,0:T(8,128)}) custom-call(s32[1]{0:T(128)} %bitcast.refs_0_, s32[4,4]{1,0:T(4,128)} %pad_add_fusion.refs_1_, bf16[4,64,2048]{2,1,0:T(8,128)(2,1)} %bitcast.7), custom_call_target="tpu_custom_call" | custom-call | bytes 2097152 | tf_op jit(solution)/shard_map/request/pallas_call | solution.py:32
  18.3 1.6 collective-permute-start.3
  19.9 2.9 %collective-permute-start.4 = (bf16[2,64,2048]{2,1,0:T(8,128)(2,1)}, bf16[2,64,2048]{2,1,0:T(8,128)(2,1)S(1)}, u32[]{:S(2)}, u32[]{:S(2)}) collective-permute-start(bf16[2,64,2048]{2,1,0:T(8,128)(2,1)} %get-tuple-element.29), channel_id=1, source_target_pairs={{0,8},{4,12},{8,0},{12,4},{1,9},{5,13},{9,1},{13,5},{2,10},{6,14},... | collective-permute-start | bytes 1572872 | tf_op jit(solution)/shard_map/ppermute | solution.py:377
  22.8 3.6 %rows.3 = (bf16[2,64,2048]{2,1,0:T(8,128)(2,1)}, bf16[2,64,2048]{2,1,0:T(8,128)(2,1)}, bf16[2,64,2048]{2,1,0:T(8,128)(2,1)}) custom-call(s32[8,128]{1,0:T(8,128)} %get-tuple-element.25.refs_0_, bf16[4,64,2048]{2,1,0:T(8,128)(2,1)} %refs_2_.1, bf16[2,64,2048]{2,1,0:T(8,128)(2,1)} %get-tuple-element.26.refs_2_), custom_call_target="tpu_custom_call" | custom-call | bytes 2097152 | tf_op jit(solution)/shard_map/rows/pallas_call | solution.py:32
  26.4 26.1 %forward.2.refs_2_ = bf16[512,8192]{1,0:T(8,128)(2,1)} custom-call(bf16[512,2048]{1,0:T(8,128)(2,1)} %refs_3_.3, bf16[2048,8192]{1,0:T(8,128)(2,1)} %refs_1_.11, bf16[2,64,2048]{2,1,0:T(8,128)(2,1)} %get-tuple-element.27.refs_2_), custom_call_target="tpu_custom_call" | custom-call | flops 16106127360 | bytes 33554432 | tf_op jit(solution)/shard_map/forward/pallas_call | solution.py:32
  52.5 10.4 %collective-permute-done.4.refs_4_ = bf16[2,64,2048]{2,1,0:T(8,128)(2,1)S(1)} collective-permute-done((bf16[2,64,2048]{2,1,0:T(8,128)(2,1)}, bf16[2,64,2048]{2,1,0:T(8,128)(2,1)S(1)}, u32[]{:S(2)}, u32[]{:S(2)}) %collective-permute-start.4) | collective-permute-done | bytes 524320 | tf_op jit(solution)/shard_map/ppermute | solution.py:377
  62.9 4.5 %collective-permute-done.5.refs_5_ = bf16[2,64,2048]{2,1,0:T(8,128)(2,1)S(1)} collective-permute-done((bf16[2,64,2048]{2,1,0:T(8,128)(2,1)}, bf16[2,64,2048]{2,1,0:T(8,128)(2,1)S(1)}, u32[]{:S(2)}, u32[]{:S(2)}) %collective-permute-start.5) | collective-permute-done | bytes 524320 | tf_op jit(solution)/shard_map/ppermute | solution.py:377
  67.4 0.8 copy-done.2
  68.2 4.3 %forward.3.refs_6_ = bf16[512,8192]{1,0:T(8,128)(2,1)} custom-call(bf16[512,2048]{1,0:T(8,128)(2,1)} %refs_3_.3, bf16[2048,8192]{1,0:T(8,128)(2,1)} %refs_1_.11, bf16[512,8192]{1,0:T(8,128)(2,1)} %forward.2.refs_2_, bf16[2,64,2048]{2,1,0:T(8,128)(2,1)} %copy-done, bf16[2,64,2048]{2,1,0:T(8,128)(2,1)} %copy-done.1, ...), custom_call_target="tpu_custom_call", output_to_operand_aliasing={{}: (2, {})} | custom-call | flops 1073741824 | bytes 33554432 | tf_op jit(solution)/shard_map/forward/pallas_call | solution.py:32
  72.6 0.0 reduce-scatter.2.cloned.1.call-update
  72.6 1.0 copy-done.18
  73.6 0.0 collective-permute-start.8
  73.6 0.2 copy-done.17
  73.7 0.2 copy-done.16
  73.9 1.2 collective-permute-start.10
  75.1 4.8 %low_rank.2 = (bf16[4,64,2048]{2,1,0:T(8,128)(2,1)}, bf16[4,64,128]{2,1,0:T(8,128)(2,1)}) custom-call(s32[8,128]{1,0:T(8,128)} %get-tuple-element.25.refs_0_, bf16[512,2048]{1,0:T(8,128)(2,1)} %refs_3_.3, bf16[4,64,2048]{2,1,0:T(8,128)(2,1)} %bitcast.8, bf16[2,64,2048]{2,1,0:T(8,128)(2,1)} %copy-done, bf16[2,64,2048]{2,1,0:T(8,128)(2,1)} %copy-done.1, ...), custom_call_target="tpu_custom_call" | custom-call | flops 134217728 | bytes 4194304 | tf_op jit(solution)/shard_map/low_rank/pallas_call | solution.py:32
  80.0 3.5 %collective-permute-start.6 = (bf16[4,64,128]{2,1,0:T(8,128)(2,1)}, bf16[4,64,128]{2,1,0:T(8,128)(2,1)S(1)}, u32[]{:S(2)}, u32[]{:S(2)}) collective-permute-start(bf16[4,64,128]{2,1,0:T(8,128)(2,1)} %get-tuple-element.30), channel_id=1, source_target_pairs={{0,1},{1,0},{2,3},{3,2},{4,5},{5,4},{6,7},{7,6},{8,9},{9,8},{10,11... | collective-permute-start | bytes 196616 | tf_op jit(solution)/shard_map/ppermute | solution.py:370
  83.4 1.2 collective-permute-done.6
  84.6 0.9 add_convert_fusion.1.refs_1_
  85.5 0.0 copy-start.12
  85.5 0.4 collective-permute-start.7
  85.9 3.1 %collective-permute-done.7.refs_2_ = bf16[4,64,128]{2,1,0:T(8,128)(2,1)S(1)} collective-permute-done((bf16[4,64,128]{2,1,0:T(8,128)(2,1)S(1)}, bf16[4,64,128]{2,1,0:T(8,128)(2,1)S(1)}, u32[]{:S(2)}, u32[]{:S(2)}) %collective-permute-start.7) | collective-permute-done | bytes 65568 | tf_op jit(solution)/shard_map/ppermute | solution.py:374
  89.0 0.6 copy-done.14
  89.6 4.7 %terms.2 = (bf16[4,64,128]{2,1,0:T(8,128)(2,1)}, bf16[4,64,2048]{2,1,0:T(8,128)(2,1)}) custom-call(s32[4]{0:T(128)} %refs_0_.7, bf16[4,64,128]{2,1,0:T(8,128)(2,1)} %copy-done.12, bf16[4,64,128]{2,1,0:T(8,128)(2,1)} %copy-done.14, bf16[512,2048]{1,0:T(8,128)(2,1)} %refs_1_.10), custom_call_target="tpu_custom_call" | custom-call | flops 134217728 | bytes 4194304 | tf_op jit(solution)/shard_map/terms/pallas_call | solution.py:32
  94.3 3.4 %rows.4 = (bf16[2,64,2048]{2,1,0:T(8,128)(2,1)}, bf16[2,64,2048]{2,1,0:T(8,128)(2,1)}, bf16[2,64,2048]{2,1,0:T(8,128)(2,1)}) custom-call(s32[8,128]{1,0:T(8,128)} %get-tuple-element.25.refs_0_, bf16[4,64,2048]{2,1,0:T(8,128)(2,1)} %get-tuple-element.34.refs_1_), custom_call_target="tpu_custom_call" | custom-call | bytes 2097152 | tf_op jit(solution)/shard_map/rows/pallas_call | solution.py:32
  97.7 0.1 collective-permute-start.13
  97.8 3.2 %collective-permute-start.14 = (bf16[2,64,2048]{2,1,0:T(8,128)(2,1)}, bf16[2,64,2048]{2,1,0:T(8,128)(2,1)S(1)}, u32[]{:S(2)}, u32[]{:S(2)}) collective-permute-start(bf16[2,64,2048]{2,1,0:T(8,128)(2,1)} %get-tuple-element.41), channel_id=1, source_target_pairs={{0,8},{4,12},{8,0},{12,4},{1,9},{5,13},{9,1},{13,5},{2,10},{6,14},... | collective-permute-start | bytes 1572872 | tf_op jit(solution)/shard_map/ppermute | solution.py:377
  101.1 0.0 collective-permute-done.8.refs_3_
  101.1 16.4 %collective-permute-done.9.refs_4_ = bf16[2,64,2048]{2,1,0:T(8,128)(2,1)S(1)} collective-permute-done((bf16[2,64,2048]{2,1,0:T(8,128)(2,1)S(1)}, bf16[2,64,2048]{2,1,0:T(8,128)(2,1)S(1)}, u32[]{:S(2)}, u32[]{:S(2)}) %collective-permute-start.9) | collective-permute-done | bytes 524320 | tf_op jit(solution)/shard_map/ppermute | solution.py:377
  117.5 24.1 %collective-permute-done.10.refs_5_ = bf16[2,64,2048]{2,1,0:T(8,128)(2,1)S(1)} collective-permute-done((bf16[2,64,2048]{2,1,0:T(8,128)(2,1)S(1)}, bf16[2,64,2048]{2,1,0:T(8,128)(2,1)S(1)}, u32[]{:S(2)}, u32[]{:S(2)}) %collective-permute-start.10) | collective-permute-done | bytes 524320 | tf_op jit(solution)/shard_map/ppermute | solution.py:377
  141.6 0.8 copy-done.8
  142.4 4.8 %low_rank.3 = (bf16[4,64,2048]{2,1,0:T(8,128)(2,1)}, bf16[4,64,128]{2,1,0:T(8,128)(2,1)}) custom-call(s32[8,128]{1,0:T(8,128)} %get-tuple-element.25.refs_0_, bf16[512,2048]{1,0:T(8,128)(2,1)} %refs_1_.10, bf16[4,64,2048]{2,1,0:T(8,128)(2,1)} %refs_2_.1, bf16[2,64,2048]{2,1,0:T(8,128)(2,1)} %copy-done.5, bf16[2,64,2048]{2,1,0:T(8,128)(2,1)} %copy-done.7, ...), custom_call_target="tpu_custom_call" | custom-call | flops 134217728 | bytes 4194304 | tf_op jit(solution)/shard_map/low_rank/pallas_call | solution.py:32
  147.3 0.6 collective-permute-start.11
  147.8 1.1 collective-permute-done.11
  148.9 0.9 add_convert_fusion.refs_1_
  149.8 0.0 copy-start.13
  149.8 0.3 collective-permute-start.12
  150.1 3.2 %collective-permute-done.12.refs_2_ = bf16[4,64,128]{2,1,0:T(8,128)(2,1)S(1)} collective-permute-done((bf16[4,64,128]{2,1,0:T(8,128)(2,1)S(1)}, bf16[4,64,128]{2,1,0:T(8,128)(2,1)S(1)}, u32[]{:S(2)}, u32[]{:S(2)}) %collective-permute-start.12) | collective-permute-done | bytes 65568 | tf_op jit(solution)/shard_map/ppermute | solution.py:374
  153.3 0.6 copy-done.15
  153.9 4.7 %terms.3 = (bf16[4,64,128]{2,1,0:T(8,128)(2,1)}, bf16[4,64,2048]{2,1,0:T(8,128)(2,1)}) custom-call(s32[4]{0:T(128)} %refs_0_.7, bf16[4,64,128]{2,1,0:T(8,128)(2,1)} %copy-done.13, bf16[4,64,128]{2,1,0:T(8,128)(2,1)} %copy-done.15, bf16[512,2048]{1,0:T(8,128)(2,1)} %refs_3_.3), custom_call_target="tpu_custom_call" | custom-call | flops 134217728 | bytes 4194304 | tf_op jit(solution)/shard_map/terms/pallas_call | solution.py:32
  158.6 3.3 %rows.5 = (bf16[2,64,2048]{2,1,0:T(8,128)(2,1)}, bf16[2,64,2048]{2,1,0:T(8,128)(2,1)}, bf16[2,64,2048]{2,1,0:T(8,128)(2,1)}) custom-call(s32[8,128]{1,0:T(8,128)} %get-tuple-element.25.refs_0_, bf16[4,64,2048]{2,1,0:T(8,128)(2,1)} %get-tuple-element.42.refs_1_), custom_call_target="tpu_custom_call" | custom-call | bytes 2097152 | tf_op jit(solution)/shard_map/rows/pallas_call | solution.py:32
  162.0 0.1 collective-permute-start.16
  162.1 5.3 %collective-permute-start.17 = (bf16[2,64,2048]{2,1,0:T(8,128)(2,1)}, bf16[2,64,2048]{2,1,0:T(8,128)(2,1)S(1)}, u32[]{:S(2)}, u32[]{:S(2)}) collective-permute-start(bf16[2,64,2048]{2,1,0:T(8,128)(2,1)} %get-tuple-element.45), channel_id=1, source_target_pairs={{0,8},{4,12},{8,0},{12,4},{1,9},{5,13},{9,1},{13,5},{2,10},{6,14},... | collective-permute-start | bytes 1572872 | tf_op jit(solution)/shard_map/ppermute | solution.py:377
  167.4 1.4 collective-permute-start.18
  168.8 0.8 copy-done.4
  169.6 0.8 copy-done.6
  170.4 4.1 %totals.2.refs_4_ = f32[4,64,2048]{2,1,0:T(8,128)} custom-call(s32[8,128]{1,0:T(8,128)} %get-tuple-element.25.refs_0_, bf16[4,64,2048]{2,1,0:T(8,128)(2,1)} %get-tuple-element.34.refs_1_, bf16[2,64,2048]{2,1,0:T(8,128)(2,1)} %copy-done.3, bf16[2,64,2048]{2,1,0:T(8,128)(2,1)} %copy-done.4, bf16[2,64,2048]{2,1,0:T(8,128)(2,1)} %copy-done.6, ...), custom_call_target="tpu_custom_call" | custom-call | bytes 2097152 | tf_op jit(solution)/shard_map/totals/pallas_call | solution.py:32
  174.5 25.5 %backward.1.refs_3_ = bf16[512,2048]{1,0:T(8,128)(2,1)} custom-call(bf16[512,8192]{1,0:T(8,128)(2,1)} %all-gather.2.cloned.1.call-done.refs_0_, bf16[2048,8192]{1,0:T(8,128)(2,1)} %refs_1_.11, bf16[4,64,128]{2,1,0:T(8,128)(2,1)} %get-tuple-element.38.refs_2_, bf16[4,64,2048]{2,1,0:T(8,128)(2,1)} %get-tuple-element.39.refs_3_, f32[4,64,2048]{2,1,0:T(8,128)} %totals.2.refs_4_), custom_call_target="tpu_custom_call" | custom-call | flops 17179869184 | bytes 33554432 | tf_op jit(solution)/shard_map/backward/pallas_call | solution.py:32
  200.0 4.5 %adapt.1.refs_5_ = bf16[512,2048]{1,0:T(8,128)(2,1)} custom-call(bf16[512,2048]{1,0:T(8,128)(2,1)} %reduce-scatter.2.cloned.1.call-done.refs_0_, bf16[4,64,128]{2,1,0:T(8,128)(2,1)} %get-tuple-element.31.refs_1_, bf16[4,64,2048]{2,1,0:T(8,128)(2,1)} %get-tuple-element.36.refs_2_, bf16[512,2048]{1,0:T(8,128)(2,1)} %backward.1.refs_3_), custom_call_target="tpu_custom_call" | custom-call | flops 134217728 | bytes 4194304 | tf_op jit(solution)/shard_map/adapt/pallas_call | solution.py:32
  204.5 3.4 %collective-permute-done.17.refs_3_ = bf16[2,64,2048]{2,1,0:T(8,128)(2,1)S(1)} collective-permute-done((bf16[2,64,2048]{2,1,0:T(8,128)(2,1)}, bf16[2,64,2048]{2,1,0:T(8,128)(2,1)S(1)}, u32[]{:S(2)}, u32[]{:S(2)}) %collective-permute-start.17) | collective-permute-done | bytes 524320 | tf_op jit(solution)/shard_map/ppermute | solution.py:377
  207.9 5.8 %collective-permute-done.18.refs_4_ = bf16[2,64,2048]{2,1,0:T(8,128)(2,1)S(1)} collective-permute-done((bf16[2,64,2048]{2,1,0:T(8,128)(2,1)}, bf16[2,64,2048]{2,1,0:T(8,128)(2,1)S(1)}, u32[]{:S(2)}, u32[]{:S(2)}) %collective-permute-start.18) | collective-permute-done | bytes 524320 | tf_op jit(solution)/shard_map/ppermute | solution.py:377
  213.7 0.8 copy-done.11
  214.5 4.1 %totals.3 = f32[4,64,2048]{2,1,0:T(8,128)} custom-call(s32[8,128]{1,0:T(8,128)} %get-tuple-element.25.refs_0_, bf16[4,64,2048]{2,1,0:T(8,128)(2,1)} %get-tuple-element.42.refs_1_, bf16[2,64,2048]{2,1,0:T(8,128)(2,1)} %copy-done.9, bf16[2,64,2048]{2,1,0:T(8,128)(2,1)} %copy-done.10, bf16[2,64,2048]{2,1,0:T(8,128)(2,1)} %copy-done.11, ...), custom_call_target="tpu_custom_call" | custom-call | bytes 2097152 | tf_op jit(solution)/shard_map/totals/pallas_call | solution.py:32
  (40 shorter events, 0.1 us)
Async XLA Ops:
  7.2 0.8 copy-start.19
  7.2 0.8 copy-start.20
  7.2 167.3 %all-gather.2.cloned.1.call-start = ((), (), s32[]{:S(2)}) async-start(), calls=%async_computation.2 | async-start | bytes 10485760 | tf_op jit(solution)/shard_map/all_gather | solution.py:382
  7.9 192.0 %reduce-scatter.2.cloned.1.call-start = ((), (), s32[]{:S(2)}) async-start(), calls=%async_computation.1 | async-start | bytes 10485760 | tf_op jit(solution)/shard_map/reduce_scatter | solution.py:399
  8.2 4.7 %collective-permute-start.2 = (s32[4]{0:T(128)S(1)}, s32[4]{0:T(128)S(1)}, u32[]{:S(2)}, u32[]{:S(2)}) collective-permute-start(s32[4]{0:T(128)S(1)} %select_reduce_fusion), channel_id=1, source_target_pairs={{0,12},{4,0},{8,4},{12,8},{1,13},{5,1},{9,5},{13,9},{2,14},{6,2},{... | collective-permute-start | bytes 56 | tf_op jit(solution)/shard_map/ppermute | solution.py:377
  8.4 4.5 %collective-permute-start.1 = (s32[4]{0:T(128)S(1)}, s32[4]{0:T(128)S(1)}, u32[]{:S(2)}, u32[]{:S(2)}) collective-permute-start(s32[4]{0:T(128)S(1)} %select_reduce_fusion), channel_id=1, source_target_pairs={{0,8},{4,12},{8,0},{12,4},{1,9},{5,13},{9,1},{13,5},{2,10},{6,14},... | collective-permute-start | bytes 56 | tf_op jit(solution)/shard_map/ppermute | solution.py:377
  10.7 2.9 %collective-permute-start = (s32[4]{0:T(128)S(1)}, s32[4]{0:T(128)S(1)}, u32[]{:S(2)}, u32[]{:S(2)}) collective-permute-start(s32[4]{0:T(128)S(1)} %select_reduce_fusion), channel_id=1, source_target_pairs={{0,4},{4,8},{8,12},{12,0},{1,5},{5,9},{9,13},{13,1},{2,6},{6,10},{... | collective-permute-start | bytes 56 | tf_op jit(solution)/shard_map/ppermute | solution.py:377
  18.3 34.2 %collective-permute-start.3 = (bf16[2,64,2048]{2,1,0:T(8,128)(2,1)}, bf16[2,64,2048]{2,1,0:T(8,128)(2,1)S(1)}, u32[]{:S(2)}, u32[]{:S(2)}) collective-permute-start(bf16[2,64,2048]{2,1,0:T(8,128)(2,1)} %get-tuple-element.28), channel_id=1, source_target_pairs={{0,4},{4,8},{8,12},{12,0},{1,5},{5,9},{9,13},{13,1},{2,6},{6,10},{... | collective-permute-start | bytes 1572872 | tf_op jit(solution)/shard_map/ppermute | solution.py:377
  19.9 43.0 %collective-permute-start.4 = (bf16[2,64,2048]{2,1,0:T(8,128)(2,1)}, bf16[2,64,2048]{2,1,0:T(8,128)(2,1)S(1)}, u32[]{:S(2)}, u32[]{:S(2)}) collective-permute-start(bf16[2,64,2048]{2,1,0:T(8,128)(2,1)} %get-tuple-element.29), channel_id=1, source_target_pairs={{0,8},{4,12},{8,0},{12,4},{1,9},{5,13},{9,1},{13,5},{2,10},{6,14},... | collective-permute-start | bytes 1572872 | tf_op jit(solution)/shard_map/ppermute | solution.py:377
  22.8 44.6 %collective-permute-start.5 = (bf16[2,64,2048]{2,1,0:T(8,128)(2,1)}, bf16[2,64,2048]{2,1,0:T(8,128)(2,1)S(1)}, u32[]{:S(2)}, u32[]{:S(2)}) collective-permute-start(bf16[2,64,2048]{2,1,0:T(8,128)(2,1)} %get-tuple-element.26.refs_2_), channel_id=1, source_target_pairs={{0,12},{4,0},{8,4},{12,8},{1,13},{5,1},{9,5},{13,9},{2,14},{6,2},{... | collective-permute-start | bytes 1572872 | tf_op jit(solution)/shard_map/ppermute | solution.py:377
  52.5 14.9 %copy-start = (bf16[2,64,2048]{2,1,0:T(8,128)(2,1)}, bf16[2,64,2048]{2,1,0:T(8,128)(2,1)S(1)}, u32[]{:S(2)}) copy-start(bf16[2,64,2048]{2,1,0:T(8,128)(2,1)S(1)} %collective-permute-done.3.refs_3_) | copy-start | bytes 1572868
  62.9 4.5 %copy-start.1 = (bf16[2,64,2048]{2,1,0:T(8,128)(2,1)}, bf16[2,64,2048]{2,1,0:T(8,128)(2,1)S(1)}, u32[]{:S(2)}) copy-start(bf16[2,64,2048]{2,1,0:T(8,128)(2,1)S(1)} %collective-permute-done.4.refs_4_) | copy-start | bytes 1572868
  67.4 0.8 copy-start.2
  72.5 1.0 copy-start.18
  72.5 1.2 copy-start.17
  72.5 1.4 copy-start.16
  73.6 27.5 %collective-permute-start.8 = (bf16[2,64,2048]{2,1,0:T(8,128)(2,1)S(1)}, bf16[2,64,2048]{2,1,0:T(8,128)(2,1)S(1)}, u32[]{:S(2)}, u32[]{:S(2)}) collective-permute-start(bf16[2,64,2048]{2,1,0:T(8,128)(2,1)S(1)} %copy-done.18), channel_id=1, source_target_pairs={{0,4},{4,8},{8,12},{12,0},{1,5},{5,9},{9,13},{13,1},{2,6},{6,10},{... | collective-permute-start | bytes 1572872 | tf_op jit(solution)/shard_map/ppermute | solution.py:377
  73.7 43.7 %collective-permute-start.9 = (bf16[2,64,2048]{2,1,0:T(8,128)(2,1)S(1)}, bf16[2,64,2048]{2,1,0:T(8,128)(2,1)S(1)}, u32[]{:S(2)}, u32[]{:S(2)}) collective-permute-start(bf16[2,64,2048]{2,1,0:T(8,128)(2,1)S(1)} %copy-done.17), channel_id=1, source_target_pairs={{0,8},{4,12},{8,0},{12,4},{1,9},{5,13},{9,1},{13,5},{2,10},{6,14},... | collective-permute-start | bytes 1572872 | tf_op jit(solution)/shard_map/ppermute | solution.py:377
  73.9 67.7 %collective-permute-start.10 = (bf16[2,64,2048]{2,1,0:T(8,128)(2,1)S(1)}, bf16[2,64,2048]{2,1,0:T(8,128)(2,1)S(1)}, u32[]{:S(2)}, u32[]{:S(2)}) collective-permute-start(bf16[2,64,2048]{2,1,0:T(8,128)(2,1)S(1)} %copy-done.16), channel_id=1, source_target_pairs={{0,12},{4,0},{8,4},{12,8},{1,13},{5,1},{9,5},{13,9},{2,14},{6,2},{... | collective-permute-start | bytes 1572872 | tf_op jit(solution)/shard_map/ppermute | solution.py:377
  80.0 4.6 %collective-permute-start.6 = (bf16[4,64,128]{2,1,0:T(8,128)(2,1)}, bf16[4,64,128]{2,1,0:T(8,128)(2,1)S(1)}, u32[]{:S(2)}, u32[]{:S(2)}) collective-permute-start(bf16[4,64,128]{2,1,0:T(8,128)(2,1)} %get-tuple-element.30), channel_id=1, source_target_pairs={{0,1},{1,0},{2,3},{3,2},{4,5},{5,4},{6,7},{7,6},{8,9},{9,8},{10,11... | collective-permute-start | bytes 196616 | tf_op jit(solution)/shard_map/ppermute | solution.py:370
  85.5 3.5 %copy-start.12 = (bf16[4,64,128]{2,1,0:T(8,128)(2,1)}, bf16[4,64,128]{2,1,0:T(8,128)(2,1)S(1)}, u32[]{:S(2)}) copy-start(bf16[4,64,128]{2,1,0:T(8,128)(2,1)S(1)} %add_convert_fusion.1.refs_1_) | copy-start | bytes 196612
  85.5 3.5 %collective-permute-start.7 = (bf16[4,64,128]{2,1,0:T(8,128)(2,1)S(1)}, bf16[4,64,128]{2,1,0:T(8,128)(2,1)S(1)}, u32[]{:S(2)}, u32[]{:S(2)}) collective-permute-start(bf16[4,64,128]{2,1,0:T(8,128)(2,1)S(1)} %add_convert_fusion.1.refs_1_), channel_id=1, source_target_pairs={{0,2},{1,3},{2,0},{3,1},{4,6},{5,7},{6,4},{7,5},{8,10},{9,11},{10,... | collective-permute-start | bytes 196616 | tf_op jit(solution)/shard_map/ppermute | solution.py:374
  89.0 0.6 copy-start.14
  97.7 69.7 %collective-permute-start.13 = (bf16[2,64,2048]{2,1,0:T(8,128)(2,1)}, bf16[2,64,2048]{2,1,0:T(8,128)(2,1)S(1)}, u32[]{:S(2)}, u32[]{:S(2)}) collective-permute-start(bf16[2,64,2048]{2,1,0:T(8,128)(2,1)} %get-tuple-element.40), channel_id=1, source_target_pairs={{0,4},{4,8},{8,12},{12,0},{1,5},{5,9},{9,13},{13,1},{2,6},{6,10},{... | collective-permute-start | bytes 1572872 | tf_op jit(solution)/shard_map/ppermute | solution.py:377
  97.8 71.0 %collective-permute-start.14 = (bf16[2,64,2048]{2,1,0:T(8,128)(2,1)}, bf16[2,64,2048]{2,1,0:T(8,128)(2,1)S(1)}, u32[]{:S(2)}, u32[]{:S(2)}) collective-permute-start(bf16[2,64,2048]{2,1,0:T(8,128)(2,1)} %get-tuple-element.41), channel_id=1, source_target_pairs={{0,8},{4,12},{8,0},{12,4},{1,9},{5,13},{9,1},{13,5},{2,10},{6,14},... | collective-permute-start | bytes 1572872 | tf_op jit(solution)/shard_map/ppermute | solution.py:377
  101.1 40.5 %copy-start.5 = (bf16[2,64,2048]{2,1,0:T(8,128)(2,1)}, bf16[2,64,2048]{2,1,0:T(8,128)(2,1)S(1)}, u32[]{:S(2)}) copy-start(bf16[2,64,2048]{2,1,0:T(8,128)(2,1)S(1)} %collective-permute-done.8.refs_3_) | copy-start | bytes 1572868
  101.1 67.8 %collective-permute-start.15 = (bf16[2,64,2048]{2,1,0:T(8,128)(2,1)}, bf16[2,64,2048]{2,1,0:T(8,128)(2,1)S(1)}, u32[]{:S(2)}, u32[]{:S(2)}) collective-permute-start(bf16[2,64,2048]{2,1,0:T(8,128)(2,1)} %get-tuple-element.35.refs_6_), channel_id=1, source_target_pairs={{0,12},{4,0},{8,4},{12,8},{1,13},{5,1},{9,5},{13,9},{2,14},{6,2},{... | collective-permute-start | bytes 1572872 | tf_op jit(solution)/shard_map/ppermute | solution.py:377
  117.5 24.2 %copy-start.7 = (bf16[2,64,2048]{2,1,0:T(8,128)(2,1)}, bf16[2,64,2048]{2,1,0:T(8,128)(2,1)S(1)}, u32[]{:S(2)}) copy-start(bf16[2,64,2048]{2,1,0:T(8,128)(2,1)S(1)} %collective-permute-done.9.refs_4_) | copy-start | bytes 1572868
  141.6 0.8 copy-start.8
  147.3 1.7 collective-permute-start.11
  149.8 3.5 %copy-start.13 = (bf16[4,64,128]{2,1,0:T(8,128)(2,1)}, bf16[4,64,128]{2,1,0:T(8,128)(2,1)S(1)}, u32[]{:S(2)}) copy-start(bf16[4,64,128]{2,1,0:T(8,128)(2,1)S(1)} %add_convert_fusion.refs_1_) | copy-start | bytes 196612
  149.8 3.5 %collective-permute-start.12 = (bf16[4,64,128]{2,1,0:T(8,128)(2,1)S(1)}, bf16[4,64,128]{2,1,0:T(8,128)(2,1)S(1)}, u32[]{:S(2)}, u32[]{:S(2)}) collective-permute-start(bf16[4,64,128]{2,1,0:T(8,128)(2,1)S(1)} %add_convert_fusion.refs_1_), channel_id=1, source_target_pairs={{0,2},{1,3},{2,0},{3,1},{4,6},{5,7},{6,4},{7,5},{8,10},{9,11},{10,... | collective-permute-start | bytes 196616 | tf_op jit(solution)/shard_map/ppermute | solution.py:374
  153.3 0.6 copy-start.15
  162.0 42.5 %collective-permute-start.16 = (bf16[2,64,2048]{2,1,0:T(8,128)(2,1)}, bf16[2,64,2048]{2,1,0:T(8,128)(2,1)S(1)}, u32[]{:S(2)}, u32[]{:S(2)}) collective-permute-start(bf16[2,64,2048]{2,1,0:T(8,128)(2,1)} %get-tuple-element.44), channel_id=1, source_target_pairs={{0,4},{4,8},{8,12},{12,0},{1,5},{5,9},{9,13},{13,1},{2,6},{6,10},{... | collective-permute-start | bytes 1572872 | tf_op jit(solution)/shard_map/ppermute | solution.py:377
  162.1 45.8 %collective-permute-start.17 = (bf16[2,64,2048]{2,1,0:T(8,128)(2,1)}, bf16[2,64,2048]{2,1,0:T(8,128)(2,1)S(1)}, u32[]{:S(2)}, u32[]{:S(2)}) collective-permute-start(bf16[2,64,2048]{2,1,0:T(8,128)(2,1)} %get-tuple-element.45), channel_id=1, source_target_pairs={{0,8},{4,12},{8,0},{12,4},{1,9},{5,13},{9,1},{13,5},{2,10},{6,14},... | collective-permute-start | bytes 1572872 | tf_op jit(solution)/shard_map/ppermute | solution.py:377
  167.4 1.4 copy-start.3
  167.4 46.3 %collective-permute-start.18 = (bf16[2,64,2048]{2,1,0:T(8,128)(2,1)}, bf16[2,64,2048]{2,1,0:T(8,128)(2,1)S(1)}, u32[]{:S(2)}, u32[]{:S(2)}) collective-permute-start(bf16[2,64,2048]{2,1,0:T(8,128)(2,1)} %get-tuple-element.43.refs_5_), channel_id=1, source_target_pairs={{0,12},{4,0},{8,4},{12,8},{1,13},{5,1},{9,5},{13,9},{2,14},{6,2},{... | collective-permute-start | bytes 1572872 | tf_op jit(solution)/shard_map/ppermute | solution.py:377
  168.8 0.8 copy-start.4
  169.6 0.8 copy-start.6
  204.5 9.2 %copy-start.9 = (bf16[2,64,2048]{2,1,0:T(8,128)(2,1)}, bf16[2,64,2048]{2,1,0:T(8,128)(2,1)S(1)}, u32[]{:S(2)}) copy-start(bf16[2,64,2048]{2,1,0:T(8,128)(2,1)S(1)} %collective-permute-done.16.refs_2_) | copy-start | bytes 1572868
  207.9 5.8 %copy-start.10 = (bf16[2,64,2048]{2,1,0:T(8,128)(2,1)}, bf16[2,64,2048]{2,1,0:T(8,128)(2,1)S(1)}, u32[]{:S(2)}) copy-start(bf16[2,64,2048]{2,1,0:T(8,128)(2,1)S(1)} %collective-permute-done.17.refs_3_) | copy-start | bytes 1572868
  213.7 0.8 copy-start.11
Sparse Core Ops, SparseCore 0:
  9.6 58.8 all-gather.1
  72.7 71.3 reduce-scatter.1

commit v2 on v1

--- a/solution.py
+++ b/solution.py
@@ -55,11 +55,15 @@
     ]
     for read in reads:
         read.start()
-    for read, write in zip(reads, writes):
-        read.wait()
-        write.start()
-    for write in writes:
-        write.wait()
+
+    def finish_copies():
+        for read, write in zip(reads, writes):
+            read.wait()
+            write.start()
+        for write in writes:
+            write.wait()
+
+    return finish_copies
 
 
 def copies_of(table, count):
@@ -74,32 +78,35 @@
     n_dev, n_seg = rel_ref.shape
     n_own = table_ref.shape[0]
     me = me_ref[0]
+    spare = COLS - 1
     for c in range((n_dev - 1) * capacity):
-        plan_ref[SEND, c] = 0
-        plan_ref[TERM, c] = -1
-        plan_ref[GIVEN, c] = -1
-    spare = COLS - 1
-    for s in range(n_dev):
+        for row in (SEND, TERM, GIVEN):
+            plan_ref[row, c] = 0 if row == SEND else -1
+    for s in range(1, n_dev):
         slots = [rel_ref[s, k] for k in range(n_seg)]
-        owners = [lax.div(v, n_own) for v in slots]
-        for k in range(n_seg):
-            local = slots[k] - owners[k] * n_own
-            order = jnp.int32(0)
-            for q in range(k):
-                order = order + (owners[q] == owners[k]).astype(jnp.int32)
-            if s == 0:
-                away = lax.rem(owners[k] - me + n_dev, n_dev)
-                plan_ref[OWN, k] = jnp.where(away == 0, local, -1)
-                from_owner = (n_dev - away - 1) * capacity + order
-                plan_ref[SOURCE, k] = jnp.where(away == 0, local, n_own + from_owner)
-                plan_ref[TERM, jnp.where(away == 0, spare, (away - 1) * capacity + order)] = k
-            else:
-                mine = owners[k] == me
-                there = (n_dev - s - 1) * capacity + order
-                plan_ref[SEND, jnp.where(mine, there, spare)] = local
-                plan_ref[GIVEN, jnp.where(mine, (s - 1) * capacity + order, spare)] = local
+        order = jnp.int32(0)
+        for slot in slots:
+            mine = lax.div(slot, n_own) == me
+            local = slot - me * n_own
+            there = (n_dev - s - 1) * capacity + order
+            plan_ref[SEND, jnp.where(mine, there, spare)] = local
+            plan_ref[GIVEN, jnp.where(mine, (s - 1) * capacity + order, spare)] = local
+            order = order + mine.astype(jnp.int32)
     rows = [plan_ref[SEND, c] for c in range(len(outs) * capacity)]
-    copy_rows(rows, table_ref, outs, held, sem)
+    finish_copies = copy_rows(rows, table_ref, outs, held, sem)
+    slots = [rel_ref[0, k] for k in range(n_seg)]
+    owners = [lax.div(v, n_own) for v in slots]
+    for k in range(n_seg):
+        local = slots[k] - owners[k] * n_own
+        order = jnp.int32(0)
+        for q in range(k):
+            order = order + (owners[q] == owners[k]).astype(jnp.int32)
+        away = lax.rem(owners[k] - me + n_dev, n_dev)
+        plan_ref[OWN, k] = jnp.where(away == 0, local, -1)
+        from_owner = (n_dev - away - 1) * capacity + order
+        plan_ref[SOURCE, k] = jnp.where(away == 0, local, n_own + from_owner)
+        plan_ref[TERM, jnp.where(away == 0, spare, (away - 1) * capacity + order)] = k
+    finish_copies()
 
 
 def request(me, relative, table, capacity):
@@ -121,7 +128,7 @@
 def rows_kernel(row, plan_ref, table_ref, *rest):
     outs, (held, sem) = rest[:-2], rest[-2:]
     rows = [jnp.maximum(plan_ref[row, c], 0) for c in range(len(outs) * outs[0].shape[0])]
-    copy_rows(rows, table_ref, outs, held, sem)
+    copy_rows(rows, table_ref, outs, held, sem)()
 
 
 def rows_of(plan, row, table, count, capacity, after=()):
@@ -265,30 +272,40 @@
     )
 
 
-def forward_kernel(x_ref, w_ref, *rest):
-    out = jnp.dot(x_ref[...], w_ref[...], preferred_element_type=F32)
-    rest[-1][...] = out.astype(rest[-1].dtype)
-
-
-def forward(x, weight, first, last, done=None, after=()):
+def forward_kernel(x_ref, w_ref, out_ref):
+    out_ref[...] = jnp.dot(x_ref[...], w_ref[...], preferred_element_type=F32).astype(out_ref.dtype)
+
+
+def forward(x, weight, after=()):
     rows, width = x.shape
     full = weight.shape[1]
-    args = [x, weight] + ([] if done is None else [done])
     return call(
         forward_kernel,
-        args,
+        (x, weight),
         [
             pl.BlockSpec((rows, width), lambda j: (0, 0)),
-            pl.BlockSpec((width, TILE), lambda j: (0, first + j)),
-        ]
-        + [ANYWHERE] * (len(args) - 2),
-        after,
-        grid=(last - first,),
+            pl.BlockSpec((width, TILE), lambda j: (0, j)),
+        ],
+        after,
+        grid=(full // TILE,),
         out_shape=jax.ShapeDtypeStruct((rows, full), BF16),
-        out_specs=pl.BlockSpec((rows, TILE), lambda j: (0, first + j)),
-        input_output_aliases={} if done is None else {2: 0},
-        cost_estimate=cost(2 * rows * width * (last - first) * TILE, 2 * width * full),
+        out_specs=pl.BlockSpec((rows, TILE), lambda j: (0, j)),
+        cost_estimate=cost(2 * rows * width * full, 2 * width * full),
         name="forward",
+    )
+
+
+def held_back(x, after):
+    return call(
+        lambda x_ref, out_ref: None,
+        (x,),
+        [ANYWHERE],
+        after,
+        out_shape=jax.ShapeDtypeStruct(x.shape, x.dtype),
+        out_specs=ANYWHERE,
+        input_output_aliases={0: 0},
+        cost_estimate=cost(0, 0),
+        name="held_back",
     )
 
 
@@ -393,9 +410,7 @@
     sends = rows_of(plan, SEND, up_table, n_dev - 1, capacity, [sends[-1]])
     up_got = [over_line(x, s) for x, s in zip(sends, shifts)]
 
-    tiles = weight.shape[1] // TILE
-    partial = forward(tokens, weight, 0, tiles - 1, after=[sends[-1]])
-    partial = forward(tokens, weight, tiles - 1, tiles, partial, down_got)
+    partial = held_back(forward(tokens, weight, [sends[-1]]), down_got)
     layer = lax.psum_scatter(partial, "tensor", scatter_dimension=1, tiled=True)
 
     def summed(part):

time: 227 us -> 222 us (0.978)
  Pallas kernels: 102 us -> 99.6 us
    pallas_call x14, Pallas kernels: 102 us -> 99.6 us  [call(): pl.pallas_call(body, grid_spec=pltpu.PrefetchScalarGridSpec(num_scalar_pr...]
  transfers between devices with their start and end apart: 21 -> 21, of which waited for: 11 -> 11; matrix products, arithmetic and copies ran while one was open for 1% -> 1% of each run, Pallas kernels for 44% -> 43%
where the time goes in v2:
time: 222 us; the launch traced here: 221 us
  Pallas kernels  99.6 us (45%)
  waiting for transfers between devices  73.5 us (33%)
  starting transfers between devices  24.1 us (11%)
  between operations  14.2 us (6%)
  local copies, waits for them, and re-layouts  6.61 us (3%)
  other arithmetic  2.53 us (1%)
    pallas_call x14, Pallas kernels, call(): pl.pallas_call(body, grid_spec=pltpu.PrefetchScalarGridSpec(num_scalar_pr...  99.6 us
    ppermute x15, waiting for transfers between devices, over_line(): return lax.ppermute(x, 'dp', [(i, (i + s) % n_dev) for i in range(n_dev)])  64.3 us
    ppermute x15, starting transfers between devices, over_line(): return lax.ppermute(x, 'dp', [(i, (i + s) % n_dev) for i in range(n_dev)])  19 us
    unnamed x42, local copies, waits for them, and re-layouts  6.61 us
    ppermute x2, waiting for transfers between devices, over_chips(): return lax.ppermute(x, 'tensor', pairs)  6.34 us
  transfers between devices with their start and end apart: 21, of which 11 were waited for; matrix products, arithmetic and copies ran while one was open for 1% of the time, Pallas kernels for 43%

profile of v2, /device:TPU:13, one launch (start us, length us, event | category | flops | bytes accessed | tf_op | source)
XLA Modules:
  0.0 220.6 jit_solution(10041050361996982182)
XLA Ops:
  7.2 0.0 all-gather.2.cloned.1.call-start
  7.2 0.7 all-gather.2.cloned.1.call-update
  7.9 0.0 reduce-scatter.2.cloned.1.call-start
  8.0 0.2 select_reduce_fusion
  8.2 0.2 collective-permute-start.2
  8.4 2.3 %collective-permute-start.1 = (s32[4]{0:T(128)S(1)}, s32[4]{0:T(128)S(1)}, u32[]{:S(2)}, u32[]{:S(2)}) collective-permute-start(s32[4]{0:T(128)S(1)} %select_reduce_fusion), channel_id=1, source_target_pairs={{0,8},{4,12},{8,0},{12,4},{1,9},{5,13},{9,1},{13,5},{2,10},{6,14},... | collective-permute-start | bytes 56 | tf_op jit(solution)/shard_map/ppermute | solution.py:394
  10.7 2.2 collective-permute-start
  12.9 0.0 collective-permute-done.1
  12.9 0.7 collective-permute-done
  13.6 0.6 pad_add_fusion.refs_1_
  14.2 4.0 %request.1 = (bf16[2,64,2048]{2,1,0:T(8,128)(2,1)}, bf16[2,64,2048]{2,1,0:T(8,128)(2,1)}, bf16[2,64,2048]{2,1,0:T(8,128)(2,1)}, s32[8,128]{1,0:T(8,128)}) custom-call(s32[1]{0:T(128)} %bitcast.refs_0_, s32[4,4]{1,0:T(4,128)} %pad_add_fusion.refs_1_, bf16[4,64,2048]{2,1,0:T(8,128)(2,1)} %bitcast.7), custom_call_target="tpu_custom_call" | custom-call | bytes 2097152 | tf_op jit(solution)/shard_map/request/pallas_call | solution.py:32
  18.2 1.8 collective-permute-start.3
  20.0 2.3 %collective-permute-start.4 = (bf16[2,64,2048]{2,1,0:T(8,128)(2,1)}, bf16[2,64,2048]{2,1,0:T(8,128)(2,1)S(1)}, u32[]{:S(2)}, u32[]{:S(2)}) collective-permute-start(bf16[2,64,2048]{2,1,0:T(8,128)(2,1)} %get-tuple-element.29), channel_id=1, source_target_pairs={{0,8},{4,12},{8,0},{12,4},{1,9},{5,13},{9,1},{13,5},{2,10},{6,14},... | collective-permute-start | bytes 1572872 | tf_op jit(solution)/shard_map/ppermute | solution.py:394
  22.3 0.0 collective-permute-start.5
  22.3 3.7 %rows.3 = (bf16[2,64,2048]{2,1,0:T(8,128)(2,1)}, bf16[2,64,2048]{2,1,0:T(8,128)(2,1)}, bf16[2,64,2048]{2,1,0:T(8,128)(2,1)}) custom-call(s32[8,128]{1,0:T(8,128)} %get-tuple-element.25.refs_0_, bf16[4,64,2048]{2,1,0:T(8,128)(2,1)} %refs_2_.1, bf16[2,64,2048]{2,1,0:T(8,128)(2,1)} %get-tuple-element.26.refs_2_), custom_call_target="tpu_custom_call" | custom-call | bytes 2097152 | tf_op jit(solution)/shard_map/rows/pallas_call | solution.py:32
  26.1 27.7 %forward.1.refs_0_ = bf16[512,8192]{1,0:T(8,128)(2,1)} custom-call(bf16[512,2048]{1,0:T(8,128)(2,1)} %refs_3_.3, bf16[2048,8192]{1,0:T(8,128)(2,1)} %refs_1_.9, bf16[2,64,2048]{2,1,0:T(8,128)(2,1)} %get-tuple-element.27.refs_2_), custom_call_target="tpu_custom_call" | custom-call | flops 17179869184 | bytes 33554432 | tf_op jit(solution)/shard_map/forward/pallas_call | solution.py:32
  53.8 9.1 %collective-permute-done.4.refs_2_.refs_4_ = bf16[2,64,2048]{2,1,0:T(8,128)(2,1)S(1)} collective-permute-done((bf16[2,64,2048]{2,1,0:T(8,128)(2,1)}, bf16[2,64,2048]{2,1,0:T(8,128)(2,1)S(1)}, u32[]{:S(2)}, u32[]{:S(2)}) %collective-permute-start.4) | collective-permute-done | bytes 524320 | tf_op jit(solution)/shard_map/ppermute | solution.py:394
  62.9 4.1 %collective-permute-done.5.refs_3_.refs_5_ = bf16[2,64,2048]{2,1,0:T(8,128)(2,1)S(1)} collective-permute-done((bf16[2,64,2048]{2,1,0:T(8,128)(2,1)}, bf16[2,64,2048]{2,1,0:T(8,128)(2,1)S(1)}, u32[]{:S(2)}, u32[]{:S(2)}) %collective-permute-start.5) | collective-permute-done | bytes 524320 | tf_op jit(solution)/shard_map/ppermute | solution.py:394
  67.0 0.8 copy-done.2
  67.8 0.0 reduce-scatter.2.cloned.1.call-update
  67.8 1.0 copy-done.18
  68.8 0.2 copy-done.17
  69.0 0.2 copy-done.16
  69.1 1.2 collective-permute-start.10
  70.3 4.8 %low_rank.2 = (bf16[4,64,2048]{2,1,0:T(8,128)(2,1)}, bf16[4,64,128]{2,1,0:T(8,128)(2,1)}) custom-call(s32[8,128]{1,0:T(8,128)} %get-tuple-element.25.refs_0_, bf16[512,2048]{1,0:T(8,128)(2,1)} %refs_3_.3, bf16[4,64,2048]{2,1,0:T(8,128)(2,1)} %bitcast.8, bf16[2,64,2048]{2,1,0:T(8,128)(2,1)} %copy-done, bf16[2,64,2048]{2,1,0:T(8,128)(2,1)} %copy-done.1, ...), custom_call_target="tpu_custom_call" | custom-call | flops 134217728 | bytes 4194304 | tf_op jit(solution)/shard_map/low_rank/pallas_call | solution.py:32
  75.2 3.8 %collective-permute-start.6 = (bf16[4,64,128]{2,1,0:T(8,128)(2,1)}, bf16[4,64,128]{2,1,0:T(8,128)(2,1)S(1)}, u32[]{:S(2)}, u32[]{:S(2)}) collective-permute-start(bf16[4,64,128]{2,1,0:T(8,128)(2,1)} %get-tuple-element.30), channel_id=1, source_target_pairs={{0,1},{1,0},{2,3},{3,2},{4,5},{5,4},{6,7},{7,6},{8,9},{9,8},{10,11... | collective-permute-start | bytes 196616 | tf_op jit(solution)/shard_map/ppermute | solution.py:387
  79.0 1.1 collective-permute-done.6
  80.1 0.9 add_convert_fusion.1.refs_1_
  81.1 0.0 copy-start.12
  81.1 0.3 collective-permute-start.7
  81.4 3.2 %collective-permute-done.7.refs_2_ = bf16[4,64,128]{2,1,0:T(8,128)(2,1)S(1)} collective-permute-done((bf16[4,64,128]{2,1,0:T(8,128)(2,1)S(1)}, bf16[4,64,128]{2,1,0:T(8,128)(2,1)S(1)}, u32[]{:S(2)}, u32[]{:S(2)}) %collective-permute-start.7) | collective-permute-done | bytes 65568 | tf_op jit(solution)/shard_map/ppermute | solution.py:391
  84.5 0.6 copy-done.14
  85.2 4.9 %terms.2 = (bf16[4,64,128]{2,1,0:T(8,128)(2,1)}, bf16[4,64,2048]{2,1,0:T(8,128)(2,1)}) custom-call(s32[4]{0:T(128)} %refs_0_.5, bf16[4,64,128]{2,1,0:T(8,128)(2,1)} %copy-done.12, bf16[4,64,128]{2,1,0:T(8,128)(2,1)} %copy-done.14, bf16[512,2048]{1,0:T(8,128)(2,1)} %refs_1_.8), custom_call_target="tpu_custom_call" | custom-call | flops 134217728 | bytes 4194304 | tf_op jit(solution)/shard_map/terms/pallas_call | solution.py:32
  90.1 3.4 %rows.4 = (bf16[2,64,2048]{2,1,0:T(8,128)(2,1)}, bf16[2,64,2048]{2,1,0:T(8,128)(2,1)}, bf16[2,64,2048]{2,1,0:T(8,128)(2,1)}) custom-call(s32[8,128]{1,0:T(8,128)} %get-tuple-element.25.refs_0_, bf16[4,64,2048]{2,1,0:T(8,128)(2,1)} %get-tuple-element.34.refs_1_), custom_call_target="tpu_custom_call" | custom-call | bytes 2097152 | tf_op jit(solution)/shard_map/rows/pallas_call | solution.py:32
  93.5 0.1 collective-permute-start.13
  93.6 2.5 %collective-permute-start.14 = (bf16[2,64,2048]{2,1,0:T(8,128)(2,1)}, bf16[2,64,2048]{2,1,0:T(8,128)(2,1)S(1)}, u32[]{:S(2)}, u32[]{:S(2)}) collective-permute-start(bf16[2,64,2048]{2,1,0:T(8,128)(2,1)} %get-tuple-element.41), channel_id=1, source_target_pairs={{0,8},{4,12},{8,0},{12,4},{1,9},{5,13},{9,1},{13,5},{2,10},{6,14},... | collective-permute-start | bytes 1572872 | tf_op jit(solution)/shard_map/ppermute | solution.py:394
  96.1 0.0 collective-permute-done.8.refs_3_
  96.1 16.6 %collective-permute-done.9.refs_4_ = bf16[2,64,2048]{2,1,0:T(8,128)(2,1)S(1)} collective-permute-done((bf16[2,64,2048]{2,1,0:T(8,128)(2,1)S(1)}, bf16[2,64,2048]{2,1,0:T(8,128)(2,1)S(1)}, u32[]{:S(2)}, u32[]{:S(2)}) %collective-permute-start.9) | collective-permute-done | bytes 524320 | tf_op jit(solution)/shard_map/ppermute | solution.py:394
  112.7 24.6 %collective-permute-done.10.refs_5_ = bf16[2,64,2048]{2,1,0:T(8,128)(2,1)S(1)} collective-permute-done((bf16[2,64,2048]{2,1,0:T(8,128)(2,1)S(1)}, bf16[2,64,2048]{2,1,0:T(8,128)(2,1)S(1)}, u32[]{:S(2)}, u32[]{:S(2)}) %collective-permute-start.10) | collective-permute-done | bytes 524320 | tf_op jit(solution)/shard_map/ppermute | solution.py:394
  137.3 0.8 copy-done.8
  138.1 4.8 %low_rank.3 = (bf16[4,64,2048]{2,1,0:T(8,128)(2,1)}, bf16[4,64,128]{2,1,0:T(8,128)(2,1)}) custom-call(s32[8,128]{1,0:T(8,128)} %get-tuple-element.25.refs_0_, bf16[512,2048]{1,0:T(8,128)(2,1)} %refs_1_.8, bf16[4,64,2048]{2,1,0:T(8,128)(2,1)} %refs_2_.1, bf16[2,64,2048]{2,1,0:T(8,128)(2,1)} %copy-done.5, bf16[2,64,2048]{2,1,0:T(8,128)(2,1)} %copy-done.7, ...), custom_call_target="tpu_custom_call" | custom-call | flops 134217728 | bytes 4194304 | tf_op jit(solution)/shard_map/low_rank/pallas_call | solution.py:32
  142.9 0.5 collective-permute-start.11
  143.5 1.1 collective-permute-done.11
  144.6 0.9 add_convert_fusion.refs_1_
  145.4 0.0 copy-start.13
  145.4 0.3 collective-permute-start.12
  145.7 3.2 %collective-permute-done.12.refs_2_ = bf16[4,64,128]{2,1,0:T(8,128)(2,1)S(1)} collective-permute-done((bf16[4,64,128]{2,1,0:T(8,128)(2,1)S(1)}, bf16[4,64,128]{2,1,0:T(8,128)(2,1)S(1)}, u32[]{:S(2)}, u32[]{:S(2)}) %collective-permute-start.12) | collective-permute-done | bytes 65568 | tf_op jit(solution)/shard_map/ppermute | solution.py:391
  148.9 0.6 copy-done.15
  149.6 4.7 %terms.3 = (bf16[4,64,128]{2,1,0:T(8,128)(2,1)}, bf16[4,64,2048]{2,1,0:T(8,128)(2,1)}) custom-call(s32[4]{0:T(128)} %refs_0_.5, bf16[4,64,128]{2,1,0:T(8,128)(2,1)} %copy-done.13, bf16[4,64,128]{2,1,0:T(8,128)(2,1)} %copy-done.15, bf16[512,2048]{1,0:T(8,128)(2,1)} %refs_3_.3), custom_call_target="tpu_custom_call" | custom-call | flops 134217728 | bytes 4194304 | tf_op jit(solution)/shard_map/terms/pallas_call | solution.py:32
  154.3 3.4 %rows.5 = (bf16[2,64,2048]{2,1,0:T(8,128)(2,1)}, bf16[2,64,2048]{2,1,0:T(8,128)(2,1)}, bf16[2,64,2048]{2,1,0:T(8,128)(2,1)}) custom-call(s32[8,128]{1,0:T(8,128)} %get-tuple-element.25.refs_0_, bf16[4,64,2048]{2,1,0:T(8,128)(2,1)} %get-tuple-element.42.refs_1_), custom_call_target="tpu_custom_call" | custom-call | bytes 2097152 | tf_op jit(solution)/shard_map/rows/pallas_call | solution.py:32
  157.6 0.1 collective-permute-start.16
  157.7 5.0 %collective-permute-start.17 = (bf16[2,64,2048]{2,1,0:T(8,128)(2,1)}, bf16[2,64,2048]{2,1,0:T(8,128)(2,1)S(1)}, u32[]{:S(2)}, u32[]{:S(2)}) collective-permute-start(bf16[2,64,2048]{2,1,0:T(8,128)(2,1)} %get-tuple-element.45), channel_id=1, source_target_pairs={{0,8},{4,12},{8,0},{12,4},{1,9},{5,13},{9,1},{13,5},{2,10},{6,14},... | collective-permute-start | bytes 1572872 | tf_op jit(solution)/shard_map/ppermute | solution.py:394
  162.7 1.4 collective-permute-start.18
  164.1 0.0 collective-permute-done.14.refs_3_
  164.1 0.0 collective-permute-done.15.refs_4_
  164.1 0.8 copy-done.4
  164.9 0.8 copy-done.6
  165.7 4.0 %totals.2.refs_4_ = f32[4,64,2048]{2,1,0:T(8,128)} custom-call(s32[8,128]{1,0:T(8,128)} %get-tuple-element.25.refs_0_, bf16[4,64,2048]{2,1,0:T(8,128)(2,1)} %get-tuple-element.34.refs_1_, bf16[2,64,2048]{2,1,0:T(8,128)(2,1)} %copy-done.3, bf16[2,64,2048]{2,1,0:T(8,128)(2,1)} %copy-done.4, bf16[2,64,2048]{2,1,0:T(8,128)(2,1)} %copy-done.6, ...), custom_call_target="tpu_custom_call" | custom-call | bytes 2097152 | tf_op jit(solution)/shard_map/totals/pallas_call | solution.py:32
  169.7 25.5 %backward.1.refs_3_ = bf16[512,2048]{1,0:T(8,128)(2,1)} custom-call(bf16[512,8192]{1,0:T(8,128)(2,1)} %all-gather.2.cloned.1.call-done.refs_0_, bf16[2048,8192]{1,0:T(8,128)(2,1)} %refs_1_.9, bf16[4,64,128]{2,1,0:T(8,128)(2,1)} %get-tuple-element.38.refs_2_, bf16[4,64,2048]{2,1,0:T(8,128)(2,1)} %get-tuple-element.39.refs_3_, f32[4,64,2048]{2,1,0:T(8,128)} %totals.2.refs_4_), custom_call_target="tpu_custom_call" | custom-call | flops 17179869184 | bytes 33554432 | tf_op jit(solution)/shard_map/backward/pallas_call | solution.py:32
  195.2 4.5 %adapt.1.refs_5_ = bf16[512,2048]{1,0:T(8,128)(2,1)} custom-call(bf16[512,2048]{1,0:T(8,128)(2,1)} %reduce-scatter.2.cloned.1.call-done.refs_0_, bf16[4,64,128]{2,1,0:T(8,128)(2,1)} %get-tuple-element.31.refs_1_, bf16[4,64,2048]{2,1,0:T(8,128)(2,1)} %get-tuple-element.36.refs_2_, bf16[512,2048]{1,0:T(8,128)(2,1)} %backward.1.refs_3_), custom_call_target="tpu_custom_call" | custom-call | flops 134217728 | bytes 4194304 | tf_op jit(solution)/shard_map/adapt/pallas_call | solution.py:32
  199.7 3.8 %collective-permute-done.17.refs_3_ = bf16[2,64,2048]{2,1,0:T(8,128)(2,1)S(1)} collective-permute-done((bf16[2,64,2048]{2,1,0:T(8,128)(2,1)}, bf16[2,64,2048]{2,1,0:T(8,128)(2,1)S(1)}, u32[]{:S(2)}, u32[]{:S(2)}) %collective-permute-start.17) | collective-permute-done | bytes 524320 | tf_op jit(solution)/shard_map/ppermute | solution.py:394
  203.5 5.4 %collective-permute-done.18.refs_4_ = bf16[2,64,2048]{2,1,0:T(8,128)(2,1)S(1)} collective-permute-done((bf16[2,64,2048]{2,1,0:T(8,128)(2,1)}, bf16[2,64,2048]{2,1,0:T(8,128)(2,1)S(1)}, u32[]{:S(2)}, u32[]{:S(2)}) %collective-permute-start.18) | collective-permute-done | bytes 524320 | tf_op jit(solution)/shard_map/ppermute | solution.py:394
  208.9 0.8 copy-done.11
  209.7 4.0 %totals.3 = f32[4,64,2048]{2,1,0:T(8,128)} custom-call(s32[8,128]{1,0:T(8,128)} %get-tuple-element.25.refs_0_, bf16[4,64,2048]{2,1,0:T(8,128)(2,1)} %get-tuple-element.42.refs_1_, bf16[2,64,2048]{2,1,0:T(8,128)(2,1)} %copy-done.9, bf16[2,64,2048]{2,1,0:T(8,128)(2,1)} %copy-done.10, bf16[2,64,2048]{2,1,0:T(8,128)(2,1)} %copy-done.11, ...), custom_call_target="tpu_custom_call" | custom-call | bytes 2097152 | tf_op jit(solution)/shard_map/totals/pallas_call | solution.py:32
  (40 shorter events, 0.1 us)
Async XLA Ops:
  7.2 0.8 copy-start.19
  7.2 0.8 copy-start.20
  7.2 162.5 %all-gather.2.cloned.1.call-start = ((), (), s32[]{:S(2)}) async-start(), calls=%async_computation.2 | async-start | bytes 10485760 | tf_op jit(solution)/shard_map/all_gather | solution.py:399
  7.9 187.3 %reduce-scatter.2.cloned.1.call-start = ((), (), s32[]{:S(2)}) async-start(), calls=%async_computation.1 | async-start | bytes 10485760 | tf_op jit(solution)/shard_map/reduce_scatter | solution.py:414
  8.2 4.7 %collective-permute-start.2 = (s32[4]{0:T(128)S(1)}, s32[4]{0:T(128)S(1)}, u32[]{:S(2)}, u32[]{:S(2)}) collective-permute-start(s32[4]{0:T(128)S(1)} %select_reduce_fusion), channel_id=1, source_target_pairs={{0,12},{4,0},{8,4},{12,8},{1,13},{5,1},{9,5},{13,9},{2,14},{6,2},{... | collective-permute-start | bytes 56 | tf_op jit(solution)/shard_map/ppermute | solution.py:394
  8.4 4.5 %collective-permute-start.1 = (s32[4]{0:T(128)S(1)}, s32[4]{0:T(128)S(1)}, u32[]{:S(2)}, u32[]{:S(2)}) collective-permute-start(s32[4]{0:T(128)S(1)} %select_reduce_fusion), channel_id=1, source_target_pairs={{0,8},{4,12},{8,0},{12,4},{1,9},{5,13},{9,1},{13,5},{2,10},{6,14},... | collective-permute-start | bytes 56 | tf_op jit(solution)/shard_map/ppermute | solution.py:394
  10.7 2.9 %collective-permute-start = (s32[4]{0:T(128)S(1)}, s32[4]{0:T(128)S(1)}, u32[]{:S(2)}, u32[]{:S(2)}) collective-permute-start(s32[4]{0:T(128)S(1)} %select_reduce_fusion), channel_id=1, source_target_pairs={{0,4},{4,8},{8,12},{12,0},{1,5},{5,9},{9,13},{13,1},{2,6},{6,10},{... | collective-permute-start | bytes 56 | tf_op jit(solution)/shard_map/ppermute | solution.py:394
  18.2 35.5 %collective-permute-start.3 = (bf16[2,64,2048]{2,1,0:T(8,128)(2,1)}, bf16[2,64,2048]{2,1,0:T(8,128)(2,1)S(1)}, u32[]{:S(2)}, u32[]{:S(2)}) collective-permute-start(bf16[2,64,2048]{2,1,0:T(8,128)(2,1)} %get-tuple-element.28), channel_id=1, source_target_pairs={{0,4},{4,8},{8,12},{12,0},{1,5},{5,9},{9,13},{13,1},{2,6},{6,10},{... | collective-permute-start | bytes 1572872 | tf_op jit(solution)/shard_map/ppermute | solution.py:394
  20.0 42.9 %collective-permute-start.4 = (bf16[2,64,2048]{2,1,0:T(8,128)(2,1)}, bf16[2,64,2048]{2,1,0:T(8,128)(2,1)S(1)}, u32[]{:S(2)}, u32[]{:S(2)}) collective-permute-start(bf16[2,64,2048]{2,1,0:T(8,128)(2,1)} %get-tuple-element.29), channel_id=1, source_target_pairs={{0,8},{4,12},{8,0},{12,4},{1,9},{5,13},{9,1},{13,5},{2,10},{6,14},... | collective-permute-start | bytes 1572872 | tf_op jit(solution)/shard_map/ppermute | solution.py:394
  22.3 44.6 %collective-permute-start.5 = (bf16[2,64,2048]{2,1,0:T(8,128)(2,1)}, bf16[2,64,2048]{2,1,0:T(8,128)(2,1)S(1)}, u32[]{:S(2)}, u32[]{:S(2)}) collective-permute-start(bf16[2,64,2048]{2,1,0:T(8,128)(2,1)} %get-tuple-element.26.refs_2_), channel_id=1, source_target_pairs={{0,12},{4,0},{8,4},{12,8},{1,13},{5,1},{9,5},{13,9},{2,14},{6,2},{... | collective-permute-start | bytes 1572872 | tf_op jit(solution)/shard_map/ppermute | solution.py:394
  53.8 13.2 %copy-start = (bf16[2,64,2048]{2,1,0:T(8,128)(2,1)}, bf16[2,64,2048]{2,1,0:T(8,128)(2,1)S(1)}, u32[]{:S(2)}) copy-start(bf16[2,64,2048]{2,1,0:T(8,128)(2,1)S(1)} %collective-permute-done.3.refs_1_.refs_3_) | copy-start | bytes 1572868
  62.9 4.1 %copy-start.1 = (bf16[2,64,2048]{2,1,0:T(8,128)(2,1)}, bf16[2,64,2048]{2,1,0:T(8,128)(2,1)S(1)}, u32[]{:S(2)}) copy-start(bf16[2,64,2048]{2,1,0:T(8,128)(2,1)S(1)} %collective-permute-done.4.refs_2_.refs_4_) | copy-start | bytes 1572868
  67.0 0.8 copy-start.2
  67.8 1.0 copy-start.18
  67.8 1.2 copy-start.17
  67.8 1.4 copy-start.16
  68.8 27.3 %collective-permute-start.8 = (bf16[2,64,2048]{2,1,0:T(8,128)(2,1)S(1)}, bf16[2,64,2048]{2,1,0:T(8,128)(2,1)S(1)}, u32[]{:S(2)}, u32[]{:S(2)}) collective-permute-start(bf16[2,64,2048]{2,1,0:T(8,128)(2,1)S(1)} %copy-done.18), channel_id=1, source_target_pairs={{0,4},{4,8},{8,12},{12,0},{1,5},{5,9},{9,13},{13,1},{2,6},{6,10},{... | collective-permute-start | bytes 1572872 | tf_op jit(solution)/shard_map/ppermute | solution.py:394
  69.0 43.7 %collective-permute-start.9 = (bf16[2,64,2048]{2,1,0:T(8,128)(2,1)S(1)}, bf16[2,64,2048]{2,1,0:T(8,128)(2,1)S(1)}, u32[]{:S(2)}, u32[]{:S(2)}) collective-permute-start(bf16[2,64,2048]{2,1,0:T(8,128)(2,1)S(1)} %copy-done.17), channel_id=1, source_target_pairs={{0,8},{4,12},{8,0},{12,4},{1,9},{5,13},{9,1},{13,5},{2,10},{6,14},... | collective-permute-start | bytes 1572872 | tf_op jit(solution)/shard_map/ppermute | solution.py:394
  69.1 68.1 %collective-permute-start.10 = (bf16[2,64,2048]{2,1,0:T(8,128)(2,1)S(1)}, bf16[2,64,2048]{2,1,0:T(8,128)(2,1)S(1)}, u32[]{:S(2)}, u32[]{:S(2)}) collective-permute-start(bf16[2,64,2048]{2,1,0:T(8,128)(2,1)S(1)} %copy-done.16), channel_id=1, source_target_pairs={{0,12},{4,0},{8,4},{12,8},{1,13},{5,1},{9,5},{13,9},{2,14},{6,2},{... | collective-permute-start | bytes 1572872 | tf_op jit(solution)/shard_map/ppermute | solution.py:394
  75.2 5.0 %collective-permute-start.6 = (bf16[4,64,128]{2,1,0:T(8,128)(2,1)}, bf16[4,64,128]{2,1,0:T(8,128)(2,1)S(1)}, u32[]{:S(2)}, u32[]{:S(2)}) collective-permute-start(bf16[4,64,128]{2,1,0:T(8,128)(2,1)} %get-tuple-element.30), channel_id=1, source_target_pairs={{0,1},{1,0},{2,3},{3,2},{4,5},{5,4},{6,7},{7,6},{8,9},{9,8},{10,11... | collective-permute-start | bytes 196616 | tf_op jit(solution)/shard_map/ppermute | solution.py:387
  81.1 3.5 %copy-start.12 = (bf16[4,64,128]{2,1,0:T(8,128)(2,1)}, bf16[4,64,128]{2,1,0:T(8,128)(2,1)S(1)}, u32[]{:S(2)}) copy-start(bf16[4,64,128]{2,1,0:T(8,128)(2,1)S(1)} %add_convert_fusion.1.refs_1_) | copy-start | bytes 196612
  81.1 3.5 %collective-permute-start.7 = (bf16[4,64,128]{2,1,0:T(8,128)(2,1)S(1)}, bf16[4,64,128]{2,1,0:T(8,128)(2,1)S(1)}, u32[]{:S(2)}, u32[]{:S(2)}) collective-permute-start(bf16[4,64,128]{2,1,0:T(8,128)(2,1)S(1)} %add_convert_fusion.1.refs_1_), channel_id=1, source_target_pairs={{0,2},{1,3},{2,0},{3,1},{4,6},{5,7},{6,4},{7,5},{8,10},{9,11},{10,... | collective-permute-start | bytes 196616 | tf_op jit(solution)/shard_map/ppermute | solution.py:391
  84.5 0.6 copy-start.14
  93.5 69.2 %collective-permute-start.13 = (bf16[2,64,2048]{2,1,0:T(8,128)(2,1)}, bf16[2,64,2048]{2,1,0:T(8,128)(2,1)S(1)}, u32[]{:S(2)}, u32[]{:S(2)}) collective-permute-start(bf16[2,64,2048]{2,1,0:T(8,128)(2,1)} %get-tuple-element.40), channel_id=1, source_target_pairs={{0,4},{4,8},{8,12},{12,0},{1,5},{5,9},{9,13},{13,1},{2,6},{6,10},{... | collective-permute-start | bytes 1572872 | tf_op jit(solution)/shard_map/ppermute | solution.py:394
  93.6 70.5 %collective-permute-start.14 = (bf16[2,64,2048]{2,1,0:T(8,128)(2,1)}, bf16[2,64,2048]{2,1,0:T(8,128)(2,1)S(1)}, u32[]{:S(2)}, u32[]{:S(2)}) collective-permute-start(bf16[2,64,2048]{2,1,0:T(8,128)(2,1)} %get-tuple-element.41), channel_id=1, source_target_pairs={{0,8},{4,12},{8,0},{12,4},{1,9},{5,13},{9,1},{13,5},{2,10},{6,14},... | collective-permute-start | bytes 1572872 | tf_op jit(solution)/shard_map/ppermute | solution.py:394
  96.1 41.1 %copy-start.5 = (bf16[2,64,2048]{2,1,0:T(8,128)(2,1)}, bf16[2,64,2048]{2,1,0:T(8,128)(2,1)S(1)}, u32[]{:S(2)}) copy-start(bf16[2,64,2048]{2,1,0:T(8,128)(2,1)S(1)} %collective-permute-done.8.refs_3_) | copy-start | bytes 1572868
  96.1 67.9 %collective-permute-start.15 = (bf16[2,64,2048]{2,1,0:T(8,128)(2,1)}, bf16[2,64,2048]{2,1,0:T(8,128)(2,1)S(1)}, u32[]{:S(2)}, u32[]{:S(2)}) collective-permute-start(bf16[2,64,2048]{2,1,0:T(8,128)(2,1)} %get-tuple-element.35.refs_6_), channel_id=1, source_target_pairs={{0,12},{4,0},{8,4},{12,8},{1,13},{5,1},{9,5},{13,9},{2,14},{6,2},{... | collective-permute-start | bytes 1572872 | tf_op jit(solution)/shard_map/ppermute | solution.py:394
  112.7 24.6 %copy-start.7 = (bf16[2,64,2048]{2,1,0:T(8,128)(2,1)}, bf16[2,64,2048]{2,1,0:T(8,128)(2,1)S(1)}, u32[]{:S(2)}) copy-start(bf16[2,64,2048]{2,1,0:T(8,128)(2,1)S(1)} %collective-permute-done.9.refs_4_) | copy-start | bytes 1572868
  137.3 0.8 copy-start.8
  142.9 1.7 collective-permute-start.11
  145.4 3.5 %copy-start.13 = (bf16[4,64,128]{2,1,0:T(8,128)(2,1)}, bf16[4,64,128]{2,1,0:T(8,128)(2,1)S(1)}, u32[]{:S(2)}) copy-start(bf16[4,64,128]{2,1,0:T(8,128)(2,1)S(1)} %add_convert_fusion.refs_1_) | copy-start | bytes 196612
  145.4 3.5 %collective-permute-start.12 = (bf16[4,64,128]{2,1,0:T(8,128)(2,1)S(1)}, bf16[4,64,128]{2,1,0:T(8,128)(2,1)S(1)}, u32[]{:S(2)}, u32[]{:S(2)}) collective-permute-start(bf16[4,64,128]{2,1,0:T(8,128)(2,1)S(1)} %add_convert_fusion.refs_1_), channel_id=1, source_target_pairs={{0,2},{1,3},{2,0},{3,1},{4,6},{5,7},{6,4},{7,5},{8,10},{9,11},{10,... | collective-permute-start | bytes 196616 | tf_op jit(solution)/shard_map/ppermute | solution.py:391
  148.9 0.6 copy-start.15
  157.6 42.1 %collective-permute-start.16 = (bf16[2,64,2048]{2,1,0:T(8,128)(2,1)}, bf16[2,64,2048]{2,1,0:T(8,128)(2,1)S(1)}, u32[]{:S(2)}, u32[]{:S(2)}) collective-permute-start(bf16[2,64,2048]{2,1,0:T(8,128)(2,1)} %get-tuple-element.44), channel_id=1, source_target_pairs={{0,4},{4,8},{8,12},{12,0},{1,5},{5,9},{9,13},{13,1},{2,6},{6,10},{... | collective-permute-start | bytes 1572872 | tf_op jit(solution)/shard_map/ppermute | solution.py:394
  157.7 45.8 %collective-permute-start.17 = (bf16[2,64,2048]{2,1,0:T(8,128)(2,1)}, bf16[2,64,2048]{2,1,0:T(8,128)(2,1)S(1)}, u32[]{:S(2)}, u32[]{:S(2)}) collective-permute-start(bf16[2,64,2048]{2,1,0:T(8,128)(2,1)} %get-tuple-element.45), channel_id=1, source_target_pairs={{0,8},{4,12},{8,0},{12,4},{1,9},{5,13},{9,1},{13,5},{2,10},{6,14},... | collective-permute-start | bytes 1572872 | tf_op jit(solution)/shard_map/ppermute | solution.py:394
  162.7 1.4 copy-start.3
  162.7 46.3 %collective-permute-start.18 = (bf16[2,64,2048]{2,1,0:T(8,128)(2,1)}, bf16[2,64,2048]{2,1,0:T(8,128)(2,1)S(1)}, u32[]{:S(2)}, u32[]{:S(2)}) collective-permute-start(bf16[2,64,2048]{2,1,0:T(8,128)(2,1)} %get-tuple-element.43.refs_5_), channel_id=1, source_target_pairs={{0,12},{4,0},{8,4},{12,8},{1,13},{5,1},{9,5},{13,9},{2,14},{6,2},{... | collective-permute-start | bytes 1572872 | tf_op jit(solution)/shard_map/ppermute | solution.py:394
  164.1 0.8 copy-start.4
  164.9 0.8 copy-start.6
  199.7 9.2 %copy-start.9 = (bf16[2,64,2048]{2,1,0:T(8,128)(2,1)}, bf16[2,64,2048]{2,1,0:T(8,128)(2,1)S(1)}, u32[]{:S(2)}) copy-start(bf16[2,64,2048]{2,1,0:T(8,128)(2,1)S(1)} %collective-permute-done.16.refs_2_) | copy-start | bytes 1572868
  203.5 5.4 %copy-start.10 = (bf16[2,64,2048]{2,1,0:T(8,128)(2,1)}, bf16[2,64,2048]{2,1,0:T(8,128)(2,1)S(1)}, u32[]{:S(2)}) copy-start(bf16[2,64,2048]{2,1,0:T(8,128)(2,1)S(1)} %collective-permute-done.17.refs_3_) | copy-start | bytes 1572868
  208.9 0.8 copy-start.11
Sparse Core Ops, SparseCore 0:
  9.6 58.8 all-gather.1
  71.1 71.2 reduce-scatter.1

commit v3 on v2

--- a/solution.py
+++ b/solution.py
@@ -73,9 +73,10 @@
     ]
 
 
-def request_kernel(capacity, me_ref, rel_ref, table_ref, *rest):
-    outs, (plan_ref, held, sem) = rest[:-3], rest[-3:]
-    n_dev, n_seg = rel_ref.shape
+def request_kernel(capacity, n_dev, me_ref, row_ref, *rest):
+    id_refs, table_ref = rest[:n_dev], rest[n_dev]
+    outs, (plan_ref, held, sem) = rest[n_dev + 1 : -3], rest[-3:]
+    n_seg = id_refs[0].shape[0]
     n_own = table_ref.shape[0]
     me = me_ref[0]
     spare = COLS - 1
@@ -83,7 +84,7 @@
         for row in (SEND, TERM, GIVEN):
             plan_ref[row, c] = 0 if row == SEND else -1
     for s in range(1, n_dev):
-        slots = [rel_ref[s, k] for k in range(n_seg)]
+        slots = [row_ref[id_refs[s][k]] for k in range(n_seg)]
         order = jnp.int32(0)
         for slot in slots:
             mine = lax.div(slot, n_own) == me
@@ -94,7 +95,7 @@
             order = order + mine.astype(jnp.int32)
     rows = [plan_ref[SEND, c] for c in range(len(outs) * capacity)]
     finish_copies = copy_rows(rows, table_ref, outs, held, sem)
-    slots = [rel_ref[0, k] for k in range(n_seg)]
+    slots = [row_ref[id_refs[0][k]] for k in range(n_seg)]
     owners = [lax.div(v, n_own) for v in slots]
     for k in range(n_seg):
         local = slots[k] - owners[k] * n_own
@@ -109,13 +110,14 @@
     finish_copies()
 
 
-def request(me, relative, table, capacity):
-    count = relative.shape[0] - 1
+def request(me, table_row, ids, table, capacity):
+    n_dev = len(ids)
+    count = n_dev - 1
     block = jax.ShapeDtypeStruct((capacity,) + table.shape[1:], table.dtype)
     *sends, plan = call(
-        functools.partial(request_kernel, capacity),
-        (me.reshape(1), relative, table),
-        [SMEM, SMEM, ANYWHERE],
+        functools.partial(request_kernel, capacity, n_dev),
+        (me.reshape(1), table_row, *ids, table),
+        [SMEM] * (2 + n_dev) + [ANYWHERE],
         out_shape=[block] * count + [jax.ShapeDtypeStruct((8, COLS), jnp.int32)],
         out_specs=[HBM] * count + [SMEM],
         scratch=copies_of(table, count * capacity),
@@ -228,33 +230,30 @@
 def total_kernel(plan_ref, terms_ref, *rest):
     blocks, out_ref = rest[:-1], rest[-1]
     capacity = blocks[0].shape[0]
+    mine = pl.program_id(0)
     out_ref[...] = jnp.zeros_like(out_ref)
     sources = [(plan_ref[OWN, k], terms_ref, k) for k in range(terms_ref.shape[0])]
     for n, ref in enumerate(blocks):
         for j in range(capacity):
-            sources.append((plan_ref[GIVEN, n * capacity + j], ref, j))
+            sources.append((plan_ref[GIVEN, (n - 1) % len(blocks) * capacity + j], ref, j))
     for at, ref, k in sources:
 
-        @pl.when(at >= 0)
-        def _(at=at, ref=ref, k=k):
-            out_ref[at] += ref[k].astype(F32)
+        @pl.when(at == mine)
+        def _(ref=ref, k=k):
+            out_ref[0] += ref[k].astype(F32)
 
 
 def totals(plan, terms, blocks, n_own, after=()):
-    n_seg, rank, width = terms.shape
-    tile = min(512, width)
-
-    def here(n):
-        return pl.BlockSpec((n, rank, tile), lambda j: (0, 0, j))
-
+    blocks = rotated(blocks)
+    _, rank, width = terms.shape
     return call(
         total_kernel,
         (plan, terms, *blocks),
-        [SMEM, here(n_seg)] + [here(b.shape[0]) for b in blocks],
-        after,
-        grid=(width // tile,),
+        [SMEM] + [VMEM] * (1 + len(blocks)),
+        after,
+        grid=(n_own,),
         out_shape=jax.ShapeDtypeStruct((n_own, rank, width), F32),
-        out_specs=here(n_own),
+        out_specs=pl.BlockSpec((1, rank, width), lambda j: (j, 0, 0)),
         cost_estimate=cost(0, 4 * terms.size),
         name="totals",
     )
@@ -295,15 +294,20 @@
     )
 
 
-def held_back(x, after):
-    return call(
-        lambda x_ref, out_ref: None,
-        (x,),
-        [ANYWHERE],
-        after,
-        out_shape=jax.ShapeDtypeStruct(x.shape, x.dtype),
-        out_specs=ANYWHERE,
-        input_output_aliases={0: 0},
+def rotated(blocks):
+    return [blocks[-1], *blocks[:-1]]
+
+
+def held_back(arrays, after):
+    n = len(arrays)
+    return call(
+        lambda *refs: None,
+        arrays,
+        [ANYWHERE] * n,
+        after,
+        out_shape=[jax.ShapeDtypeStruct(x.shape, x.dtype) for x in arrays],
+        out_specs=[ANYWHERE] * n,
+        input_output_aliases={i: i for i in range(n)},
         cost_estimate=cost(0, 0),
         name="held_back",
     )
@@ -398,37 +402,35 @@
 
     cot_rows = lax.all_gather(cotangent, "tensor", axis=1, tiled=True)
 
-    one = segment_adapter_id[:, None] == jnp.arange(adapter_table_row.shape[0])[None, :]
-    slots = jnp.sum(jnp.where(one, adapter_table_row[None, :], 0), axis=1).astype(jnp.int32)
-    relative = jnp.stack([slots] + [over_line(slots, s) for s in shifts])
+    ids = [segment_adapter_id] + [over_line(segment_adapter_id, s) for s in shifts]
 
     down_t = jnp.swapaxes(down_table, 1, 2)
     me_dev = lax.axis_index("dp").astype(jnp.int32)
-    sends, plan = request(me_dev, relative, down_t, capacity)
+    sends, plan = request(me_dev, adapter_table_row, ids, down_t, capacity)
     down_got = [over_line(x, s) for x, s in zip(sends, shifts)]
 
     sends = rows_of(plan, SEND, up_table, n_dev - 1, capacity, [sends[-1]])
     up_got = [over_line(x, s) for x, s in zip(sends, shifts)]
 
-    partial = held_back(forward(tokens, weight, [sends[-1]]), down_got)
+    (partial,) = held_back([forward(tokens, weight, [sends[-1]])], rotated(down_got))
     layer = lax.psum_scatter(partial, "tensor", scatter_dimension=1, tiled=True)
 
     def summed(part):
         part = (part.astype(F32) + over_core(part).astype(F32)).astype(BF16)
         return [part] + [over_chips(part, s) for s in hops]
 
-    def give(terms):
-        sends = rows_of(plan, TERM, terms, n_dev - 1, capacity)
+    def give(terms, after):
+        sends = held_back(rows_of(plan, TERM, terms, n_dev - 1, capacity), rotated(after))
         return sends, [over_line(x, s) for x, s in zip(sends, shifts)]
 
     down_seg, part = low_rank(plan, tokens, down_t, down_got, n_seg, [partial])
     act, up_terms = make_terms(segment_live_length, summed(part), cotangent)
 
-    sends, up_back = give(up_terms)
+    sends, up_back = give(up_terms, up_got)
     up_seg, part = low_rank(plan, cotangent, up_table, up_got, n_seg, [sends[-1]])
     grad, down_terms = make_terms(segment_live_length, summed(part), tokens)
 
-    sends, down_back = give(down_terms)
+    sends, down_back = give(down_terms, up_back)
     up_grad = totals(plan, up_terms, up_back, n_own, [sends[-1]])
     token_input_gradient = backward(cot_rows, weight, grad, down_seg, [up_grad])
     layer_result = adapt(layer, act, up_seg, [token_input_gradient])

time: 222 us -> 222 us (level)
  the two profiles are of different devices: /device:TPU:13 before, /device:TPU:0 now
where the time goes in v3:
time: 222 us; the launch traced here: 220 us
  Pallas kernels  98.7 us (44%)
  waiting for transfers between devices  66.7 us (30%)
  starting transfers between devices  32.4 us (15%)
  between operations  14.2 us (6%)
  local copies, waits for them, and re-layouts  6.17 us (3%)
    pallas_call x16, Pallas kernels, call(): pl.pallas_call(body, grid_spec=pltpu.PrefetchScalarGridSpec(num_scalar_pr...  98.7 us
    ppermute x15, waiting for transfers between devices, over_line(): return lax.ppermute(x, 'dp', [(i, (i + s) % n_dev) for i in range(n_dev)])  55.8 us
    ppermute x15, starting transfers between devices, over_line(): return lax.ppermute(x, 'dp', [(i, (i + s) % n_dev) for i in range(n_dev)])  29 us
    ppermute x2, waiting for transfers between devices, over_chips(): return lax.ppermute(x, 'tensor', pairs)  7.24 us
    unnamed x46, local copies, waits for them, and re-layouts  6.17 us
  transfers between devices with their start and end apart: 21, of which 11 were waited for; matrix products, arithmetic and copies ran while one was open for 1% of the time, Pallas kernels for 43%

profile of v3, /device:TPU:0, one launch (start us, length us, event | category | flops | bytes accessed | tf_op | source)
XLA Modules:
  0.0 220.0 jit_solution(5195105472263748899)
XLA Ops:
  7.2 0.0 all-gather.2.cloned.1.call-start
  7.2 0.7 all-gather.2.cloned.1.call-update
  7.9 0.0 reduce-scatter.2.cloned.1.call-start
  8.0 3.1 %collective-permute-start = (s32[4]{0:T(128)S(1)}, s32[4]{0:T(128)S(1)}, u32[]{:S(2)}, u32[]{:S(2)}) collective-permute-start(s32[4]{0:T(128)S(1)} %copy-done.16), channel_id=1, source_target_pairs={{0,4},{4,8},{8,12},{12,0},{1,5},{5,9},{9,13},{13,1},{2,6},{6,10},{... | collective-permute-start | bytes 56 | tf_op jit(solution)/shard_map/ppermute | solution.py:398
  11.0 2.6 %collective-permute-start.1 = (s32[4]{0:T(128)S(1)}, s32[4]{0:T(128)S(1)}, u32[]{:S(2)}, u32[]{:S(2)}) collective-permute-start(s32[4]{0:T(128)S(1)} %copy-done.16), channel_id=1, source_target_pairs={{0,8},{4,12},{8,0},{12,4},{1,9},{5,13},{9,1},{13,5},{2,10},{6,14},... | collective-permute-start | bytes 56 | tf_op jit(solution)/shard_map/ppermute | solution.py:398
  13.6 1.3 collective-permute-start.2
  15.0 0.0 collective-permute-done.refs_3_
  15.0 0.5 collective-permute-done.1.refs_4_
  15.5 1.7 collective-permute-done.2.refs_5_
  17.2 0.5 copy-done.19
  17.7 4.1 %request.1 = (bf16[2,64,2048]{2,1,0:T(8,128)(2,1)}, bf16[2,64,2048]{2,1,0:T(8,128)(2,1)}, bf16[2,64,2048]{2,1,0:T(8,128)(2,1)}, s32[8,128]{1,0:T(8,128)}) custom-call(s32[1]{0:T(128)} %bitcast.refs_0_, s32[16]{0:T(128)} %refs_1_.6, s32[4]{0:T(128)} %refs_2_.2, s32[4]{0:T(128)} %copy-done.17, s32[4]{0:T(128)} %copy-done.18, s32[4]{0:T(128)} %copy-done.19, ...), custom_call_target="tpu_custom_call" | custom-call | bytes 2097152 | tf_op jit(solution)/shard_map/request/pallas_call | solution.py:32
  21.8 3.0 %collective-permute-start.3 = (bf16[2,64,2048]{2,1,0:T(8,128)(2,1)}, bf16[2,64,2048]{2,1,0:T(8,128)(2,1)S(1)}, u32[]{:S(2)}, u32[]{:S(2)}) collective-permute-start(bf16[2,64,2048]{2,1,0:T(8,128)(2,1)} %get-tuple-element.32.refs_2_), channel_id=1, source_target_pairs={{0,12},{4,0},{8,4},{12,8},{1,13},{5,1},{9,5},{13,9},{2,14},{6,2},{... | collective-permute-start | bytes 1572872 | tf_op jit(solution)/shard_map/ppermute | solution.py:398
  24.8 0.0 collective-permute-start.4
  24.8 0.6 collective-permute-start.5
  25.4 3.8 %rows.3 = (bf16[2,64,2048]{2,1,0:T(8,128)(2,1)}, bf16[2,64,2048]{2,1,0:T(8,128)(2,1)}, bf16[2,64,2048]{2,1,0:T(8,128)(2,1)}) custom-call(s32[8,128]{1,0:T(8,128)} %get-tuple-element.31.refs_0_, bf16[4,64,2048]{2,1,0:T(8,128)(2,1)} %refs_2_.3, bf16[2,64,2048]{2,1,0:T(8,128)(2,1)} %get-tuple-element.32.refs_2_), custom_call_target="tpu_custom_call" | custom-call | bytes 2097152 | tf_op jit(solution)/shard_map/rows/pallas_call | solution.py:32
  29.3 27.6 %forward.1.refs_0_ = bf16[512,8192]{1,0:T(8,128)(2,1)} custom-call(bf16[512,2048]{1,0:T(8,128)(2,1)} %refs_3_.3, bf16[2048,8192]{1,0:T(8,128)(2,1)} %refs_1_.11, bf16[2,64,2048]{2,1,0:T(8,128)(2,1)} %get-tuple-element.33.refs_2_), custom_call_target="tpu_custom_call" | custom-call | flops 17179869184 | bytes 33554432 | tf_op jit(solution)/shard_map/forward/pallas_call | solution.py:32
  56.9 10.4 %collective-permute-done.5.refs_3_.refs_4_ = bf16[2,64,2048]{2,1,0:T(8,128)(2,1)S(1)} collective-permute-done((bf16[2,64,2048]{2,1,0:T(8,128)(2,1)}, bf16[2,64,2048]{2,1,0:T(8,128)(2,1)S(1)}, u32[]{:S(2)}, u32[]{:S(2)}) %collective-permute-start.5) | collective-permute-done | bytes 524320 | tf_op jit(solution)/shard_map/ppermute | solution.py:398
  67.3 0.8 copy-done.2
  68.1 0.0 reduce-scatter.2.cloned.1.call-update
  68.2 1.0 copy-done.22
  69.2 0.2 collective-permute-start.8
  69.3 3.3 %collective-permute-start.9 = (bf16[2,64,2048]{2,1,0:T(8,128)(2,1)S(1)}, bf16[2,64,2048]{2,1,0:T(8,128)(2,1)S(1)}, u32[]{:S(2)}, u32[]{:S(2)}) collective-permute-start(bf16[2,64,2048]{2,1,0:T(8,128)(2,1)S(1)} %copy-done.21), channel_id=1, source_target_pairs={{0,8},{4,12},{8,0},{12,4},{1,9},{5,13},{9,1},{13,5},{2,10},{6,14},... | collective-permute-start | bytes 1572872 | tf_op jit(solution)/shard_map/ppermute | solution.py:398
  72.6 0.5 collective-permute-start.10
  73.1 4.8 %low_rank.2 = (bf16[4,64,2048]{2,1,0:T(8,128)(2,1)}, bf16[4,64,128]{2,1,0:T(8,128)(2,1)}) custom-call(s32[8,128]{1,0:T(8,128)} %get-tuple-element.31.refs_0_, bf16[512,2048]{1,0:T(8,128)(2,1)} %refs_3_.3, bf16[4,64,2048]{2,1,0:T(8,128)(2,1)} %bitcast.4, bf16[2,64,2048]{2,1,0:T(8,128)(2,1)} %copy-done.1, bf16[2,64,2048]{2,1,0:T(8,128)(2,1)} %copy-done.2, ...), custom_call_target="tpu_custom_call" | custom-call | flops 134217728 | bytes 4194304 | tf_op jit(solution)/shard_map/low_rank/pallas_call | solution.py:32
  77.9 0.1 collective-permute-start.6
  78.0 1.5 collective-permute-done.6
  79.5 0.9 add_convert_fusion.1.refs_1_
  80.4 0.0 copy-start.12
  80.4 1.6 collective-permute-start.7
  82.0 2.7 %collective-permute-done.7.refs_2_ = bf16[4,64,128]{2,1,0:T(8,128)(2,1)S(1)} collective-permute-done((bf16[4,64,128]{2,1,0:T(8,128)(2,1)S(1)}, bf16[4,64,128]{2,1,0:T(8,128)(2,1)S(1)}, u32[]{:S(2)}, u32[]{:S(2)}) %collective-permute-start.7) | collective-permute-done | bytes 65568 | tf_op jit(solution)/shard_map/ppermute | solution.py:395
  84.7 0.6 copy-done.14
  85.4 4.9 %terms.2 = (bf16[4,64,128]{2,1,0:T(8,128)(2,1)}, bf16[4,64,2048]{2,1,0:T(8,128)(2,1)}) custom-call(s32[4]{0:T(128)} %refs_0_.5, bf16[4,64,128]{2,1,0:T(8,128)(2,1)} %copy-done.12, bf16[4,64,128]{2,1,0:T(8,128)(2,1)} %copy-done.14, bf16[512,2048]{1,0:T(8,128)(2,1)} %refs_1_.10), custom_call_target="tpu_custom_call" | custom-call | flops 134217728 | bytes 4194304 | tf_op jit(solution)/shard_map/terms/pallas_call | solution.py:32
  90.3 3.4 %rows.4 = (bf16[2,64,2048]{2,1,0:T(8,128)(2,1)}, bf16[2,64,2048]{2,1,0:T(8,128)(2,1)}, bf16[2,64,2048]{2,1,0:T(8,128)(2,1)}) custom-call(s32[8,128]{1,0:T(8,128)} %get-tuple-element.31.refs_0_, bf16[4,64,2048]{2,1,0:T(8,128)(2,1)} %get-tuple-element.40.refs_1_), custom_call_target="tpu_custom_call" | custom-call | bytes 2097152 | tf_op jit(solution)/shard_map/rows/pallas_call | solution.py:32
  93.7 0.0 copy-start.3
  93.7 11.3 %collective-permute-done.9.refs_5_.refs_4_ = bf16[2,64,2048]{2,1,0:T(8,128)(2,1)S(1)} collective-permute-done((bf16[2,64,2048]{2,1,0:T(8,128)(2,1)S(1)}, bf16[2,64,2048]{2,1,0:T(8,128)(2,1)S(1)}, u32[]{:S(2)}, u32[]{:S(2)}) %collective-permute-start.9) | collective-permute-done | bytes 524320 | tf_op jit(solution)/shard_map/ppermute | solution.py:398
  105.0 0.0 collective-permute-done.10.refs_3_.refs_5_
  105.0 0.8 copy-done.5
  105.8 0.2 copy-done.7
  105.9 10.1 %collective-permute-start.13 = (bf16[2,64,2048]{2,1,0:T(8,128)(2,1)}, bf16[2,64,2048]{2,1,0:T(8,128)(2,1)S(1)}, u32[]{:S(2)}, u32[]{:S(2)}) collective-permute-start(bf16[2,64,2048]{2,1,0:T(8,128)(2,1)} %get-tuple-element.44.refs_6_), channel_id=1, source_target_pairs={{0,12},{4,0},{8,4},{12,8},{1,13},{5,1},{9,5},{13,9},{2,14},{6,2},{... | collective-permute-start | bytes 1572872 | tf_op jit(solution)/shard_map/ppermute | solution.py:398
  116.0 0.9 collective-permute-start.14
  116.9 1.5 collective-permute-start.15
  118.4 4.8 %low_rank.3 = (bf16[4,64,2048]{2,1,0:T(8,128)(2,1)}, bf16[4,64,128]{2,1,0:T(8,128)(2,1)}) custom-call(s32[8,128]{1,0:T(8,128)} %get-tuple-element.31.refs_0_, bf16[512,2048]{1,0:T(8,128)(2,1)} %refs_1_.10, bf16[4,64,2048]{2,1,0:T(8,128)(2,1)} %refs_2_.3, bf16[2,64,2048]{2,1,0:T(8,128)(2,1)} %copy-done.3, bf16[2,64,2048]{2,1,0:T(8,128)(2,1)} %copy-done.5, ...), custom_call_target="tpu_custom_call" | custom-call | flops 134217728 | bytes 4194304 | tf_op jit(solution)/shard_map/low_rank/pallas_call | solution.py:32
  123.2 0.1 collective-permute-start.11
  123.3 1.5 collective-permute-done.11
  124.7 0.9 add_convert_fusion.refs_1_
  125.6 0.0 copy-start.13
  125.6 1.6 collective-permute-start.12
  127.2 4.5 %collective-permute-done.12.refs_2_ = bf16[4,64,128]{2,1,0:T(8,128)(2,1)S(1)} collective-permute-done((bf16[4,64,128]{2,1,0:T(8,128)(2,1)S(1)}, bf16[4,64,128]{2,1,0:T(8,128)(2,1)S(1)}, u32[]{:S(2)}, u32[]{:S(2)}) %collective-permute-start.12) | collective-permute-done | bytes 65568 | tf_op jit(solution)/shard_map/ppermute | solution.py:395
  131.7 0.6 copy-done.15
  132.4 4.7 %terms.3 = (bf16[4,64,128]{2,1,0:T(8,128)(2,1)}, bf16[4,64,2048]{2,1,0:T(8,128)(2,1)}) custom-call(s32[4]{0:T(128)} %refs_0_.5, bf16[4,64,128]{2,1,0:T(8,128)(2,1)} %copy-done.13, bf16[4,64,128]{2,1,0:T(8,128)(2,1)} %copy-done.15, bf16[512,2048]{1,0:T(8,128)(2,1)} %refs_3_.3), custom_call_target="tpu_custom_call" | custom-call | flops 134217728 | bytes 4194304 | tf_op jit(solution)/shard_map/terms/pallas_call | solution.py:32
  137.1 3.3 %rows.5 = (bf16[2,64,2048]{2,1,0:T(8,128)(2,1)}, bf16[2,64,2048]{2,1,0:T(8,128)(2,1)}, bf16[2,64,2048]{2,1,0:T(8,128)(2,1)}) custom-call(s32[8,128]{1,0:T(8,128)} %get-tuple-element.31.refs_0_, bf16[4,64,2048]{2,1,0:T(8,128)(2,1)} %get-tuple-element.51.refs_1_), custom_call_target="tpu_custom_call" | custom-call | bytes 2097152 | tf_op jit(solution)/shard_map/rows/pallas_call | solution.py:32
  140.4 0.0 collective-permute-done.13.refs_3_.refs_2_
  140.4 0.0 copy-start.4
  140.4 1.3 collective-permute-done.14.refs_4_.refs_3_
  141.7 21.9 %collective-permute-done.15.refs_5_.refs_4_ = bf16[2,64,2048]{2,1,0:T(8,128)(2,1)S(1)} collective-permute-done((bf16[2,64,2048]{2,1,0:T(8,128)(2,1)}, bf16[2,64,2048]{2,1,0:T(8,128)(2,1)S(1)}, u32[]{:S(2)}, u32[]{:S(2)}) %collective-permute-start.15) | collective-permute-done | bytes 524320 | tf_op jit(solution)/shard_map/ppermute | solution.py:398
  163.7 0.8 copy-done.8
  164.4 0.0 collective-permute-start.16
  164.4 2.0 collective-permute-start.17
  166.5 3.6 %totals.2.refs_4_ = f32[4,64,2048]{2,1,0:T(8,128)} custom-call(s32[8,128]{1,0:T(8,128)} %get-tuple-element.31.refs_0_, bf16[4,64,2048]{2,1,0:T(8,128)(2,1)} %get-tuple-element.40.refs_1_, bf16[2,64,2048]{2,1,0:T(8,128)(2,1)} %copy-done.4, bf16[2,64,2048]{2,1,0:T(8,128)(2,1)} %copy-done.6, bf16[2,64,2048]{2,1,0:T(8,128)(2,1)} %copy-done.8, ...), custom_call_target="tpu_custom_call" | custom-call | bytes 2097152 | tf_op jit(solution)/shard_map/totals/pallas_call | solution.py:32
  170.1 25.5 %backward.1.refs_3_ = bf16[512,2048]{1,0:T(8,128)(2,1)} custom-call(bf16[512,8192]{1,0:T(8,128)(2,1)} %all-gather.2.cloned.1.call-done.refs_0_, bf16[2048,8192]{1,0:T(8,128)(2,1)} %refs_1_.11, bf16[4,64,128]{2,1,0:T(8,128)(2,1)} %get-tuple-element.47.refs_2_, bf16[4,64,2048]{2,1,0:T(8,128)(2,1)} %get-tuple-element.48.refs_3_, f32[4,64,2048]{2,1,0:T(8,128)} %totals.2.refs_4_), custom_call_target="tpu_custom_call" | custom-call | flops 17179869184 | bytes 33554432 | tf_op jit(solution)/shard_map/backward/pallas_call | solution.py:32
  195.5 4.5 %adapt.1.refs_5_ = bf16[512,2048]{1,0:T(8,128)(2,1)} custom-call(bf16[512,2048]{1,0:T(8,128)(2,1)} %reduce-scatter.2.cloned.1.call-done.refs_0_, bf16[4,64,128]{2,1,0:T(8,128)(2,1)} %get-tuple-element.37.refs_1_, bf16[4,64,2048]{2,1,0:T(8,128)(2,1)} %get-tuple-element.45.refs_2_, bf16[512,2048]{1,0:T(8,128)(2,1)} %backward.1.refs_3_), custom_call_target="tpu_custom_call" | custom-call | flops 134217728 | bytes 4194304 | tf_op jit(solution)/shard_map/adapt/pallas_call | solution.py:32
  200.1 8.6 %collective-permute-done.18.refs_4_ = bf16[2,64,2048]{2,1,0:T(8,128)(2,1)S(1)} collective-permute-done((bf16[2,64,2048]{2,1,0:T(8,128)(2,1)}, bf16[2,64,2048]{2,1,0:T(8,128)(2,1)S(1)}, u32[]{:S(2)}, u32[]{:S(2)}) %collective-permute-start.18) | collective-permute-done | bytes 524320 | tf_op jit(solution)/shard_map/ppermute | solution.py:398
  208.8 0.8 copy-done.11
  209.5 3.6 %totals.3 = f32[4,64,2048]{2,1,0:T(8,128)} custom-call(s32[8,128]{1,0:T(8,128)} %get-tuple-element.31.refs_0_, bf16[4,64,2048]{2,1,0:T(8,128)(2,1)} %get-tuple-element.51.refs_1_, bf16[2,64,2048]{2,1,0:T(8,128)(2,1)} %copy-done.9, bf16[2,64,2048]{2,1,0:T(8,128)(2,1)} %copy-done.10, bf16[2,64,2048]{2,1,0:T(8,128)(2,1)} %copy-done.11, ...), custom_call_target="tpu_custom_call" | custom-call | bytes 2097152 | tf_op jit(solution)/shard_map/totals/pallas_call | solution.py:32
  (44 shorter events, 0.1 us)
Async XLA Ops:
  7.2 0.8 copy-start.16
  7.2 162.9 %all-gather.2.cloned.1.call-start = ((), (), s32[]{:S(2)}) async-start(), calls=%async_computation.2 | async-start | bytes 10485760 | tf_op jit(solution)/shard_map/all_gather | solution.py:403
  7.9 187.6 %reduce-scatter.2.cloned.1.call-start = ((), (), s32[]{:S(2)}) async-start(), calls=%async_computation.1 | async-start | bytes 10485760 | tf_op jit(solution)/shard_map/reduce_scatter | solution.py:416
  8.0 7.0 %collective-permute-start = (s32[4]{0:T(128)S(1)}, s32[4]{0:T(128)S(1)}, u32[]{:S(2)}, u32[]{:S(2)}) collective-permute-start(s32[4]{0:T(128)S(1)} %copy-done.16), channel_id=1, source_target_pairs={{0,4},{4,8},{8,12},{12,0},{1,5},{5,9},{9,13},{13,1},{2,6},{6,10},{... | collective-permute-start | bytes 56 | tf_op jit(solution)/shard_map/ppermute | solution.py:398
  11.0 4.4 %collective-permute-start.1 = (s32[4]{0:T(128)S(1)}, s32[4]{0:T(128)S(1)}, u32[]{:S(2)}, u32[]{:S(2)}) collective-permute-start(s32[4]{0:T(128)S(1)} %copy-done.16), channel_id=1, source_target_pairs={{0,8},{4,12},{8,0},{12,4},{1,9},{5,13},{9,1},{13,5},{2,10},{6,14},... | collective-permute-start | bytes 56 | tf_op jit(solution)/shard_map/ppermute | solution.py:398
  13.6 3.5 %collective-permute-start.2 = (s32[4]{0:T(128)S(1)}, s32[4]{0:T(128)S(1)}, u32[]{:S(2)}, u32[]{:S(2)}) collective-permute-start(s32[4]{0:T(128)S(1)} %copy-done.16), channel_id=1, source_target_pairs={{0,12},{4,0},{8,4},{12,8},{1,13},{5,1},{9,5},{13,9},{2,14},{6,2},{... | collective-permute-start | bytes 56 | tf_op jit(solution)/shard_map/ppermute | solution.py:398
  15.0 2.2 copy-start.17
  15.5 1.7 copy-start.18
  17.2 0.5 copy-start.19
  21.8 35.1 %collective-permute-start.3 = (bf16[2,64,2048]{2,1,0:T(8,128)(2,1)}, bf16[2,64,2048]{2,1,0:T(8,128)(2,1)S(1)}, u32[]{:S(2)}, u32[]{:S(2)}) collective-permute-start(bf16[2,64,2048]{2,1,0:T(8,128)(2,1)} %get-tuple-element.32.refs_2_), channel_id=1, source_target_pairs={{0,12},{4,0},{8,4},{12,8},{1,13},{5,1},{9,5},{13,9},{2,14},{6,2},{... | collective-permute-start | bytes 1572872 | tf_op jit(solution)/shard_map/ppermute | solution.py:398
  24.8 32.1 %collective-permute-start.4 = (bf16[2,64,2048]{2,1,0:T(8,128)(2,1)}, bf16[2,64,2048]{2,1,0:T(8,128)(2,1)S(1)}, u32[]{:S(2)}, u32[]{:S(2)}) collective-permute-start(bf16[2,64,2048]{2,1,0:T(8,128)(2,1)} %get-tuple-element.34), channel_id=1, source_target_pairs={{0,4},{4,8},{8,12},{12,0},{1,5},{5,9},{9,13},{13,1},{2,6},{6,10},{... | collective-permute-start | bytes 1572872 | tf_op jit(solution)/shard_map/ppermute | solution.py:398
  24.8 42.5 %collective-permute-start.5 = (bf16[2,64,2048]{2,1,0:T(8,128)(2,1)}, bf16[2,64,2048]{2,1,0:T(8,128)(2,1)S(1)}, u32[]{:S(2)}, u32[]{:S(2)}) collective-permute-start(bf16[2,64,2048]{2,1,0:T(8,128)(2,1)} %get-tuple-element.35), channel_id=1, source_target_pairs={{0,8},{4,12},{8,0},{12,4},{1,9},{5,13},{9,1},{13,5},{2,10},{6,14},... | collective-permute-start | bytes 1572872 | tf_op jit(solution)/shard_map/ppermute | solution.py:398
  56.9 10.4 %copy-start = (bf16[2,64,2048]{2,1,0:T(8,128)(2,1)}, bf16[2,64,2048]{2,1,0:T(8,128)(2,1)S(1)}, u32[]{:S(2)}) copy-start(bf16[2,64,2048]{2,1,0:T(8,128)(2,1)S(1)} %collective-permute-done.3.refs_1_.refs_5_) | copy-start | bytes 1572868
  56.9 10.4 %copy-start.1 = (bf16[2,64,2048]{2,1,0:T(8,128)(2,1)}, bf16[2,64,2048]{2,1,0:T(8,128)(2,1)S(1)}, u32[]{:S(2)}) copy-start(bf16[2,64,2048]{2,1,0:T(8,128)(2,1)S(1)} %collective-permute-done.4.refs_2_.refs_3_) | copy-start | bytes 1572868
  67.3 0.8 copy-start.2
  68.1 1.0 copy-start.22
  68.1 1.2 copy-start.21
  68.1 4.5 %copy-start.20 = (bf16[2,64,2048]{2,1,0:T(8,128)(2,1)S(1)}, bf16[2,64,2048]{2,1,0:T(8,128)(2,1)}, u32[]{:S(2)}) copy-start(bf16[2,64,2048]{2,1,0:T(8,128)(2,1)} %get-tuple-element.33.refs_2_) | copy-start | bytes 1572868
  69.2 24.5 %collective-permute-start.8 = (bf16[2,64,2048]{2,1,0:T(8,128)(2,1)S(1)}, bf16[2,64,2048]{2,1,0:T(8,128)(2,1)S(1)}, u32[]{:S(2)}, u32[]{:S(2)}) collective-permute-start(bf16[2,64,2048]{2,1,0:T(8,128)(2,1)S(1)} %copy-done.22), channel_id=1, source_target_pairs={{0,4},{4,8},{8,12},{12,0},{1,5},{5,9},{9,13},{13,1},{2,6},{6,10},{... | collective-permute-start | bytes 1572872 | tf_op jit(solution)/shard_map/ppermute | solution.py:398
  69.3 35.6 %collective-permute-start.9 = (bf16[2,64,2048]{2,1,0:T(8,128)(2,1)S(1)}, bf16[2,64,2048]{2,1,0:T(8,128)(2,1)S(1)}, u32[]{:S(2)}, u32[]{:S(2)}) collective-permute-start(bf16[2,64,2048]{2,1,0:T(8,128)(2,1)S(1)} %copy-done.21), channel_id=1, source_target_pairs={{0,8},{4,12},{8,0},{12,4},{1,9},{5,13},{9,1},{13,5},{2,10},{6,14},... | collective-permute-start | bytes 1572872 | tf_op jit(solution)/shard_map/ppermute | solution.py:398
  72.6 32.4 %collective-permute-start.10 = (bf16[2,64,2048]{2,1,0:T(8,128)(2,1)S(1)}, bf16[2,64,2048]{2,1,0:T(8,128)(2,1)S(1)}, u32[]{:S(2)}, u32[]{:S(2)}) collective-permute-start(bf16[2,64,2048]{2,1,0:T(8,128)(2,1)S(1)} %copy-done.20), channel_id=1, source_target_pairs={{0,12},{4,0},{8,4},{12,8},{1,13},{5,1},{9,5},{13,9},{2,14},{6,2},{... | collective-permute-start | bytes 1572872 | tf_op jit(solution)/shard_map/ppermute | solution.py:398
  77.9 1.6 collective-permute-start.6
  80.4 4.3 %copy-start.12 = (bf16[4,64,128]{2,1,0:T(8,128)(2,1)}, bf16[4,64,128]{2,1,0:T(8,128)(2,1)S(1)}, u32[]{:S(2)}) copy-start(bf16[4,64,128]{2,1,0:T(8,128)(2,1)S(1)} %add_convert_fusion.1.refs_1_) | copy-start | bytes 196612
  80.4 4.3 %collective-permute-start.7 = (bf16[4,64,128]{2,1,0:T(8,128)(2,1)S(1)}, bf16[4,64,128]{2,1,0:T(8,128)(2,1)S(1)}, u32[]{:S(2)}, u32[]{:S(2)}) collective-permute-start(bf16[4,64,128]{2,1,0:T(8,128)(2,1)S(1)} %add_convert_fusion.1.refs_1_), channel_id=1, source_target_pairs={{0,2},{1,3},{2,0},{3,1},{4,6},{5,7},{6,4},{7,5},{8,10},{9,11},{10,... | collective-permute-start | bytes 196616 | tf_op jit(solution)/shard_map/ppermute | solution.py:395
  84.7 0.6 copy-start.14
  93.7 11.3 %copy-start.3 = (bf16[2,64,2048]{2,1,0:T(8,128)(2,1)}, bf16[2,64,2048]{2,1,0:T(8,128)(2,1)S(1)}, u32[]{:S(2)}) copy-start(bf16[2,64,2048]{2,1,0:T(8,128)(2,1)S(1)} %collective-permute-done.8.refs_4_.refs_3_) | copy-start | bytes 1572868
  105.0 0.8 copy-start.5
  105.0 1.0 copy-start.7
  105.9 34.4 %collective-permute-start.13 = (bf16[2,64,2048]{2,1,0:T(8,128)(2,1)}, bf16[2,64,2048]{2,1,0:T(8,128)(2,1)S(1)}, u32[]{:S(2)}, u32[]{:S(2)}) collective-permute-start(bf16[2,64,2048]{2,1,0:T(8,128)(2,1)} %get-tuple-element.44.refs_6_), channel_id=1, source_target_pairs={{0,12},{4,0},{8,4},{12,8},{1,13},{5,1},{9,5},{13,9},{2,14},{6,2},{... | collective-permute-start | bytes 1572872 | tf_op jit(solution)/shard_map/ppermute | solution.py:398
  116.0 25.7 %collective-permute-start.14 = (bf16[2,64,2048]{2,1,0:T(8,128)(2,1)}, bf16[2,64,2048]{2,1,0:T(8,128)(2,1)S(1)}, u32[]{:S(2)}, u32[]{:S(2)}) collective-permute-start(bf16[2,64,2048]{2,1,0:T(8,128)(2,1)} %get-tuple-element.49), channel_id=1, source_target_pairs={{0,4},{4,8},{8,12},{12,0},{1,5},{5,9},{9,13},{13,1},{2,6},{6,10},{... | collective-permute-start | bytes 1572872 | tf_op jit(solution)/shard_map/ppermute | solution.py:398
  116.9 46.7 %collective-permute-start.15 = (bf16[2,64,2048]{2,1,0:T(8,128)(2,1)}, bf16[2,64,2048]{2,1,0:T(8,128)(2,1)S(1)}, u32[]{:S(2)}, u32[]{:S(2)}) collective-permute-start(bf16[2,64,2048]{2,1,0:T(8,128)(2,1)} %get-tuple-element.50), channel_id=1, source_target_pairs={{0,8},{4,12},{8,0},{12,4},{1,9},{5,13},{9,1},{13,5},{2,10},{6,14},... | collective-permute-start | bytes 1572872 | tf_op jit(solution)/shard_map/ppermute | solution.py:398
  123.2 1.5 collective-permute-start.11
  125.6 6.1 %copy-start.13 = (bf16[4,64,128]{2,1,0:T(8,128)(2,1)}, bf16[4,64,128]{2,1,0:T(8,128)(2,1)S(1)}, u32[]{:S(2)}) copy-start(bf16[4,64,128]{2,1,0:T(8,128)(2,1)S(1)} %add_convert_fusion.refs_1_) | copy-start | bytes 196612
  125.6 6.1 %collective-permute-start.12 = (bf16[4,64,128]{2,1,0:T(8,128)(2,1)S(1)}, bf16[4,64,128]{2,1,0:T(8,128)(2,1)S(1)}, u32[]{:S(2)}, u32[]{:S(2)}) collective-permute-start(bf16[4,64,128]{2,1,0:T(8,128)(2,1)S(1)} %add_convert_fusion.refs_1_), channel_id=1, source_target_pairs={{0,2},{1,3},{2,0},{3,1},{4,6},{5,7},{6,4},{7,5},{8,10},{9,11},{10,... | collective-permute-start | bytes 196616 | tf_op jit(solution)/shard_map/ppermute | solution.py:395
  131.7 0.6 copy-start.15
  140.4 23.3 %copy-start.4 = (bf16[2,64,2048]{2,1,0:T(8,128)(2,1)}, bf16[2,64,2048]{2,1,0:T(8,128)(2,1)S(1)}, u32[]{:S(2)}) copy-start(bf16[2,64,2048]{2,1,0:T(8,128)(2,1)S(1)} %collective-permute-done.13.refs_3_.refs_2_) | copy-start | bytes 1572868
  141.7 21.9 %copy-start.6 = (bf16[2,64,2048]{2,1,0:T(8,128)(2,1)}, bf16[2,64,2048]{2,1,0:T(8,128)(2,1)S(1)}, u32[]{:S(2)}) copy-start(bf16[2,64,2048]{2,1,0:T(8,128)(2,1)S(1)} %collective-permute-done.14.refs_4_.refs_3_) | copy-start | bytes 1572868
  163.6 0.8 copy-start.8
  164.4 35.6 %collective-permute-start.16 = (bf16[2,64,2048]{2,1,0:T(8,128)(2,1)}, bf16[2,64,2048]{2,1,0:T(8,128)(2,1)S(1)}, u32[]{:S(2)}, u32[]{:S(2)}) collective-permute-start(bf16[2,64,2048]{2,1,0:T(8,128)(2,1)} %get-tuple-element.55.refs_5_), channel_id=1, source_target_pairs={{0,12},{4,0},{8,4},{12,8},{1,13},{5,1},{9,5},{13,9},{2,14},{6,2},{... | collective-permute-start | bytes 1572872 | tf_op jit(solution)/shard_map/ppermute | solution.py:398
  164.4 35.6 %collective-permute-start.17 = (bf16[2,64,2048]{2,1,0:T(8,128)(2,1)}, bf16[2,64,2048]{2,1,0:T(8,128)(2,1)S(1)}, u32[]{:S(2)}, u32[]{:S(2)}) collective-permute-start(bf16[2,64,2048]{2,1,0:T(8,128)(2,1)} %get-tuple-element.56), channel_id=1, source_target_pairs={{0,4},{4,8},{8,12},{12,0},{1,5},{5,9},{9,13},{13,1},{2,6},{6,10},{... | collective-permute-start | bytes 1572872 | tf_op jit(solution)/shard_map/ppermute | solution.py:398
  166.5 42.3 %collective-permute-start.18 = (bf16[2,64,2048]{2,1,0:T(8,128)(2,1)}, bf16[2,64,2048]{2,1,0:T(8,128)(2,1)S(1)}, u32[]{:S(2)}, u32[]{:S(2)}) collective-permute-start(bf16[2,64,2048]{2,1,0:T(8,128)(2,1)} %get-tuple-element.57), channel_id=1, source_target_pairs={{0,8},{4,12},{8,0},{12,4},{1,9},{5,13},{9,1},{13,5},{2,10},{6,14},... | collective-permute-start | bytes 1572872 | tf_op jit(solution)/shard_map/ppermute | solution.py:398
  200.1 8.7 %copy-start.9 = (bf16[2,64,2048]{2,1,0:T(8,128)(2,1)}, bf16[2,64,2048]{2,1,0:T(8,128)(2,1)S(1)}, u32[]{:S(2)}) copy-start(bf16[2,64,2048]{2,1,0:T(8,128)(2,1)S(1)} %collective-permute-done.16.refs_2_) | copy-start | bytes 1572868
  200.1 8.7 %copy-start.10 = (bf16[2,64,2048]{2,1,0:T(8,128)(2,1)}, bf16[2,64,2048]{2,1,0:T(8,128)(2,1)S(1)}, u32[]{:S(2)}) copy-start(bf16[2,64,2048]{2,1,0:T(8,128)(2,1)S(1)} %collective-permute-done.17.refs_3_) | copy-start | bytes 1572868
  208.8 0.8 copy-start.11
Sparse Core Ops, SparseCore 0:
  9.6 60.9 all-gather.1
  73.2 73.1 reduce-scatter.1

commit v4 on v3

--- a/solution.py
+++ b/solution.py
@@ -420,13 +420,15 @@
         return [part] + [over_chips(part, s) for s in hops]
 
     def give(terms, after):
-        sends = held_back(rows_of(plan, TERM, terms, n_dev - 1, capacity), rotated(after))
+        sends = rows_of(plan, TERM, terms, n_dev - 1, capacity)
+        if after:
+            sends = held_back(sends, rotated(after))
         return sends, [over_line(x, s) for x, s in zip(sends, shifts)]
 
     down_seg, part = low_rank(plan, tokens, down_t, down_got, n_seg, [partial])
     act, up_terms = make_terms(segment_live_length, summed(part), cotangent)
 
-    sends, up_back = give(up_terms, up_got)
+    sends, up_back = give(up_terms, ())
     up_seg, part = low_rank(plan, cotangent, up_table, up_got, n_seg, [sends[-1]])
     grad, down_terms = make_terms(segment_live_length, summed(part), tokens)
 

time: 222 us -> 220 us (level)
  waiting for transfers between devices: 66.7 us -> 54.2 us
  starting transfers between devices: 32.4 us -> 43.1 us
    ppermute x15, waiting for transfers between devices: 55.8 us -> 44.9 us  [over_line(): return lax.ppermute(x, 'dp', [(i, (i + s) % n_dev) for i in range(n_dev)])]
    ppermute x15, starting transfers between devices: 29 us -> 39.8 us  [over_line(): return lax.ppermute(x, 'dp', [(i, (i + s) % n_dev) for i in range(n_dev)])]
    pallas_call x16 -> x15, Pallas kernels: 98.7 us -> 98.6 us  [call(): pl.pallas_call(body, grid_spec=pltpu.PrefetchScalarGridSpec(num_scalar_pr...]
  transfers between devices with their start and end apart: 21 -> 21, of which waited for: 11 -> 9; matrix products, arithmetic and copies ran while one was open for 1% -> 1% of each run, Pallas kernels for 43% -> 43%
where the time goes in v4:
time: 220 us; the launch traced here: 219 us
  Pallas kernels  98.6 us (45%)
  waiting for transfers between devices  54.2 us (25%)
  starting transfers between devices  43.1 us (20%)
  between operations  14.3 us (6%)
  local copies, waits for them, and re-layouts  7.2 us (3%)
    pallas_call x15, Pallas kernels, call(): pl.pallas_call(body, grid_spec=pltpu.PrefetchScalarGridSpec(num_scalar_pr...  98.6 us
    ppermute x15, waiting for transfers between devices, over_line(): return lax.ppermute(x, 'dp', [(i, (i + s) % n_dev) for i in range(n_dev)])  44.9 us
    ppermute x15, starting transfers between devices, over_line(): return lax.ppermute(x, 'dp', [(i, (i + s) % n_dev) for i in range(n_dev)])  39.8 us
    unnamed x46, local copies, waits for them, and re-layouts  7.2 us
    ppermute x2, waiting for transfers between devices, over_chips(): return lax.ppermute(x, 'tensor', pairs)  5.59 us
  transfers between devices with their start and end apart: 21, of which 9 were waited for; matrix products, arithmetic and copies ran while one was open for 1% of the time, Pallas kernels for 43%

profile of v4, /device:TPU:0, one launch (start us, length us, event | category | flops | bytes accessed | tf_op | source)
XLA Modules:
  0.0 219.1 jit_solution(1179595675149640457)
XLA Ops:
  7.2 0.0 all-gather.2.cloned.1.call-start
  7.2 0.7 all-gather.2.cloned.1.call-update
  7.9 0.0 reduce-scatter.2.cloned.1.call-start
  8.0 3.1 %collective-permute-start = (s32[4]{0:T(128)S(1)}, s32[4]{0:T(128)S(1)}, u32[]{:S(2)}, u32[]{:S(2)}) collective-permute-start(s32[4]{0:T(128)S(1)} %copy-done.16), channel_id=1, source_target_pairs={{0,4},{4,8},{8,12},{12,0},{1,5},{5,9},{9,13},{13,1},{2,6},{6,10},{... | collective-permute-start | bytes 56 | tf_op jit(solution)/shard_map/ppermute | solution.py:398
  11.0 2.6 %collective-permute-start.1 = (s32[4]{0:T(128)S(1)}, s32[4]{0:T(128)S(1)}, u32[]{:S(2)}, u32[]{:S(2)}) collective-permute-start(s32[4]{0:T(128)S(1)} %copy-done.16), channel_id=1, source_target_pairs={{0,8},{4,12},{8,0},{12,4},{1,9},{5,13},{9,1},{13,5},{2,10},{6,14},... | collective-permute-start | bytes 56 | tf_op jit(solution)/shard_map/ppermute | solution.py:398
  13.6 1.3 collective-permute-start.2
  15.0 0.5 collective-permute-done.1.refs_4_
  15.5 1.7 collective-permute-done.2.refs_5_
  17.2 0.5 copy-done.19
  17.7 3.9 %request.1 = (bf16[2,64,2048]{2,1,0:T(8,128)(2,1)}, bf16[2,64,2048]{2,1,0:T(8,128)(2,1)}, bf16[2,64,2048]{2,1,0:T(8,128)(2,1)}, s32[8,128]{1,0:T(8,128)}) custom-call(s32[1]{0:T(128)} %bitcast.refs_0_, s32[16]{0:T(128)} %refs_1_.6, s32[4]{0:T(128)} %refs_2_.2, s32[4]{0:T(128)} %copy-done.17, s32[4]{0:T(128)} %copy-done.18, s32[4]{0:T(128)} %copy-done.19, ...), custom_call_target="tpu_custom_call" | custom-call | bytes 2097152 | tf_op jit(solution)/shard_map/request/pallas_call | solution.py:32
  21.6 3.3 %collective-permute-start.3 = (bf16[2,64,2048]{2,1,0:T(8,128)(2,1)}, bf16[2,64,2048]{2,1,0:T(8,128)(2,1)S(1)}, u32[]{:S(2)}, u32[]{:S(2)}) collective-permute-start(bf16[2,64,2048]{2,1,0:T(8,128)(2,1)} %get-tuple-element.29.refs_2_), channel_id=1, source_target_pairs={{0,12},{4,0},{8,4},{12,8},{1,13},{5,1},{9,5},{13,9},{2,14},{6,2},{... | collective-permute-start | bytes 1572872 | tf_op jit(solution)/shard_map/ppermute | solution.py:398
  24.9 0.0 collective-permute-start.4
  24.9 0.6 collective-permute-start.5
  25.5 3.7 %rows.3 = (bf16[2,64,2048]{2,1,0:T(8,128)(2,1)}, bf16[2,64,2048]{2,1,0:T(8,128)(2,1)}, bf16[2,64,2048]{2,1,0:T(8,128)(2,1)}) custom-call(s32[8,128]{1,0:T(8,128)} %get-tuple-element.28.refs_0_, bf16[4,64,2048]{2,1,0:T(8,128)(2,1)} %refs_2_.3, bf16[2,64,2048]{2,1,0:T(8,128)(2,1)} %get-tuple-element.29.refs_2_), custom_call_target="tpu_custom_call" | custom-call | bytes 2097152 | tf_op jit(solution)/shard_map/rows/pallas_call | solution.py:32
  29.3 27.7 %forward.1.refs_0_ = bf16[512,8192]{1,0:T(8,128)(2,1)} custom-call(bf16[512,2048]{1,0:T(8,128)(2,1)} %refs_3_.3, bf16[2048,8192]{1,0:T(8,128)(2,1)} %refs_1_.11, bf16[2,64,2048]{2,1,0:T(8,128)(2,1)} %get-tuple-element.30.refs_2_), custom_call_target="tpu_custom_call" | custom-call | flops 17179869184 | bytes 33554432 | tf_op jit(solution)/shard_map/forward/pallas_call | solution.py:32
  56.9 0.0 collective-permute-done.3.refs_1_.refs_5_
  56.9 0.0 collective-permute-done.4.refs_2_.refs_3_
  57.0 10.4 %collective-permute-done.5.refs_3_.refs_4_ = bf16[2,64,2048]{2,1,0:T(8,128)(2,1)S(1)} collective-permute-done((bf16[2,64,2048]{2,1,0:T(8,128)(2,1)}, bf16[2,64,2048]{2,1,0:T(8,128)(2,1)S(1)}, u32[]{:S(2)}, u32[]{:S(2)}) %collective-permute-start.5) | collective-permute-done | bytes 524320 | tf_op jit(solution)/shard_map/ppermute | solution.py:398
  67.4 0.8 copy-done.2
  68.2 0.0 reduce-scatter.2.cloned.1.call-update
  68.2 1.0 copy-done.22
  69.2 0.0 collective-permute-start.8
  69.3 0.1 copy-done.20
  69.4 3.7 %collective-permute-start.10 = (bf16[2,64,2048]{2,1,0:T(8,128)(2,1)S(1)}, bf16[2,64,2048]{2,1,0:T(8,128)(2,1)S(1)}, u32[]{:S(2)}, u32[]{:S(2)}) collective-permute-start(bf16[2,64,2048]{2,1,0:T(8,128)(2,1)S(1)} %copy-done.20), channel_id=1, source_target_pairs={{0,12},{4,0},{8,4},{12,8},{1,13},{5,1},{9,5},{13,9},{2,14},{6,2},{... | collective-permute-start | bytes 1572872 | tf_op jit(solution)/shard_map/ppermute | solution.py:398
  73.1 4.8 %low_rank.2 = (bf16[4,64,2048]{2,1,0:T(8,128)(2,1)}, bf16[4,64,128]{2,1,0:T(8,128)(2,1)}) custom-call(s32[8,128]{1,0:T(8,128)} %get-tuple-element.28.refs_0_, bf16[512,2048]{1,0:T(8,128)(2,1)} %refs_3_.3, bf16[4,64,2048]{2,1,0:T(8,128)(2,1)} %bitcast.4, bf16[2,64,2048]{2,1,0:T(8,128)(2,1)} %copy-done.1, bf16[2,64,2048]{2,1,0:T(8,128)(2,1)} %copy-done.2, ...), custom_call_target="tpu_custom_call" | custom-call | flops 134217728 | bytes 4194304 | tf_op jit(solution)/shard_map/low_rank/pallas_call | solution.py:32
  77.9 0.1 collective-permute-start.6
  78.0 1.5 collective-permute-done.6
  79.5 0.9 add_convert_fusion.1.refs_1_
  80.4 0.0 copy-start.12
  80.4 1.6 collective-permute-start.7
  82.0 2.7 %collective-permute-done.7.refs_2_ = bf16[4,64,128]{2,1,0:T(8,128)(2,1)S(1)} collective-permute-done((bf16[4,64,128]{2,1,0:T(8,128)(2,1)S(1)}, bf16[4,64,128]{2,1,0:T(8,128)(2,1)S(1)}, u32[]{:S(2)}, u32[]{:S(2)}) %collective-permute-start.7) | collective-permute-done | bytes 65568 | tf_op jit(solution)/shard_map/ppermute | solution.py:395
  84.8 0.6 copy-done.14
  85.4 4.9 %terms.2 = (bf16[4,64,128]{2,1,0:T(8,128)(2,1)}, bf16[4,64,2048]{2,1,0:T(8,128)(2,1)}) custom-call(s32[4]{0:T(128)} %refs_0_.5, bf16[4,64,128]{2,1,0:T(8,128)(2,1)} %copy-done.12, bf16[4,64,128]{2,1,0:T(8,128)(2,1)} %copy-done.14, bf16[512,2048]{1,0:T(8,128)(2,1)} %refs_1_.10), custom_call_target="tpu_custom_call" | custom-call | flops 134217728 | bytes 4194304 | tf_op jit(solution)/shard_map/terms/pallas_call | solution.py:32
  90.3 3.4 %rows.4 = (bf16[2,64,2048]{2,1,0:T(8,128)(2,1)}, bf16[2,64,2048]{2,1,0:T(8,128)(2,1)}, bf16[2,64,2048]{2,1,0:T(8,128)(2,1)}) custom-call(s32[8,128]{1,0:T(8,128)} %get-tuple-element.28.refs_0_, bf16[4,64,2048]{2,1,0:T(8,128)(2,1)} %get-tuple-element.37.refs_1_), custom_call_target="tpu_custom_call" | custom-call | bytes 2097152 | tf_op jit(solution)/shard_map/rows/pallas_call | solution.py:32
  93.7 1.1 collective-permute-start.13
  94.8 1.0 collective-permute-start.14
  95.8 20.3 %collective-permute-start.15 = (bf16[2,64,2048]{2,1,0:T(8,128)(2,1)}, bf16[2,64,2048]{2,1,0:T(8,128)(2,1)S(1)}, u32[]{:S(2)}, u32[]{:S(2)}) collective-permute-start(bf16[2,64,2048]{2,1,0:T(8,128)(2,1)} %get-tuple-element.44), channel_id=1, source_target_pairs={{0,8},{4,12},{8,0},{12,4},{1,9},{5,13},{9,1},{13,5},{2,10},{6,14},... | collective-permute-start | bytes 1572872 | tf_op jit(solution)/shard_map/ppermute | solution.py:398
  116.2 22.6 %collective-permute-done.9.refs_4_ = bf16[2,64,2048]{2,1,0:T(8,128)(2,1)S(1)} collective-permute-done((bf16[2,64,2048]{2,1,0:T(8,128)(2,1)S(1)}, bf16[2,64,2048]{2,1,0:T(8,128)(2,1)S(1)}, u32[]{:S(2)}, u32[]{:S(2)}) %collective-permute-start.9) | collective-permute-done | bytes 524320 | tf_op jit(solution)/shard_map/ppermute | solution.py:398
  138.7 0.0 collective-permute-done.10.refs_5_
  138.7 0.8 copy-done.8
  139.5 0.8 copy-done.7
  140.3 4.8 %low_rank.3 = (bf16[4,64,2048]{2,1,0:T(8,128)(2,1)}, bf16[4,64,128]{2,1,0:T(8,128)(2,1)}) custom-call(s32[8,128]{1,0:T(8,128)} %get-tuple-element.28.refs_0_, bf16[512,2048]{1,0:T(8,128)(2,1)} %refs_1_.10, bf16[4,64,2048]{2,1,0:T(8,128)(2,1)} %refs_2_.3, bf16[2,64,2048]{2,1,0:T(8,128)(2,1)} %copy-done.6, bf16[2,64,2048]{2,1,0:T(8,128)(2,1)} %copy-done.8, ...), custom_call_target="tpu_custom_call" | custom-call | flops 134217728 | bytes 4194304 | tf_op jit(solution)/shard_map/low_rank/pallas_call | solution.py:32
  145.2 0.1 collective-permute-start.11
  145.2 1.5 collective-permute-done.11
  146.7 0.9 add_convert_fusion.refs_1_
  147.5 0.0 copy-start.13
  147.6 1.4 collective-permute-start.12
  149.0 2.9 %collective-permute-done.12.refs_2_ = bf16[4,64,128]{2,1,0:T(8,128)(2,1)S(1)} collective-permute-done((bf16[4,64,128]{2,1,0:T(8,128)(2,1)S(1)}, bf16[4,64,128]{2,1,0:T(8,128)(2,1)S(1)}, u32[]{:S(2)}, u32[]{:S(2)}) %collective-permute-start.12) | collective-permute-done | bytes 65568 | tf_op jit(solution)/shard_map/ppermute | solution.py:395
  151.9 0.6 copy-done.15
  152.5 4.7 %terms.3 = (bf16[4,64,128]{2,1,0:T(8,128)(2,1)}, bf16[4,64,2048]{2,1,0:T(8,128)(2,1)}) custom-call(s32[4]{0:T(128)} %refs_0_.5, bf16[4,64,128]{2,1,0:T(8,128)(2,1)} %copy-done.13, bf16[4,64,128]{2,1,0:T(8,128)(2,1)} %copy-done.15, bf16[512,2048]{1,0:T(8,128)(2,1)} %refs_3_.3), custom_call_target="tpu_custom_call" | custom-call | flops 134217728 | bytes 4194304 | tf_op jit(solution)/shard_map/terms/pallas_call | solution.py:32
  157.3 3.2 %rows.5 = (bf16[2,64,2048]{2,1,0:T(8,128)(2,1)}, bf16[2,64,2048]{2,1,0:T(8,128)(2,1)}, bf16[2,64,2048]{2,1,0:T(8,128)(2,1)}) custom-call(s32[8,128]{1,0:T(8,128)} %get-tuple-element.28.refs_0_, bf16[4,64,2048]{2,1,0:T(8,128)(2,1)} %get-tuple-element.45.refs_1_), custom_call_target="tpu_custom_call" | custom-call | bytes 2097152 | tf_op jit(solution)/shard_map/rows/pallas_call | solution.py:32
  160.5 0.0 copy-start.3
  160.5 0.0 collective-permute-done.14.refs_4_.refs_3_
  160.6 0.7 copy-done.3
  161.3 0.2 copy-done.4
  161.5 0.2 copy-done.5
  161.7 2.2 collective-permute-start.16
  163.9 0.6 collective-permute-start.18
  164.4 3.6 %totals.2.refs_4_ = f32[4,64,2048]{2,1,0:T(8,128)} custom-call(s32[8,128]{1,0:T(8,128)} %get-tuple-element.28.refs_0_, bf16[4,64,2048]{2,1,0:T(8,128)(2,1)} %get-tuple-element.37.refs_1_, bf16[2,64,2048]{2,1,0:T(8,128)(2,1)} %copy-done.3, bf16[2,64,2048]{2,1,0:T(8,128)(2,1)} %copy-done.4, bf16[2,64,2048]{2,1,0:T(8,128)(2,1)} %copy-done.5, ...), custom_call_target="tpu_custom_call" | custom-call | bytes 2097152 | tf_op jit(solution)/shard_map/totals/pallas_call | solution.py:32
  168.1 25.5 %backward.1.refs_3_ = bf16[512,2048]{1,0:T(8,128)(2,1)} custom-call(bf16[512,8192]{1,0:T(8,128)(2,1)} %all-gather.2.cloned.1.call-done.refs_0_, bf16[2048,8192]{1,0:T(8,128)(2,1)} %refs_1_.11, bf16[4,64,128]{2,1,0:T(8,128)(2,1)} %get-tuple-element.41.refs_2_, bf16[4,64,2048]{2,1,0:T(8,128)(2,1)} %get-tuple-element.42.refs_3_, f32[4,64,2048]{2,1,0:T(8,128)} %totals.2.refs_4_), custom_call_target="tpu_custom_call" | custom-call | flops 17179869184 | bytes 33554432 | tf_op jit(solution)/shard_map/backward/pallas_call | solution.py:32
  193.5 4.5 %adapt.1.refs_5_ = bf16[512,2048]{1,0:T(8,128)(2,1)} custom-call(bf16[512,2048]{1,0:T(8,128)(2,1)} %reduce-scatter.2.cloned.1.call-done.refs_0_, bf16[4,64,128]{2,1,0:T(8,128)(2,1)} %get-tuple-element.34.refs_1_, bf16[4,64,2048]{2,1,0:T(8,128)(2,1)} %get-tuple-element.39.refs_2_, bf16[512,2048]{1,0:T(8,128)(2,1)} %backward.1.refs_3_), custom_call_target="tpu_custom_call" | custom-call | flops 134217728 | bytes 4194304 | tf_op jit(solution)/shard_map/adapt/pallas_call | solution.py:32
  198.1 9.7 %collective-permute-done.18.refs_4_ = bf16[2,64,2048]{2,1,0:T(8,128)(2,1)S(1)} collective-permute-done((bf16[2,64,2048]{2,1,0:T(8,128)(2,1)}, bf16[2,64,2048]{2,1,0:T(8,128)(2,1)S(1)}, u32[]{:S(2)}, u32[]{:S(2)}) %collective-permute-start.18) | collective-permute-done | bytes 524320 | tf_op jit(solution)/shard_map/ppermute | solution.py:398
  207.8 0.8 copy-done.11
  208.6 3.6 %totals.3 = f32[4,64,2048]{2,1,0:T(8,128)} custom-call(s32[8,128]{1,0:T(8,128)} %get-tuple-element.28.refs_0_, bf16[4,64,2048]{2,1,0:T(8,128)(2,1)} %get-tuple-element.45.refs_1_, bf16[2,64,2048]{2,1,0:T(8,128)(2,1)} %copy-done.9, bf16[2,64,2048]{2,1,0:T(8,128)(2,1)} %copy-done.10, bf16[2,64,2048]{2,1,0:T(8,128)(2,1)} %copy-done.11, ...), custom_call_target="tpu_custom_call" | custom-call | bytes 2097152 | tf_op jit(solution)/shard_map/totals/pallas_call | solution.py:32
  (43 shorter events, 0.1 us)
Async XLA Ops:
  7.2 0.8 copy-start.16
  7.2 160.9 %all-gather.2.cloned.1.call-start = ((), (), s32[]{:S(2)}) async-start(), calls=%async_computation.2 | async-start | bytes 10485760 | tf_op jit(solution)/shard_map/all_gather | solution.py:403
  7.9 185.6 %reduce-scatter.2.cloned.1.call-start = ((), (), s32[]{:S(2)}) async-start(), calls=%async_computation.1 | async-start | bytes 10485760 | tf_op jit(solution)/shard_map/reduce_scatter | solution.py:416
  8.0 7.0 %collective-permute-start = (s32[4]{0:T(128)S(1)}, s32[4]{0:T(128)S(1)}, u32[]{:S(2)}, u32[]{:S(2)}) collective-permute-start(s32[4]{0:T(128)S(1)} %copy-done.16), channel_id=1, source_target_pairs={{0,4},{4,8},{8,12},{12,0},{1,5},{5,9},{9,13},{13,1},{2,6},{6,10},{... | collective-permute-start | bytes 56 | tf_op jit(solution)/shard_map/ppermute | solution.py:398
  11.0 4.4 %collective-permute-start.1 = (s32[4]{0:T(128)S(1)}, s32[4]{0:T(128)S(1)}, u32[]{:S(2)}, u32[]{:S(2)}) collective-permute-start(s32[4]{0:T(128)S(1)} %copy-done.16), channel_id=1, source_target_pairs={{0,8},{4,12},{8,0},{12,4},{1,9},{5,13},{9,1},{13,5},{2,10},{6,14},... | collective-permute-start | bytes 56 | tf_op jit(solution)/shard_map/ppermute | solution.py:398
  13.6 3.5 %collective-permute-start.2 = (s32[4]{0:T(128)S(1)}, s32[4]{0:T(128)S(1)}, u32[]{:S(2)}, u32[]{:S(2)}) collective-permute-start(s32[4]{0:T(128)S(1)} %copy-done.16), channel_id=1, source_target_pairs={{0,12},{4,0},{8,4},{12,8},{1,13},{5,1},{9,5},{13,9},{2,14},{6,2},{... | collective-permute-start | bytes 56 | tf_op jit(solution)/shard_map/ppermute | solution.py:398
  15.0 2.2 %copy-start.17 = (s32[4]{0:T(128)}, s32[4]{0:T(128)S(1)}, u32[]{:S(2)}) copy-start(s32[4]{0:T(128)S(1)} %collective-permute-done.refs_3_) | copy-start | bytes 52
  15.5 1.7 copy-start.18
  17.2 0.5 copy-start.19
  21.6 35.3 %collective-permute-start.3 = (bf16[2,64,2048]{2,1,0:T(8,128)(2,1)}, bf16[2,64,2048]{2,1,0:T(8,128)(2,1)S(1)}, u32[]{:S(2)}, u32[]{:S(2)}) collective-permute-start(bf16[2,64,2048]{2,1,0:T(8,128)(2,1)} %get-tuple-element.29.refs_2_), channel_id=1, source_target_pairs={{0,12},{4,0},{8,4},{12,8},{1,13},{5,1},{9,5},{13,9},{2,14},{6,2},{... | collective-permute-start | bytes 1572872 | tf_op jit(solution)/shard_map/ppermute | solution.py:398
  24.9 32.0 %collective-permute-start.4 = (bf16[2,64,2048]{2,1,0:T(8,128)(2,1)}, bf16[2,64,2048]{2,1,0:T(8,128)(2,1)S(1)}, u32[]{:S(2)}, u32[]{:S(2)}) collective-permute-start(bf16[2,64,2048]{2,1,0:T(8,128)(2,1)} %get-tuple-element.31), channel_id=1, source_target_pairs={{0,4},{4,8},{8,12},{12,0},{1,5},{5,9},{9,13},{13,1},{2,6},{6,10},{... | collective-permute-start | bytes 1572872 | tf_op jit(solution)/shard_map/ppermute | solution.py:398
  24.9 42.5 %collective-permute-start.5 = (bf16[2,64,2048]{2,1,0:T(8,128)(2,1)}, bf16[2,64,2048]{2,1,0:T(8,128)(2,1)S(1)}, u32[]{:S(2)}, u32[]{:S(2)}) collective-permute-start(bf16[2,64,2048]{2,1,0:T(8,128)(2,1)} %get-tuple-element.32), channel_id=1, source_target_pairs={{0,8},{4,12},{8,0},{12,4},{1,9},{5,13},{9,1},{13,5},{2,10},{6,14},... | collective-permute-start | bytes 1572872 | tf_op jit(solution)/shard_map/ppermute | solution.py:398
  56.9 10.5 %copy-start = (bf16[2,64,2048]{2,1,0:T(8,128)(2,1)}, bf16[2,64,2048]{2,1,0:T(8,128)(2,1)S(1)}, u32[]{:S(2)}) copy-start(bf16[2,64,2048]{2,1,0:T(8,128)(2,1)S(1)} %collective-permute-done.3.refs_1_.refs_5_) | copy-start | bytes 1572868
  57.0 10.4 %copy-start.1 = (bf16[2,64,2048]{2,1,0:T(8,128)(2,1)}, bf16[2,64,2048]{2,1,0:T(8,128)(2,1)S(1)}, u32[]{:S(2)}) copy-start(bf16[2,64,2048]{2,1,0:T(8,128)(2,1)S(1)} %collective-permute-done.4.refs_2_.refs_3_) | copy-start | bytes 1572868
  67.4 0.8 copy-start.2
  68.2 1.0 copy-start.22
  68.2 1.2 copy-start.20
  68.2 4.9 %copy-start.21 = (bf16[2,64,2048]{2,1,0:T(8,128)(2,1)S(1)}, bf16[2,64,2048]{2,1,0:T(8,128)(2,1)}, u32[]{:S(2)}) copy-start(bf16[2,64,2048]{2,1,0:T(8,128)(2,1)} %get-tuple-element.36) | copy-start | bytes 1572868
  69.2 26.6 %collective-permute-start.8 = (bf16[2,64,2048]{2,1,0:T(8,128)(2,1)S(1)}, bf16[2,64,2048]{2,1,0:T(8,128)(2,1)S(1)}, u32[]{:S(2)}, u32[]{:S(2)}) collective-permute-start(bf16[2,64,2048]{2,1,0:T(8,128)(2,1)S(1)} %copy-done.22), channel_id=1, source_target_pairs={{0,4},{4,8},{8,12},{12,0},{1,5},{5,9},{9,13},{13,1},{2,6},{6,10},{... | collective-permute-start | bytes 1572872 | tf_op jit(solution)/shard_map/ppermute | solution.py:398
  69.4 69.3 %collective-permute-start.10 = (bf16[2,64,2048]{2,1,0:T(8,128)(2,1)S(1)}, bf16[2,64,2048]{2,1,0:T(8,128)(2,1)S(1)}, u32[]{:S(2)}, u32[]{:S(2)}) collective-permute-start(bf16[2,64,2048]{2,1,0:T(8,128)(2,1)S(1)} %copy-done.20), channel_id=1, source_target_pairs={{0,12},{4,0},{8,4},{12,8},{1,13},{5,1},{9,5},{13,9},{2,14},{6,2},{... | collective-permute-start | bytes 1572872 | tf_op jit(solution)/shard_map/ppermute | solution.py:398
  73.1 65.7 %collective-permute-start.9 = (bf16[2,64,2048]{2,1,0:T(8,128)(2,1)S(1)}, bf16[2,64,2048]{2,1,0:T(8,128)(2,1)S(1)}, u32[]{:S(2)}, u32[]{:S(2)}) collective-permute-start(bf16[2,64,2048]{2,1,0:T(8,128)(2,1)S(1)} %copy-done.21), channel_id=1, source_target_pairs={{0,8},{4,12},{8,0},{12,4},{1,9},{5,13},{9,1},{13,5},{2,10},{6,14},... | collective-permute-start | bytes 1572872 | tf_op jit(solution)/shard_map/ppermute | solution.py:398
  77.9 1.6 collective-permute-start.6
  80.4 4.3 %copy-start.12 = (bf16[4,64,128]{2,1,0:T(8,128)(2,1)}, bf16[4,64,128]{2,1,0:T(8,128)(2,1)S(1)}, u32[]{:S(2)}) copy-start(bf16[4,64,128]{2,1,0:T(8,128)(2,1)S(1)} %add_convert_fusion.1.refs_1_) | copy-start | bytes 196612
  80.4 4.3 %collective-permute-start.7 = (bf16[4,64,128]{2,1,0:T(8,128)(2,1)S(1)}, bf16[4,64,128]{2,1,0:T(8,128)(2,1)S(1)}, u32[]{:S(2)}, u32[]{:S(2)}) collective-permute-start(bf16[4,64,128]{2,1,0:T(8,128)(2,1)S(1)} %add_convert_fusion.1.refs_1_), channel_id=1, source_target_pairs={{0,2},{1,3},{2,0},{3,1},{4,6},{5,7},{6,4},{7,5},{8,10},{9,11},{10,... | collective-permute-start | bytes 196616 | tf_op jit(solution)/shard_map/ppermute | solution.py:395
  84.8 0.6 copy-start.14
  93.7 66.8 %collective-permute-start.13 = (bf16[2,64,2048]{2,1,0:T(8,128)(2,1)}, bf16[2,64,2048]{2,1,0:T(8,128)(2,1)S(1)}, u32[]{:S(2)}, u32[]{:S(2)}) collective-permute-start(bf16[2,64,2048]{2,1,0:T(8,128)(2,1)} %get-tuple-element.38.refs_6_), channel_id=1, source_target_pairs={{0,12},{4,0},{8,4},{12,8},{1,13},{5,1},{9,5},{13,9},{2,14},{6,2},{... | collective-permute-start | bytes 1572872 | tf_op jit(solution)/shard_map/ppermute | solution.py:398
  94.8 65.7 %collective-permute-start.14 = (bf16[2,64,2048]{2,1,0:T(8,128)(2,1)}, bf16[2,64,2048]{2,1,0:T(8,128)(2,1)S(1)}, u32[]{:S(2)}, u32[]{:S(2)}) collective-permute-start(bf16[2,64,2048]{2,1,0:T(8,128)(2,1)} %get-tuple-element.43), channel_id=1, source_target_pairs={{0,4},{4,8},{8,12},{12,0},{1,5},{5,9},{9,13},{13,1},{2,6},{6,10},{... | collective-permute-start | bytes 1572872 | tf_op jit(solution)/shard_map/ppermute | solution.py:398
  95.8 42.9 %copy-start.6 = (bf16[2,64,2048]{2,1,0:T(8,128)(2,1)}, bf16[2,64,2048]{2,1,0:T(8,128)(2,1)S(1)}, u32[]{:S(2)}) copy-start(bf16[2,64,2048]{2,1,0:T(8,128)(2,1)S(1)} %collective-permute-done.8.refs_3_) | copy-start | bytes 1572868
  95.8 64.7 %collective-permute-start.15 = (bf16[2,64,2048]{2,1,0:T(8,128)(2,1)}, bf16[2,64,2048]{2,1,0:T(8,128)(2,1)S(1)}, u32[]{:S(2)}, u32[]{:S(2)}) collective-permute-start(bf16[2,64,2048]{2,1,0:T(8,128)(2,1)} %get-tuple-element.44), channel_id=1, source_target_pairs={{0,8},{4,12},{8,0},{12,4},{1,9},{5,13},{9,1},{13,5},{2,10},{6,14},... | collective-permute-start | bytes 1572872 | tf_op jit(solution)/shard_map/ppermute | solution.py:398
  138.7 0.8 copy-start.8
  139.5 0.8 copy-start.7
  145.2 1.5 collective-permute-start.11
  147.5 4.3 %copy-start.13 = (bf16[4,64,128]{2,1,0:T(8,128)(2,1)}, bf16[4,64,128]{2,1,0:T(8,128)(2,1)S(1)}, u32[]{:S(2)}) copy-start(bf16[4,64,128]{2,1,0:T(8,128)(2,1)S(1)} %add_convert_fusion.refs_1_) | copy-start | bytes 196612
  147.6 4.3 %collective-permute-start.12 = (bf16[4,64,128]{2,1,0:T(8,128)(2,1)S(1)}, bf16[4,64,128]{2,1,0:T(8,128)(2,1)S(1)}, u32[]{:S(2)}, u32[]{:S(2)}) collective-permute-start(bf16[4,64,128]{2,1,0:T(8,128)(2,1)S(1)} %add_convert_fusion.refs_1_), channel_id=1, source_target_pairs={{0,2},{1,3},{2,0},{3,1},{4,6},{5,7},{6,4},{7,5},{8,10},{9,11},{10,... | collective-permute-start | bytes 196616 | tf_op jit(solution)/shard_map/ppermute | solution.py:395
  151.9 0.6 copy-start.15
  160.5 0.8 copy-start.3
  160.5 1.0 copy-start.4
  160.6 1.1 copy-start.5
  161.7 36.4 %collective-permute-start.16 = (bf16[2,64,2048]{2,1,0:T(8,128)(2,1)}, bf16[2,64,2048]{2,1,0:T(8,128)(2,1)S(1)}, u32[]{:S(2)}, u32[]{:S(2)}) collective-permute-start(bf16[2,64,2048]{2,1,0:T(8,128)(2,1)} %get-tuple-element.49.refs_5_), channel_id=1, source_target_pairs={{0,12},{4,0},{8,4},{12,8},{1,13},{5,1},{9,5},{13,9},{2,14},{6,2},{... | collective-permute-start | bytes 1572872 | tf_op jit(solution)/shard_map/ppermute | solution.py:398
  163.9 34.2 %collective-permute-start.17 = (bf16[2,64,2048]{2,1,0:T(8,128)(2,1)}, bf16[2,64,2048]{2,1,0:T(8,128)(2,1)S(1)}, u32[]{:S(2)}, u32[]{:S(2)}) collective-permute-start(bf16[2,64,2048]{2,1,0:T(8,128)(2,1)} %get-tuple-element.50), channel_id=1, source_target_pairs={{0,4},{4,8},{8,12},{12,0},{1,5},{5,9},{9,13},{13,1},{2,6},{6,10},{... | collective-permute-start | bytes 1572872 | tf_op jit(solution)/shard_map/ppermute | solution.py:398
  163.9 43.9 %collective-permute-start.18 = (bf16[2,64,2048]{2,1,0:T(8,128)(2,1)}, bf16[2,64,2048]{2,1,0:T(8,128)(2,1)S(1)}, u32[]{:S(2)}, u32[]{:S(2)}) collective-permute-start(bf16[2,64,2048]{2,1,0:T(8,128)(2,1)} %get-tuple-element.51), channel_id=1, source_target_pairs={{0,8},{4,12},{8,0},{12,4},{1,9},{5,13},{9,1},{13,5},{2,10},{6,14},... | collective-permute-start | bytes 1572872 | tf_op jit(solution)/shard_map/ppermute | solution.py:398
  198.1 9.7 %copy-start.9 = (bf16[2,64,2048]{2,1,0:T(8,128)(2,1)}, bf16[2,64,2048]{2,1,0:T(8,128)(2,1)S(1)}, u32[]{:S(2)}) copy-start(bf16[2,64,2048]{2,1,0:T(8,128)(2,1)S(1)} %collective-permute-done.16.refs_2_) | copy-start | bytes 1572868
  198.1 9.7 %copy-start.10 = (bf16[2,64,2048]{2,1,0:T(8,128)(2,1)}, bf16[2,64,2048]{2,1,0:T(8,128)(2,1)S(1)}, u32[]{:S(2)}) copy-start(bf16[2,64,2048]{2,1,0:T(8,128)(2,1)S(1)} %collective-permute-done.17.refs_3_) | copy-start | bytes 1572868
  207.8 0.8 copy-start.11
Sparse Core Ops, SparseCore 0:
  9.6 60.9 all-gather.1
  73.2 71.7 reduce-scatter.1

commit v5 on v4

--- a/solution.py
+++ b/solution.py
@@ -56,14 +56,16 @@
     for read in reads:
         read.start()
 
-    def finish_copies():
+    def pass_on():
         for read, write in zip(reads, writes):
             read.wait()
             write.start()
+
+    def finish():
         for write in writes:
             write.wait()
 
-    return finish_copies
+    return pass_on, finish
 
 
 def copies_of(table, count):
@@ -94,7 +96,8 @@
             plan_ref[GIVEN, jnp.where(mine, (s - 1) * capacity + order, spare)] = local
             order = order + mine.astype(jnp.int32)
     rows = [plan_ref[SEND, c] for c in range(len(outs) * capacity)]
-    finish_copies = copy_rows(rows, table_ref, outs, held, sem)
+    pass_on, finish = copy_rows(rows, table_ref, outs, held, sem)
+    pass_on()
     slots = [row_ref[id_refs[0][k]] for k in range(n_seg)]
     owners = [lax.div(v, n_own) for v in slots]
     for k in range(n_seg):
@@ -107,7 +110,7 @@
         from_owner = (n_dev - away - 1) * capacity + order
         plan_ref[SOURCE, k] = jnp.where(away == 0, local, n_own + from_owner)
         plan_ref[TERM, jnp.where(away == 0, spare, (away - 1) * capacity + order)] = k
-    finish_copies()
+    finish()
 
 
 def request(me, table_row, ids, table, capacity):
@@ -130,7 +133,8 @@
 def rows_kernel(row, plan_ref, table_ref, *rest):
     outs, (held, sem) = rest[:-2], rest[-2:]
     rows = [jnp.maximum(plan_ref[row, c], 0) for c in range(len(outs) * outs[0].shape[0])]
-    copy_rows(rows, table_ref, outs, held, sem)()
+    for step in copy_rows(rows, table_ref, outs, held, sem):
+        step()
 
 
 def rows_of(plan, row, table, count, capacity, after=()):

time: 220 us -> 220 us (level)
  no operation moved by 1% of the time
where the time goes in v5:
time: 220 us; the launch traced here: 219 us
  Pallas kernels  99.1 us (45%)
  waiting for transfers between devices  54.4 us (25%)
  starting transfers between devices  42.4 us (19%)
  between operations  14.3 us (6%)
  local copies, waits for them, and re-layouts  7.24 us (3%)
    pallas_call x15, Pallas kernels, call(): pl.pallas_call(body, grid_spec=pltpu.PrefetchScalarGridSpec(num_scalar_pr...  99.1 us
    ppermute x15, waiting for transfers between devices, over_line(): return lax.ppermute(x, 'dp', [(i, (i + s) % n_dev) for i in range(n_dev)])  45 us
    ppermute x15, starting transfers between devices, over_line(): return lax.ppermute(x, 'dp', [(i, (i + s) % n_dev) for i in range(n_dev)])  39.2 us
    unnamed x46, local copies, waits for them, and re-layouts  7.24 us
    ppermute x2, waiting for transfers between devices, over_chips(): return lax.ppermute(x, 'tensor', pairs)  5.63 us
  transfers between devices with their start and end apart: 21, of which 9 were waited for; matrix products, arithmetic and copies ran while one was open for 1% of the time, Pallas kernels for 43%

profile of v5, /device:TPU:0, one launch (start us, length us, event | category | flops | bytes accessed | tf_op | source)
XLA Modules:
  0.0 219.2 jit_solution(389180559965149383)
XLA Ops:
  7.2 0.0 all-gather.2.cloned.1.call-start
  7.2 0.7 all-gather.2.cloned.1.call-update
  7.9 0.0 reduce-scatter.2.cloned.1.call-start
  8.0 3.1 %collective-permute-start = (s32[4]{0:T(128)S(1)}, s32[4]{0:T(128)S(1)}, u32[]{:S(2)}, u32[]{:S(2)}) collective-permute-start(s32[4]{0:T(128)S(1)} %copy-done.16), channel_id=1, source_target_pairs={{0,4},{4,8},{8,12},{12,0},{1,5},{5,9},{9,13},{13,1},{2,6},{6,10},{... | collective-permute-start | bytes 56 | tf_op jit(solution)/shard_map/ppermute | solution.py:402
  11.0 2.6 %collective-permute-start.1 = (s32[4]{0:T(128)S(1)}, s32[4]{0:T(128)S(1)}, u32[]{:S(2)}, u32[]{:S(2)}) collective-permute-start(s32[4]{0:T(128)S(1)} %copy-done.16), channel_id=1, source_target_pairs={{0,8},{4,12},{8,0},{12,4},{1,9},{5,13},{9,1},{13,5},{2,10},{6,14},... | collective-permute-start | bytes 56 | tf_op jit(solution)/shard_map/ppermute | solution.py:402
  13.6 1.3 collective-permute-start.2
  15.0 0.0 collective-permute-done.refs_3_
  15.0 0.5 collective-permute-done.1.refs_4_
  15.5 1.7 collective-permute-done.2.refs_5_
  17.2 0.5 copy-done.19
  17.7 3.7 %request.1 = (bf16[2,64,2048]{2,1,0:T(8,128)(2,1)}, bf16[2,64,2048]{2,1,0:T(8,128)(2,1)}, bf16[2,64,2048]{2,1,0:T(8,128)(2,1)}, s32[8,128]{1,0:T(8,128)}) custom-call(s32[1]{0:T(128)} %bitcast.refs_0_, s32[16]{0:T(128)} %refs_1_.6, s32[4]{0:T(128)} %refs_2_.2, s32[4]{0:T(128)} %copy-done.17, s32[4]{0:T(128)} %copy-done.18, s32[4]{0:T(128)} %copy-done.19, ...), custom_call_target="tpu_custom_call" | custom-call | bytes 2097152 | tf_op jit(solution)/shard_map/request/pallas_call | solution.py:32
  21.4 3.2 %collective-permute-start.3 = (bf16[2,64,2048]{2,1,0:T(8,128)(2,1)}, bf16[2,64,2048]{2,1,0:T(8,128)(2,1)S(1)}, u32[]{:S(2)}, u32[]{:S(2)}) collective-permute-start(bf16[2,64,2048]{2,1,0:T(8,128)(2,1)} %get-tuple-element.29.refs_2_), channel_id=1, source_target_pairs={{0,12},{4,0},{8,4},{12,8},{1,13},{5,1},{9,5},{13,9},{2,14},{6,2},{... | collective-permute-start | bytes 1572872 | tf_op jit(solution)/shard_map/ppermute | solution.py:402
  24.6 0.0 collective-permute-start.4
  24.6 0.6 collective-permute-start.5
  25.3 3.5 %rows.3 = (bf16[2,64,2048]{2,1,0:T(8,128)(2,1)}, bf16[2,64,2048]{2,1,0:T(8,128)(2,1)}, bf16[2,64,2048]{2,1,0:T(8,128)(2,1)}) custom-call(s32[8,128]{1,0:T(8,128)} %get-tuple-element.28.refs_0_, bf16[4,64,2048]{2,1,0:T(8,128)(2,1)} %refs_2_.3, bf16[2,64,2048]{2,1,0:T(8,128)(2,1)} %get-tuple-element.29.refs_2_), custom_call_target="tpu_custom_call" | custom-call | bytes 2097152 | tf_op jit(solution)/shard_map/rows/pallas_call | solution.py:32
  28.8 27.6 %forward.1.refs_0_ = bf16[512,8192]{1,0:T(8,128)(2,1)} custom-call(bf16[512,2048]{1,0:T(8,128)(2,1)} %refs_3_.3, bf16[2048,8192]{1,0:T(8,128)(2,1)} %refs_1_.11, bf16[2,64,2048]{2,1,0:T(8,128)(2,1)} %get-tuple-element.30.refs_2_), custom_call_target="tpu_custom_call" | custom-call | flops 17179869184 | bytes 33554432 | tf_op jit(solution)/shard_map/forward/pallas_call | solution.py:32
  56.4 0.0 collective-permute-done.3.refs_1_.refs_5_
  56.5 11.1 %collective-permute-done.5.refs_3_.refs_4_ = bf16[2,64,2048]{2,1,0:T(8,128)(2,1)S(1)} collective-permute-done((bf16[2,64,2048]{2,1,0:T(8,128)(2,1)}, bf16[2,64,2048]{2,1,0:T(8,128)(2,1)S(1)}, u32[]{:S(2)}, u32[]{:S(2)}) %collective-permute-start.5) | collective-permute-done | bytes 524320 | tf_op jit(solution)/shard_map/ppermute | solution.py:402
  67.5 0.8 copy-done.2
  68.3 0.0 reduce-scatter.2.cloned.1.call-update
  68.4 1.0 copy-done.22
  69.4 0.0 collective-permute-start.8
  69.4 0.2 copy-done.20
  69.5 3.7 %collective-permute-start.10 = (bf16[2,64,2048]{2,1,0:T(8,128)(2,1)S(1)}, bf16[2,64,2048]{2,1,0:T(8,128)(2,1)S(1)}, u32[]{:S(2)}, u32[]{:S(2)}) collective-permute-start(bf16[2,64,2048]{2,1,0:T(8,128)(2,1)S(1)} %copy-done.20), channel_id=1, source_target_pairs={{0,12},{4,0},{8,4},{12,8},{1,13},{5,1},{9,5},{13,9},{2,14},{6,2},{... | collective-permute-start | bytes 1572872 | tf_op jit(solution)/shard_map/ppermute | solution.py:402
  73.2 0.0 collective-permute-start.9
  73.2 4.8 %low_rank.2 = (bf16[4,64,2048]{2,1,0:T(8,128)(2,1)}, bf16[4,64,128]{2,1,0:T(8,128)(2,1)}) custom-call(s32[8,128]{1,0:T(8,128)} %get-tuple-element.28.refs_0_, bf16[512,2048]{1,0:T(8,128)(2,1)} %refs_3_.3, bf16[4,64,2048]{2,1,0:T(8,128)(2,1)} %bitcast.4, bf16[2,64,2048]{2,1,0:T(8,128)(2,1)} %copy-done.1, bf16[2,64,2048]{2,1,0:T(8,128)(2,1)} %copy-done.2, ...), custom_call_target="tpu_custom_call" | custom-call | flops 134217728 | bytes 4194304 | tf_op jit(solution)/shard_map/low_rank/pallas_call | solution.py:32
  78.1 0.1 collective-permute-start.6
  78.1 1.5 collective-permute-done.6
  79.7 0.9 add_convert_fusion.1.refs_1_
  80.5 0.0 copy-start.12
  80.6 1.6 collective-permute-start.7
  82.1 2.7 %collective-permute-done.7.refs_2_ = bf16[4,64,128]{2,1,0:T(8,128)(2,1)S(1)} collective-permute-done((bf16[4,64,128]{2,1,0:T(8,128)(2,1)S(1)}, bf16[4,64,128]{2,1,0:T(8,128)(2,1)S(1)}, u32[]{:S(2)}, u32[]{:S(2)}) %collective-permute-start.7) | collective-permute-done | bytes 65568 | tf_op jit(solution)/shard_map/ppermute | solution.py:399
  84.9 0.6 copy-done.14
  85.5 5.0 %terms.2 = (bf16[4,64,128]{2,1,0:T(8,128)(2,1)}, bf16[4,64,2048]{2,1,0:T(8,128)(2,1)}) custom-call(s32[4]{0:T(128)} %refs_0_.5, bf16[4,64,128]{2,1,0:T(8,128)(2,1)} %copy-done.12, bf16[4,64,128]{2,1,0:T(8,128)(2,1)} %copy-done.14, bf16[512,2048]{1,0:T(8,128)(2,1)} %refs_1_.10), custom_call_target="tpu_custom_call" | custom-call | flops 134217728 | bytes 4194304 | tf_op jit(solution)/shard_map/terms/pallas_call | solution.py:32
  90.5 3.7 %rows.4 = (bf16[2,64,2048]{2,1,0:T(8,128)(2,1)}, bf16[2,64,2048]{2,1,0:T(8,128)(2,1)}, bf16[2,64,2048]{2,1,0:T(8,128)(2,1)}) custom-call(s32[8,128]{1,0:T(8,128)} %get-tuple-element.28.refs_0_, bf16[4,64,2048]{2,1,0:T(8,128)(2,1)} %get-tuple-element.37.refs_1_), custom_call_target="tpu_custom_call" | custom-call | bytes 2097152 | tf_op jit(solution)/shard_map/rows/pallas_call | solution.py:32
  94.2 0.8 collective-permute-start.13
  95.0 1.3 collective-permute-start.14
  96.3 20.0 %collective-permute-start.15 = (bf16[2,64,2048]{2,1,0:T(8,128)(2,1)}, bf16[2,64,2048]{2,1,0:T(8,128)(2,1)S(1)}, u32[]{:S(2)}, u32[]{:S(2)}) collective-permute-start(bf16[2,64,2048]{2,1,0:T(8,128)(2,1)} %get-tuple-element.44), channel_id=1, source_target_pairs={{0,8},{4,12},{8,0},{12,4},{1,9},{5,13},{9,1},{13,5},{2,10},{6,14},... | collective-permute-start | bytes 1572872 | tf_op jit(solution)/shard_map/ppermute | solution.py:402
  116.3 22.5 %collective-permute-done.9.refs_4_ = bf16[2,64,2048]{2,1,0:T(8,128)(2,1)S(1)} collective-permute-done((bf16[2,64,2048]{2,1,0:T(8,128)(2,1)S(1)}, bf16[2,64,2048]{2,1,0:T(8,128)(2,1)S(1)}, u32[]{:S(2)}, u32[]{:S(2)}) %collective-permute-start.9) | collective-permute-done | bytes 524320 | tf_op jit(solution)/shard_map/ppermute | solution.py:402
  138.9 0.8 copy-done.8
  139.7 0.8 copy-done.7
  140.5 4.8 %low_rank.3 = (bf16[4,64,2048]{2,1,0:T(8,128)(2,1)}, bf16[4,64,128]{2,1,0:T(8,128)(2,1)}) custom-call(s32[8,128]{1,0:T(8,128)} %get-tuple-element.28.refs_0_, bf16[512,2048]{1,0:T(8,128)(2,1)} %refs_1_.10, bf16[4,64,2048]{2,1,0:T(8,128)(2,1)} %refs_2_.3, bf16[2,64,2048]{2,1,0:T(8,128)(2,1)} %copy-done.6, bf16[2,64,2048]{2,1,0:T(8,128)(2,1)} %copy-done.8, ...), custom_call_target="tpu_custom_call" | custom-call | flops 134217728 | bytes 4194304 | tf_op jit(solution)/shard_map/low_rank/pallas_call | solution.py:32
  145.3 0.1 collective-permute-start.11
  145.4 1.5 collective-permute-done.11
  146.8 0.9 add_convert_fusion.refs_1_
  147.7 0.0 copy-start.13
  147.7 1.4 collective-permute-start.12
  149.1 2.9 %collective-permute-done.12.refs_2_ = bf16[4,64,128]{2,1,0:T(8,128)(2,1)S(1)} collective-permute-done((bf16[4,64,128]{2,1,0:T(8,128)(2,1)S(1)}, bf16[4,64,128]{2,1,0:T(8,128)(2,1)S(1)}, u32[]{:S(2)}, u32[]{:S(2)}) %collective-permute-start.12) | collective-permute-done | bytes 65568 | tf_op jit(solution)/shard_map/ppermute | solution.py:399
  152.0 0.6 copy-done.15
  152.7 4.7 %terms.3 = (bf16[4,64,128]{2,1,0:T(8,128)(2,1)}, bf16[4,64,2048]{2,1,0:T(8,128)(2,1)}) custom-call(s32[4]{0:T(128)} %refs_0_.5, bf16[4,64,128]{2,1,0:T(8,128)(2,1)} %copy-done.13, bf16[4,64,128]{2,1,0:T(8,128)(2,1)} %copy-done.15, bf16[512,2048]{1,0:T(8,128)(2,1)} %refs_3_.3), custom_call_target="tpu_custom_call" | custom-call | flops 134217728 | bytes 4194304 | tf_op jit(solution)/shard_map/terms/pallas_call | solution.py:32
  157.4 3.5 %rows.5 = (bf16[2,64,2048]{2,1,0:T(8,128)(2,1)}, bf16[2,64,2048]{2,1,0:T(8,128)(2,1)}, bf16[2,64,2048]{2,1,0:T(8,128)(2,1)}) custom-call(s32[8,128]{1,0:T(8,128)} %get-tuple-element.28.refs_0_, bf16[4,64,2048]{2,1,0:T(8,128)(2,1)} %get-tuple-element.45.refs_1_), custom_call_target="tpu_custom_call" | custom-call | bytes 2097152 | tf_op jit(solution)/shard_map/rows/pallas_call | solution.py:32
  160.9 0.0 copy-start.3
  161.0 0.7 copy-done.3
  161.7 0.2 copy-done.4
  161.9 0.2 copy-done.5
  162.1 2.0 collective-permute-start.16
  164.1 0.0 collective-permute-start.17
  164.1 0.5 collective-permute-start.18
  164.6 3.8 %totals.2.refs_4_ = f32[4,64,2048]{2,1,0:T(8,128)} custom-call(s32[8,128]{1,0:T(8,128)} %get-tuple-element.28.refs_0_, bf16[4,64,2048]{2,1,0:T(8,128)(2,1)} %get-tuple-element.37.refs_1_, bf16[2,64,2048]{2,1,0:T(8,128)(2,1)} %copy-done.3, bf16[2,64,2048]{2,1,0:T(8,128)(2,1)} %copy-done.4, bf16[2,64,2048]{2,1,0:T(8,128)(2,1)} %copy-done.5, ...), custom_call_target="tpu_custom_call" | custom-call | bytes 2097152 | tf_op jit(solution)/shard_map/totals/pallas_call | solution.py:32
  168.4 25.5 %backward.1.refs_3_ = bf16[512,2048]{1,0:T(8,128)(2,1)} custom-call(bf16[512,8192]{1,0:T(8,128)(2,1)} %all-gather.2.cloned.1.call-done.refs_0_, bf16[2048,8192]{1,0:T(8,128)(2,1)} %refs_1_.11, bf16[4,64,128]{2,1,0:T(8,128)(2,1)} %get-tuple-element.41.refs_2_, bf16[4,64,2048]{2,1,0:T(8,128)(2,1)} %get-tuple-element.42.refs_3_, f32[4,64,2048]{2,1,0:T(8,128)} %totals.2.refs_4_), custom_call_target="tpu_custom_call" | custom-call | flops 17179869184 | bytes 33554432 | tf_op jit(solution)/shard_map/backward/pallas_call | solution.py:32
  193.9 4.5 %adapt.1.refs_5_ = bf16[512,2048]{1,0:T(8,128)(2,1)} custom-call(bf16[512,2048]{1,0:T(8,128)(2,1)} %reduce-scatter.2.cloned.1.call-done.refs_0_, bf16[4,64,128]{2,1,0:T(8,128)(2,1)} %get-tuple-element.34.refs_1_, bf16[4,64,2048]{2,1,0:T(8,128)(2,1)} %get-tuple-element.39.refs_2_, bf16[512,2048]{1,0:T(8,128)(2,1)} %backward.1.refs_3_), custom_call_target="tpu_custom_call" | custom-call | flops 134217728 | bytes 4194304 | tf_op jit(solution)/shard_map/adapt/pallas_call | solution.py:32
  198.5 9.2 %collective-permute-done.18.refs_4_ = bf16[2,64,2048]{2,1,0:T(8,128)(2,1)S(1)} collective-permute-done((bf16[2,64,2048]{2,1,0:T(8,128)(2,1)}, bf16[2,64,2048]{2,1,0:T(8,128)(2,1)S(1)}, u32[]{:S(2)}, u32[]{:S(2)}) %collective-permute-start.18) | collective-permute-done | bytes 524320 | tf_op jit(solution)/shard_map/ppermute | solution.py:402
  207.7 0.8 copy-done.11
  208.5 3.8 %totals.3 = f32[4,64,2048]{2,1,0:T(8,128)} custom-call(s32[8,128]{1,0:T(8,128)} %get-tuple-element.28.refs_0_, bf16[4,64,2048]{2,1,0:T(8,128)(2,1)} %get-tuple-element.45.refs_1_, bf16[2,64,2048]{2,1,0:T(8,128)(2,1)} %copy-done.9, bf16[2,64,2048]{2,1,0:T(8,128)(2,1)} %copy-done.10, bf16[2,64,2048]{2,1,0:T(8,128)(2,1)} %copy-done.11, ...), custom_call_target="tpu_custom_call" | custom-call | bytes 2097152 | tf_op jit(solution)/shard_map/totals/pallas_call | solution.py:32
  (43 shorter events, 0.1 us)
Async XLA Ops:
  7.2 0.8 copy-start.16
  7.2 161.3 %all-gather.2.cloned.1.call-start = ((), (), s32[]{:S(2)}) async-start(), calls=%async_computation.2 | async-start | bytes 10485760 | tf_op jit(solution)/shard_map/all_gather | solution.py:407
  7.9 186.0 %reduce-scatter.2.cloned.1.call-start = ((), (), s32[]{:S(2)}) async-start(), calls=%async_computation.1 | async-start | bytes 10485760 | tf_op jit(solution)/shard_map/reduce_scatter | solution.py:420
  8.0 7.0 %collective-permute-start = (s32[4]{0:T(128)S(1)}, s32[4]{0:T(128)S(1)}, u32[]{:S(2)}, u32[]{:S(2)}) collective-permute-start(s32[4]{0:T(128)S(1)} %copy-done.16), channel_id=1, source_target_pairs={{0,4},{4,8},{8,12},{12,0},{1,5},{5,9},{9,13},{13,1},{2,6},{6,10},{... | collective-permute-start | bytes 56 | tf_op jit(solution)/shard_map/ppermute | solution.py:402
  11.0 4.4 %collective-permute-start.1 = (s32[4]{0:T(128)S(1)}, s32[4]{0:T(128)S(1)}, u32[]{:S(2)}, u32[]{:S(2)}) collective-permute-start(s32[4]{0:T(128)S(1)} %copy-done.16), channel_id=1, source_target_pairs={{0,8},{4,12},{8,0},{12,4},{1,9},{5,13},{9,1},{13,5},{2,10},{6,14},... | collective-permute-start | bytes 56 | tf_op jit(solution)/shard_map/ppermute | solution.py:402
  13.6 3.5 %collective-permute-start.2 = (s32[4]{0:T(128)S(1)}, s32[4]{0:T(128)S(1)}, u32[]{:S(2)}, u32[]{:S(2)}) collective-permute-start(s32[4]{0:T(128)S(1)} %copy-done.16), channel_id=1, source_target_pairs={{0,12},{4,0},{8,4},{12,8},{1,13},{5,1},{9,5},{13,9},{2,14},{6,2},{... | collective-permute-start | bytes 56 | tf_op jit(solution)/shard_map/ppermute | solution.py:402
  15.0 2.2 %copy-start.17 = (s32[4]{0:T(128)}, s32[4]{0:T(128)S(1)}, u32[]{:S(2)}) copy-start(s32[4]{0:T(128)S(1)} %collective-permute-done.refs_3_) | copy-start | bytes 52
  15.5 1.7 copy-start.18
  17.2 0.5 copy-start.19
  21.4 35.0 %collective-permute-start.3 = (bf16[2,64,2048]{2,1,0:T(8,128)(2,1)}, bf16[2,64,2048]{2,1,0:T(8,128)(2,1)S(1)}, u32[]{:S(2)}, u32[]{:S(2)}) collective-permute-start(bf16[2,64,2048]{2,1,0:T(8,128)(2,1)} %get-tuple-element.29.refs_2_), channel_id=1, source_target_pairs={{0,12},{4,0},{8,4},{12,8},{1,13},{5,1},{9,5},{13,9},{2,14},{6,2},{... | collective-permute-start | bytes 1572872 | tf_op jit(solution)/shard_map/ppermute | solution.py:402
  24.6 31.8 %collective-permute-start.4 = (bf16[2,64,2048]{2,1,0:T(8,128)(2,1)}, bf16[2,64,2048]{2,1,0:T(8,128)(2,1)S(1)}, u32[]{:S(2)}, u32[]{:S(2)}) collective-permute-start(bf16[2,64,2048]{2,1,0:T(8,128)(2,1)} %get-tuple-element.31), channel_id=1, source_target_pairs={{0,4},{4,8},{8,12},{12,0},{1,5},{5,9},{9,13},{13,1},{2,6},{6,10},{... | collective-permute-start | bytes 1572872 | tf_op jit(solution)/shard_map/ppermute | solution.py:402
  24.6 42.9 %collective-permute-start.5 = (bf16[2,64,2048]{2,1,0:T(8,128)(2,1)}, bf16[2,64,2048]{2,1,0:T(8,128)(2,1)S(1)}, u32[]{:S(2)}, u32[]{:S(2)}) collective-permute-start(bf16[2,64,2048]{2,1,0:T(8,128)(2,1)} %get-tuple-element.32), channel_id=1, source_target_pairs={{0,8},{4,12},{8,0},{12,4},{1,9},{5,13},{9,1},{13,5},{2,10},{6,14},... | collective-permute-start | bytes 1572872 | tf_op jit(solution)/shard_map/ppermute | solution.py:402
  56.4 11.1 %copy-start = (bf16[2,64,2048]{2,1,0:T(8,128)(2,1)}, bf16[2,64,2048]{2,1,0:T(8,128)(2,1)S(1)}, u32[]{:S(2)}) copy-start(bf16[2,64,2048]{2,1,0:T(8,128)(2,1)S(1)} %collective-permute-done.3.refs_1_.refs_5_) | copy-start | bytes 1572868
  56.5 11.1 %copy-start.1 = (bf16[2,64,2048]{2,1,0:T(8,128)(2,1)}, bf16[2,64,2048]{2,1,0:T(8,128)(2,1)S(1)}, u32[]{:S(2)}) copy-start(bf16[2,64,2048]{2,1,0:T(8,128)(2,1)S(1)} %collective-permute-done.4.refs_2_.refs_3_) | copy-start | bytes 1572868
  67.5 0.8 copy-start.2
  68.3 1.0 copy-start.22
  68.3 1.2 copy-start.20
  68.3 4.9 %copy-start.21 = (bf16[2,64,2048]{2,1,0:T(8,128)(2,1)S(1)}, bf16[2,64,2048]{2,1,0:T(8,128)(2,1)}, u32[]{:S(2)}) copy-start(bf16[2,64,2048]{2,1,0:T(8,128)(2,1)} %get-tuple-element.36) | copy-start | bytes 1572868
  69.4 26.9 %collective-permute-start.8 = (bf16[2,64,2048]{2,1,0:T(8,128)(2,1)S(1)}, bf16[2,64,2048]{2,1,0:T(8,128)(2,1)S(1)}, u32[]{:S(2)}, u32[]{:S(2)}) collective-permute-start(bf16[2,64,2048]{2,1,0:T(8,128)(2,1)S(1)} %copy-done.22), channel_id=1, source_target_pairs={{0,4},{4,8},{8,12},{12,0},{1,5},{5,9},{9,13},{13,1},{2,6},{6,10},{... | collective-permute-start | bytes 1572872 | tf_op jit(solution)/shard_map/ppermute | solution.py:402
  69.5 69.3 %collective-permute-start.10 = (bf16[2,64,2048]{2,1,0:T(8,128)(2,1)S(1)}, bf16[2,64,2048]{2,1,0:T(8,128)(2,1)S(1)}, u32[]{:S(2)}, u32[]{:S(2)}) collective-permute-start(bf16[2,64,2048]{2,1,0:T(8,128)(2,1)S(1)} %copy-done.20), channel_id=1, source_target_pairs={{0,12},{4,0},{8,4},{12,8},{1,13},{5,1},{9,5},{13,9},{2,14},{6,2},{... | collective-permute-start | bytes 1572872 | tf_op jit(solution)/shard_map/ppermute | solution.py:402
  73.2 65.7 %collective-permute-start.9 = (bf16[2,64,2048]{2,1,0:T(8,128)(2,1)S(1)}, bf16[2,64,2048]{2,1,0:T(8,128)(2,1)S(1)}, u32[]{:S(2)}, u32[]{:S(2)}) collective-permute-start(bf16[2,64,2048]{2,1,0:T(8,128)(2,1)S(1)} %copy-done.21), channel_id=1, source_target_pairs={{0,8},{4,12},{8,0},{12,4},{1,9},{5,13},{9,1},{13,5},{2,10},{6,14},... | collective-permute-start | bytes 1572872 | tf_op jit(solution)/shard_map/ppermute | solution.py:402
  78.1 1.6 collective-permute-start.6
  80.5 4.3 %copy-start.12 = (bf16[4,64,128]{2,1,0:T(8,128)(2,1)}, bf16[4,64,128]{2,1,0:T(8,128)(2,1)S(1)}, u32[]{:S(2)}) copy-start(bf16[4,64,128]{2,1,0:T(8,128)(2,1)S(1)} %add_convert_fusion.1.refs_1_) | copy-start | bytes 196612
  80.6 4.3 %collective-permute-start.7 = (bf16[4,64,128]{2,1,0:T(8,128)(2,1)S(1)}, bf16[4,64,128]{2,1,0:T(8,128)(2,1)S(1)}, u32[]{:S(2)}, u32[]{:S(2)}) collective-permute-start(bf16[4,64,128]{2,1,0:T(8,128)(2,1)S(1)} %add_convert_fusion.1.refs_1_), channel_id=1, source_target_pairs={{0,2},{1,3},{2,0},{3,1},{4,6},{5,7},{6,4},{7,5},{8,10},{9,11},{10,... | collective-permute-start | bytes 196616 | tf_op jit(solution)/shard_map/ppermute | solution.py:399
  84.9 0.6 copy-start.14
  94.2 66.7 %collective-permute-start.13 = (bf16[2,64,2048]{2,1,0:T(8,128)(2,1)}, bf16[2,64,2048]{2,1,0:T(8,128)(2,1)S(1)}, u32[]{:S(2)}, u32[]{:S(2)}) collective-permute-start(bf16[2,64,2048]{2,1,0:T(8,128)(2,1)} %get-tuple-element.38.refs_6_), channel_id=1, source_target_pairs={{0,12},{4,0},{8,4},{12,8},{1,13},{5,1},{9,5},{13,9},{2,14},{6,2},{... | collective-permute-start | bytes 1572872 | tf_op jit(solution)/shard_map/ppermute | solution.py:402
  95.0 65.9 %collective-permute-start.14 = (bf16[2,64,2048]{2,1,0:T(8,128)(2,1)}, bf16[2,64,2048]{2,1,0:T(8,128)(2,1)S(1)}, u32[]{:S(2)}, u32[]{:S(2)}) collective-permute-start(bf16[2,64,2048]{2,1,0:T(8,128)(2,1)} %get-tuple-element.43), channel_id=1, source_target_pairs={{0,4},{4,8},{8,12},{12,0},{1,5},{5,9},{9,13},{13,1},{2,6},{6,10},{... | collective-permute-start | bytes 1572872 | tf_op jit(solution)/shard_map/ppermute | solution.py:402
  96.3 42.6 %copy-start.6 = (bf16[2,64,2048]{2,1,0:T(8,128)(2,1)}, bf16[2,64,2048]{2,1,0:T(8,128)(2,1)S(1)}, u32[]{:S(2)}) copy-start(bf16[2,64,2048]{2,1,0:T(8,128)(2,1)S(1)} %collective-permute-done.8.refs_3_) | copy-start | bytes 1572868
  96.3 64.7 %collective-permute-start.15 = (bf16[2,64,2048]{2,1,0:T(8,128)(2,1)}, bf16[2,64,2048]{2,1,0:T(8,128)(2,1)S(1)}, u32[]{:S(2)}, u32[]{:S(2)}) collective-permute-start(bf16[2,64,2048]{2,1,0:T(8,128)(2,1)} %get-tuple-element.44), channel_id=1, source_target_pairs={{0,8},{4,12},{8,0},{12,4},{1,9},{5,13},{9,1},{13,5},{2,10},{6,14},... | collective-permute-start | bytes 1572872 | tf_op jit(solution)/shard_map/ppermute | solution.py:402
  138.9 0.8 copy-start.8
  139.7 0.8 copy-start.7
  145.3 1.5 collective-permute-start.11
  147.7 4.3 %copy-start.13 = (bf16[4,64,128]{2,1,0:T(8,128)(2,1)}, bf16[4,64,128]{2,1,0:T(8,128)(2,1)S(1)}, u32[]{:S(2)}) copy-start(bf16[4,64,128]{2,1,0:T(8,128)(2,1)S(1)} %add_convert_fusion.refs_1_) | copy-start | bytes 196612
  147.7 4.3 %collective-permute-start.12 = (bf16[4,64,128]{2,1,0:T(8,128)(2,1)S(1)}, bf16[4,64,128]{2,1,0:T(8,128)(2,1)S(1)}, u32[]{:S(2)}, u32[]{:S(2)}) collective-permute-start(bf16[4,64,128]{2,1,0:T(8,128)(2,1)S(1)} %add_convert_fusion.refs_1_), channel_id=1, source_target_pairs={{0,2},{1,3},{2,0},{3,1},{4,6},{5,7},{6,4},{7,5},{8,10},{9,11},{10,... | collective-permute-start | bytes 196616 | tf_op jit(solution)/shard_map/ppermute | solution.py:399
  152.0 0.6 copy-start.15
  160.9 0.8 copy-start.3
  161.0 1.0 copy-start.4
  161.0 1.1 copy-start.5
  162.1 36.4 %collective-permute-start.16 = (bf16[2,64,2048]{2,1,0:T(8,128)(2,1)}, bf16[2,64,2048]{2,1,0:T(8,128)(2,1)S(1)}, u32[]{:S(2)}, u32[]{:S(2)}) collective-permute-start(bf16[2,64,2048]{2,1,0:T(8,128)(2,1)} %get-tuple-element.49.refs_5_), channel_id=1, source_target_pairs={{0,12},{4,0},{8,4},{12,8},{1,13},{5,1},{9,5},{13,9},{2,14},{6,2},{... | collective-permute-start | bytes 1572872 | tf_op jit(solution)/shard_map/ppermute | solution.py:402
  164.1 34.4 %collective-permute-start.17 = (bf16[2,64,2048]{2,1,0:T(8,128)(2,1)}, bf16[2,64,2048]{2,1,0:T(8,128)(2,1)S(1)}, u32[]{:S(2)}, u32[]{:S(2)}) collective-permute-start(bf16[2,64,2048]{2,1,0:T(8,128)(2,1)} %get-tuple-element.50), channel_id=1, source_target_pairs={{0,4},{4,8},{8,12},{12,0},{1,5},{5,9},{9,13},{13,1},{2,6},{6,10},{... | collective-permute-start | bytes 1572872 | tf_op jit(solution)/shard_map/ppermute | solution.py:402
  164.1 43.6 %collective-permute-start.18 = (bf16[2,64,2048]{2,1,0:T(8,128)(2,1)}, bf16[2,64,2048]{2,1,0:T(8,128)(2,1)S(1)}, u32[]{:S(2)}, u32[]{:S(2)}) collective-permute-start(bf16[2,64,2048]{2,1,0:T(8,128)(2,1)} %get-tuple-element.51), channel_id=1, source_target_pairs={{0,8},{4,12},{8,0},{12,4},{1,9},{5,13},{9,1},{13,5},{2,10},{6,14},... | collective-permute-start | bytes 1572872 | tf_op jit(solution)/shard_map/ppermute | solution.py:402
  198.4 9.3 %copy-start.9 = (bf16[2,64,2048]{2,1,0:T(8,128)(2,1)}, bf16[2,64,2048]{2,1,0:T(8,128)(2,1)S(1)}, u32[]{:S(2)}) copy-start(bf16[2,64,2048]{2,1,0:T(8,128)(2,1)S(1)} %collective-permute-done.16.refs_2_) | copy-start | bytes 1572868
  198.5 9.3 %copy-start.10 = (bf16[2,64,2048]{2,1,0:T(8,128)(2,1)}, bf16[2,64,2048]{2,1,0:T(8,128)(2,1)S(1)}, u32[]{:S(2)}) copy-start(bf16[2,64,2048]{2,1,0:T(8,128)(2,1)S(1)} %collective-permute-done.17.refs_3_) | copy-start | bytes 1572868
  207.7 0.8 copy-start.11
Sparse Core Ops, SparseCore 0:
  9.6 60.9 all-gather.1
  73.2 71.7 reduce-scatter.1
